TPU v7x, 32 devices: a whole 2x2x4 slice. The times are simulated.
32 devices in a mesh: expert: 16 (over z, y, x), half: 2 (over core).
Axes of the slice: x: 2, y: 2, z: 4, core: 2. Of those that a mesh axis runs over, the one named last changes fastest.
Arguments:
- tokens: bfloat16 [1024, 2048], P('expert'), may hold values from -6 to 6
- cotangent: bfloat16 [1024, 2048], P('expert'), may hold values from -1 to 1
- expert_ids: int32 [1024, 8], P('expert'), may hold values from 0 to 15, all different within a row; in each aligned block of 64 rows (0 to 63, 64 to 127, ...) at most 48 rows name the same one
- gate_weights: float32 [1024, 8], P('expert'), may hold values from 0.1 to 0.6
- w_gate: bfloat16 [16, 2048, 768], P('expert', None, 'half'), may hold values from -0.125 to 0.125
- w_up: bfloat16 [16, 2048, 768], P('expert', None, 'half'), may hold values from -0.125 to 0.125
- w_down: bfloat16 [16, 768, 2048], P('expert', 'half'), may hold values from -0.21875 to 0.21875
Outputs:
- input_grad: bfloat16 [1024, 2048], P('expert')
- gate_grad: bfloat16 [1024, 8], P('expert')
Inputs may be any that keep to these rules, and one draw needn't show every extreme that they name: `expert_ids`: each token names 8 different experts. Among the 64 tokens of one index of expert, no expert is named by more than 48 tokens, a bound that some block reaches; every expert is named somewhere.
All inputs are finite; a program needn't handle non-finite values.
Results may differ from a plain program's by a relative error of at most 0.0085.
Values may be sent and summed in bfloat16 or wider, within the bound.
No kernel may reach another device: no remote copies, remote signals or barrier semaphores. Data moves between devices by JAX's collectives and lax.ppermute only.
A program may use at most 64 MiB of HBM per device.

v0:
```python
import jax
import jax.numpy as jnp
from jax import lax
from jax.sharding import PartitionSpec as P


def expert_terms(rows, grads, gate_one, up_one, down_one):
    gate_pre = jnp.einsum("ncd,df->ncf", rows, gate_one, preferred_element_type=jnp.float32)
    up_pre = jnp.einsum("ncd,df->ncf", rows, up_one, preferred_element_type=jnp.float32)
    grad_hidden = jnp.einsum("ncd,fd->ncf", grads, down_one, preferred_element_type=jnp.float32)
    sigmoid_gate = jax.nn.sigmoid(gate_pre)
    silu_gate = gate_pre * sigmoid_gate
    scores = jnp.sum(grad_hidden * silu_gate * up_pre, axis=-1)
    grad_up = (grad_hidden * silu_gate).astype(jnp.bfloat16)
    grad_gate = (
        grad_hidden * up_pre * sigmoid_gate * (1.0 + gate_pre * (1.0 - sigmoid_gate))
    ).astype(jnp.bfloat16)
    input_part = jnp.einsum("ncf,df->ncd", grad_gate, gate_one, preferred_element_type=jnp.float32)
    input_part = input_part + jnp.einsum(
        "ncf,df->ncd", grad_up, up_one, preferred_element_type=jnp.float32
    )
    return (input_part, scores)


def owner_sum(back, slot_index, gate_weights):
    width = back.shape[2]
    picked = back.reshape(-1, width)[slot_index]
    picked = picked.reshape(gate_weights.shape[0], gate_weights.shape[1], width)
    return jnp.einsum(
        "tk,tkw->tw", gate_weights, picked, preferred_element_type=jnp.float32
    ).astype(jnp.bfloat16)


def per_device(tokens, cotangent, expert_ids, gate_weights, w_gate, w_up, w_down):
    tok_count, top_count = expert_ids.shape
    experts = lax.axis_size("expert")
    capacity = 3 * tok_count * top_count // (2 * experts)
    routed = expert_ids.reshape(-1)
    onehot = (routed[:, None] == jnp.arange(experts, dtype=jnp.int32)[None, :]).astype(jnp.int32)
    earlier = jnp.cumsum(onehot, axis=0) - onehot
    slot_index = routed * capacity + jnp.sum(earlier * onehot, axis=1)
    owner_rows = jnp.arange(tok_count * top_count, dtype=jnp.int32) // top_count + 1
    slot_token = jnp.zeros((experts * capacity,), jnp.int32).at[slot_index].set(owner_rows)
    slot_live = (slot_token > 0)[:, None]
    picked = jnp.maximum(slot_token - 1, 0)
    sent_tokens = jnp.where(slot_live, tokens[picked], jnp.zeros((), tokens.dtype)).reshape(
        experts, capacity, -1
    )
    sent_grads = jnp.where(slot_live, cotangent[picked], jnp.zeros((), cotangent.dtype)).reshape(
        experts, capacity, -1
    )
    gate_one = w_gate[0]
    up_one = w_up[0]
    down_one = w_down[0]
    gate_full, up_full = (
        lax.all_gather(gate_one, "half", axis=1, tiled=True),
        lax.all_gather(up_one, "half", axis=1, tiled=True),
    )
    down_full = lax.all_gather(down_one, "half", axis=0, tiled=True)
    half_slots = capacity // 2
    first_slot = lax.axis_index("half") * half_slots
    own_tokens = lax.dynamic_slice_in_dim(sent_tokens, first_slot, half_slots, 1)
    own_grads = lax.dynamic_slice_in_dim(sent_grads, first_slot, half_slots, 1)
    rows = lax.all_to_all(own_tokens, "expert", split_axis=0, concat_axis=0, tiled=True)
    grads = lax.all_to_all(own_grads, "expert", split_axis=0, concat_axis=0, tiled=True)
    part, score = expert_terms(rows, grads, gate_full, up_full, down_full)
    slot_part = part.astype(jnp.bfloat16)
    slot_scores = score.astype(jnp.bfloat16)
    back_part, back_part_scores = (
        lax.all_to_all(slot_part, "expert", split_axis=0, concat_axis=0, tiled=True),
        lax.all_to_all(slot_scores, "expert", split_axis=0, concat_axis=0, tiled=True),
    )
    back, back_scores = (
        lax.all_gather(back_part, "half", axis=1, tiled=True),
        lax.all_gather(back_part_scores, "half", axis=1, tiled=True),
    )
    input_grad = owner_sum(back, slot_index, gate_weights)
    gate_grad = back_scores.reshape(-1)[slot_index].reshape(tok_count, top_count)
    return (input_grad, gate_grad)


def solution(mesh):
    placed = (
        P("expert", None),
        P("expert", None),
        P("expert", None),
        P("expert", None),
        P("expert", None, "half"),
        P("expert", None, "half"),
        P("expert", "half", None),
    )
    return jax.shard_map(
        per_device,
        mesh=mesh,
        in_specs=placed,
        out_specs=(P("expert", None), P("expert", None)),
        check_vma=False,
    )
```

profile of v0, /device:TPU:0, one launch (start us, length us, event | category | flops | bytes accessed | tf_op | source)
XLA Modules:
  0.0 198.7 jit_solution(10806493836926176371)
XLA Ops:
  8.2 1.2 reduce-window.6
  9.9 2.4 %scatter_custom_fusion = s32[768]{0:T(1024)S(1)} fusion(s32[512]{0:T(512)S(1)} %bitcast.64, s32[512]{0:T(512)S(1)} %fusion.20, s32[]{:T(128)} %constant.16.clone.1), kind=kCustom, calls=%fused_computation.50 | custom fusion | bytes 3076 | tf_op jit(solution)/shard_map/scatter | solution.py:43
  12.5 4.3 %gather_fusion = bf16[768,2048]{1,0:T(8,128)(2,1)} fusion(bf16[64,2048]{1,0:T(8,128)(2,1)S(1)} %copy-done, s32[1024]{0:T(1024)S(1)} %pad_clamp_fusion.1), kind=kCustom, calls=%fused_computation | custom fusion | bytes 6294528 | tf_op jit(solution)/shard_map/gather | solution.py:49
  16.8 4.3 %gather_fusion.1 = bf16[768,2048]{1,0:T(8,128)(2,1)} fusion(bf16[64,2048]{1,0:T(8,128)(2,1)S(1)} %copy-done.1, s32[1024]{0:T(1024)S(1)} %pad_clamp_fusion.1), kind=kCustom, calls=%fused_computation.1 | custom fusion | bytes 6294528 | tf_op jit(solution)/shard_map/gather | solution.py:46
  21.2 5.1 %dynamic-slice_select_fusion.1 = (bf16[16,24,2048]{2,1,0:T(8,128)(2,1)}, bf16[16,24,2048]{2,1,0:T(8,128)(2,1)}) fusion(bf16[16,48,2048]{2,1,0:T(8,128)(2,1)} %bitcast.61, s32[]{:T(128)S(6)} %select_n.35, pred[16,24]{1,0:T(8,128)(4,1)S(1)} %constant_dynamic-slice_fusion, bf16[16,48,2048]{2,1,0:T(8,128)(2,1)} %bitcast.62), kind=kLoop, calls=%fused_computation.19 | loop fusion | flops 1572864 | bytes 6291844 | tf_op jit(solution)/shard_map/jit(_where)/select_n | solution.py:49
  26.3 7.9 %all-to-all-start.1 = ((bf16[16,24,2048]{2,1,0:T(8,128)(2,1)}), bf16[16,24,2048]{2,1,0:T(8,128)(2,1)S(1)}, u32[]{:S(2)}, u32[]{:S(2)}) async-start(bf16[16,24,2048]{2,1,0:T(8,128)(2,1)} %get-tuple-element.9), calls=%async_computation.1 | async-start | bytes 3145728 | tf_op jit(solution)/shard_map/all_to_all | solution.py:64
  34.3 0.7 all-gather.11.cloned.1.call-update
  35.0 33.4 %all-to-all-done.1 = bf16[16,24,2048]{2,1,0:T(8,128)(2,1)S(1)} async-done(((bf16[16,24,2048]{2,1,0:T(8,128)(2,1)}), bf16[16,24,2048]{2,1,0:T(8,128)(2,1)S(1)}, u32[]{:S(2)}, u32[]{:S(2)}) %all-to-all-start.1) | async-done | bytes 1572896 | tf_op jit(solution)/shard_map/all_to_all | solution.py:64
  68.4 7.6 %all-to-all-start = ((bf16[16,24,2048]{2,1,0:T(8,128)(2,1)}), bf16[16,24,2048]{2,1,0:T(8,128)(2,1)S(1)}, u32[]{:S(2)}, u32[]{:S(2)}) async-start(bf16[16,24,2048]{2,1,0:T(8,128)(2,1)} %get-tuple-element.8), calls=%async_computation | async-start | bytes 3145728 | tf_op jit(solution)/shard_map/all_to_all | solution.py:65
  76.1 0.7 all-gather.13.cloned.1.call-update
  76.8 4.3 %fusion.2 = f32[16,24,768]{2,1,0:T(8,128)} fusion(bf16[16,24,2048]{2,1,0:T(8,128)(2,1)S(1)} %all-to-all-done.1, bf16[1,2048,768]{2,1,0:T(8,128)(2,1)} %all-gather.15.cloned.1.call-done), kind=kOutput, calls=%fused_computation.7 | convolution fusion | flops 1207959552 | bytes 5898240 | tf_op jit(solution)/shard_map/ncd,df->ncf/dot_general | solution.py:8
  81.2 28.4 %all-to-all-done = bf16[16,24,2048]{2,1,0:T(8,128)(2,1)S(1)} async-done(((bf16[16,24,2048]{2,1,0:T(8,128)(2,1)}), bf16[16,24,2048]{2,1,0:T(8,128)(2,1)S(1)}, u32[]{:S(2)}, u32[]{:S(2)}) %all-to-all-start) | async-done | bytes 1572896 | tf_op jit(solution)/shard_map/all_to_all | solution.py:65
  109.5 4.4 %fusion.8 = f32[16,24,768]{2,1,0:T(8,128)} fusion(bf16[16,24,2048]{2,1,0:T(8,128)(2,1)S(1)} %all-to-all-done, bf16[1,768,2048]{2,1,0:T(8,128)(2,1)} %all-gather.11.cloned.1.call-done), kind=kOutput, calls=%fused_computation.13 | convolution fusion | flops 1207959552 | bytes 5898240 | tf_op jit(solution)/shard_map/ncd,fd->ncf/dot_general | solution.py:10
  114.0 4.3 %multiply_reduce_fusion = (bf16[16,24]{1,0:T(8,128)(2,1)S(1)}, f32[16,24,768]{2,1,0:T(8,128)S(1)}) fusion(f32[16,24,768]{2,1,0:T(8,128)} %fusion.8, f32[16,24,768]{2,1,0:T(8,128)} %fusion.2, bf16[16,24,2048]{2,1,0:T(8,128)(2,1)S(1)} %all-to-all-done.1, bf16[1,2048,768]{2,1,0:T(8,128)(2,1)} %all-gather.13.cloned.1.call-done), kind=kOutput, calls=%fused_computation.20 | convolution fusion | flops 1210023552 | bytes 8258304 | tf_op jit(solution)/shard_map/ncd,df->ncf/dot_general | solution.py:9
  118.3 1.8 fusion
  120.2 1.5 add_convert_fusion
  121.7 44.1 %all_to_all.24 = bf16[16,24,2048]{2,1,0:T(8,128)(2,1)} all-to-all(bf16[16,24,2048]{2,1,0:T(8,128)(2,1)S(1)} %add_convert_fusion), channel_id=1, replica_groups=mesh['expert'=16,'half'=2] {'expert'}, dimensions={0} | all-to-all | bytes 3145728 | tf_op jit(solution)/shard_map/all_to_all | solution.py:70
  166.4 3.9 %all-to-all-start.3 = ((bf16[16,1,24]{2,1,0:T(2,128)(2,1)}), bf16[16,1,24]{2,1,0:T(2,128)(2,1)S(1)}, u32[]{:S(2)}, u32[]{:S(2)}) async-start(bf16[16,1,24]{2,1,0:T(2,128)(2,1)} %copy.24), calls=%async_computation.3 | async-start | bytes 16384 | tf_op jit(solution)/shard_map/all_to_all | solution.py:71
  170.5 7.1 %all-to-all-done.3 = bf16[16,1,24]{2,1,0:T(2,128)(2,1)S(1)} async-done(((bf16[16,1,24]{2,1,0:T(2,128)(2,1)}), bf16[16,1,24]{2,1,0:T(2,128)(2,1)S(1)}, u32[]{:S(2)}, u32[]{:S(2)}) %all-to-all-start.3) | async-done | bytes 800 | tf_op jit(solution)/shard_map/all_to_all | solution.py:71
  177.6 1.8 all-gather.3
  179.6 3.5 %gather_fusion.3 = bf16[512]{0:T(512)(128)(2,1)S(1)} fusion(bf16[768]{0:T(1024)(128)(2,1)S(1)} %reshape.89, s32[1024]{0:T(1024)S(1)} %pad_clamp_fusion), kind=kCustom, calls=%fused_computation.3 | custom fusion | bytes 4096 | tf_op jit(solution)/shard_map/gather | solution.py:78
  183.9 6.7 %gather_fusion.2 = bf16[512,2048]{1,0:T(8,128)(2,1)S(1)} fusion(bf16[768,2048]{1,0:T(8,128)(2,1)} %bitcast.60, s32[1024]{0:T(1024)S(1)} %pad_clamp_fusion), kind=kCustom, calls=%fused_computation.2 | custom fusion | bytes 4196352 | tf_op jit(solution)/shard_map/gather | solution.py:27
  190.6 0.7 fusion.12
  191.3 0.9 copy.33
  (52 shorter events, 3.7 us)
Async XLA Ops:
  7.2 5.3 %copy-start = (bf16[64,2048]{1,0:T(8,128)(2,1)S(1)}, bf16[64,2048]{1,0:T(8,128)(2,1)}, u32[]{:S(2)}) copy-start(bf16[64,2048]{1,0:T(8,128)(2,1)} %param.8) | copy-start | bytes 786436
  7.2 0.7 copy-start.2
  7.2 69.6 %all-gather.15.cloned.1.call-start = ((), (), s32[]{:S(2)}) async-start(), calls=%async_computation.7 | async-start | bytes 4718592 | tf_op jit(solution)/shard_map/all_gather | solution.py:56
  12.5 4.3 %copy-start.1 = (bf16[64,2048]{1,0:T(8,128)(2,1)S(1)}, bf16[64,2048]{1,0:T(8,128)(2,1)}, u32[]{:S(2)}) copy-start(bf16[64,2048]{1,0:T(8,128)(2,1)} %param.7) | copy-start | bytes 786436
  26.3 42.1 %all-to-all-start.1 = ((bf16[16,24,2048]{2,1,0:T(8,128)(2,1)}), bf16[16,24,2048]{2,1,0:T(8,128)(2,1)S(1)}, u32[]{:S(2)}, u32[]{:S(2)}) async-start(bf16[16,24,2048]{2,1,0:T(8,128)(2,1)} %get-tuple-element.9), calls=%async_computation.1 | async-start | bytes 3145728 | tf_op jit(solution)/shard_map/all_to_all | solution.py:64
  34.2 75.3 %all-gather.11.cloned.1.call-start = ((), (), s32[]{:S(2)}) async-start(), calls=%async_computation.5 | async-start | bytes 4718592 | tf_op jit(solution)/shard_map/all_gather | solution.py:59
  68.4 41.2 %all-to-all-start = ((bf16[16,24,2048]{2,1,0:T(8,128)(2,1)}), bf16[16,24,2048]{2,1,0:T(8,128)(2,1)S(1)}, u32[]{:S(2)}, u32[]{:S(2)}) async-start(bf16[16,24,2048]{2,1,0:T(8,128)(2,1)} %get-tuple-element.8), calls=%async_computation | async-start | bytes 3145728 | tf_op jit(solution)/shard_map/all_to_all | solution.py:65
  76.0 37.9 %all-gather.13.cloned.1.call-start = ((), (), s32[]{:S(2)}) async-start(), calls=%async_computation.6 | async-start | bytes 4718592 | tf_op jit(solution)/shard_map/all_gather | solution.py:57
  76.8 107.1 %all-gather.9.cloned.1.call-start = ((), (), s32[]{:S(2)}) async-start(), calls=%async_computation.4 | async-start | bytes 4718592 | tf_op jit(solution)/shard_map/all_gather | solution.py:74
  114.0 4.3 %copy-start.6 = (f32[16,24,768]{2,1,0:T(8,128)S(1)}, f32[16,24,768]{2,1,0:T(8,128)}, u32[]{:S(2)}) copy-start(f32[16,24,768]{2,1,0:T(8,128)} %fusion.2) | copy-start | bytes 3538948
  114.0 4.3 %copy-start.4 = (bf16[1,2048,768]{2,1,0:T(8,128)(2,1)S(1)}, bf16[1,2048,768]{2,1,0:T(8,128)(2,1)}, u32[]{:S(2)}) copy-start(bf16[1,2048,768]{2,1,0:T(8,128)(2,1)} %all-gather.15.cloned.1.call-done) | copy-start | bytes 9437188
  114.0 4.3 %copy-start.7 = (f32[16,24,768]{2,1,0:T(8,128)S(1)}, f32[16,24,768]{2,1,0:T(8,128)}, u32[]{:S(2)}) copy-start(f32[16,24,768]{2,1,0:T(8,128)} %fusion.8) | copy-start | bytes 3538948
  118.3 1.9 copy-start.5
  165.8 4.6 %copy-start.3 = (f32[64,8]{0,1:T(8,128)S(1)}, f32[64,8]{0,1:T(8,128)}, u32[]{:S(2)}) copy-start(f32[64,8]{0,1:T(8,128)} %param.10) | copy-start | bytes 6148
  166.4 11.1 %all-to-all-start.3 = ((bf16[16,1,24]{2,1,0:T(2,128)(2,1)}), bf16[16,1,24]{2,1,0:T(2,128)(2,1)S(1)}, u32[]{:S(2)}, u32[]{:S(2)}) async-start(bf16[16,1,24]{2,1,0:T(2,128)(2,1)} %copy.24), calls=%async_computation.3 | async-start | bytes 16384 | tf_op jit(solution)/shard_map/all_to_all | solution.py:71
Sparse Core Ops, SparseCore 0:
  9.6 14.7 all-gather.14
  36.6 13.4 all-gather.10
  78.4 13.3 all-gather.12
  166.0 10.3 all-gather.8
where the time goes:
time: 199 us
  waiting for transfers between devices  71 us (36%)
  blocking collectives  45.9 us (23%)
  local copies, waits for them, and re-layouts  24.8 us (12%)
  starting transfers between devices  19.6 us (10%)
  matrix products  17 us (9%)
  between operations  14 us (7%)
  other arithmetic  6.4 us (3%)
    all_to_all x1, blocking collectives, per_device(): lax.all_to_all(slot_part, 'expert', split_axis=0, concat_axis=0, tiled=True)  44.1 us
    all_to_all x1, waiting for transfers between devices, per_device(): lax.all_to_all(own_tokens, 'expert', split_axis=0, concat_axis=0, tiled=T...  33.4 us
    all_to_all x1, waiting for transfers between devices, per_device(): lax.all_to_all(own_grads, 'expert', split_axis=0, concat_axis=0, tiled=True)  28.4 us
    all_to_all x1, starting transfers between devices, per_device(): lax.all_to_all(own_tokens, 'expert', split_axis=0, concat_axis=0, tiled=T...  7.88 us
    all_to_all x1, starting transfers between devices, per_device(): lax.all_to_all(own_grads, 'expert', split_axis=0, concat_axis=0, tiled=True)  7.63 us
    all_to_all x1, waiting for transfers between devices, per_device(): lax.all_to_all(slot_scores, 'expert', split_axis=0, concat_axis=0, tiled=...  7.06 us
    gather x1, local copies, waits for them, and re-layouts, owner_sum(): picked = back.reshape(-1, width)[slot_index]  6.7 us
    select_n x1, other arithmetic, per_device(): jnp.where(slot_live, cotangent[picked], jnp.zeros((), cotangent.dtype))  5.07 us
  transfers between devices with their start and end apart: 7, of which 3 were waited for; matrix products, arithmetic and copies ran while one was open for 16% of the time, Pallas kernels for 0%

commit v1 on v0

--- a/solution.py
+++ b/solution.py
@@ -1,7 +1,13 @@
+import functools
+
 import jax
 import jax.numpy as jnp
 from jax import lax
+from jax.experimental import pallas as pl
+from jax.experimental.pallas import tpu as pltpu
 from jax.sharding import PartitionSpec as P
+
+LANES = 128
 
 
 def expert_terms(rows, grads, gate_one, up_one, down_one):
@@ -31,7 +37,7 @@
     ).astype(jnp.bfloat16)
 
 
-def per_device(tokens, cotangent, expert_ids, gate_weights, w_gate, w_up, w_down):
+def routed_plan(tokens, cotangent, expert_ids, gate_weights, w_gate, w_up, w_down):
     tok_count, top_count = expert_ids.shape
     experts = lax.axis_size("expert")
     capacity = 3 * tok_count * top_count // (2 * experts)
@@ -79,6 +85,185 @@
     return (input_grad, gate_grad)
 
 
+def padded(count):
+    return -(-count // LANES) * LANES
+
+
+def pack_kernel(experts, half_ref, tok_ref, cot_ref, ids_ref, gw_ref, out_ref):
+    rows, width = tok_ref.shape
+    out_ref[:, 0:width] = tok_ref[...]
+    out_ref[:, width : 2 * width] = cot_ref[...]
+    lane = lax.broadcasted_iota(jnp.int32, (rows, out_ref.shape[1] - 2 * width), 1)
+    total = jnp.zeros(lane.shape, jnp.float32)
+    weights = gw_ref[...]
+    high = weights.astype(jnp.bfloat16).astype(jnp.float32)
+    low = weights - high
+    ids = ids_ref[...]
+    for k in range(ids.shape[1]):
+        one = ids[:, k : k + 1]
+        total = jnp.where(lane == one, high[:, k : k + 1], total)
+        total = jnp.where(lane == one + experts, low[:, k : k + 1], total)
+    out_ref[:, 2 * width :] = total.astype(jnp.bfloat16)
+
+
+def pack(half, tokens, cotangent, expert_ids, gate_weights, experts):
+    tok_count, width = tokens.shape
+    rows, top = tok_count // 2, expert_ids.shape[1]
+    own = lambda i, half: (half[0], 0)
+    return pl.pallas_call(
+        functools.partial(pack_kernel, experts),
+        grid_spec=pltpu.PrefetchScalarGridSpec(
+            num_scalar_prefetch=1,
+            grid=(1,),
+            in_specs=[
+                pl.BlockSpec((rows, width), own),
+                pl.BlockSpec((rows, width), own),
+                pl.BlockSpec((rows, top), own),
+                pl.BlockSpec((rows, top), own),
+            ],
+            out_specs=pl.BlockSpec((rows, 2 * width + padded(2 * experts)), lambda i, half: (0, 0)),
+        ),
+        out_shape=jax.ShapeDtypeStruct((rows, 2 * width + padded(2 * experts)), jnp.bfloat16),
+        name="pack",
+    )(half, tokens, cotangent, expert_ids, gate_weights)
+
+
+def expert_kernel(experts, expert_ref, own_ref, first_ref, rest_ref, gate_up_ref, down_ref, near_ref, far_ref):
+    rows = own_ref.shape[0]
+    width, units = gate_up_ref.shape[0], down_ref.shape[0]
+    contract_last = (((1,), (1,)), ((), ()))
+    packed = jnp.concatenate([own_ref[...], first_ref[...], rest_ref[...]], axis=0)
+    pre = jnp.dot(packed[:, :width], gate_up_ref[...], preferred_element_type=jnp.float32)
+    grad_hidden = lax.dot_general(
+        packed[:, width : 2 * width], down_ref[...], contract_last, preferred_element_type=jnp.float32
+    )
+    gate_pre, up_pre = pre[:, :units], pre[:, units:]
+    sigmoid_gate = 1.0 / (1.0 + jnp.exp(-gate_pre))
+    grad_up = grad_hidden * gate_pre * sigmoid_gate
+    scores = jnp.sum(grad_up * up_pre, axis=1, keepdims=True)
+    grad_gate = grad_hidden * up_pre * sigmoid_gate * (1.0 + gate_pre * (1.0 - sigmoid_gate))
+    grads = jnp.concatenate([grad_gate.astype(jnp.bfloat16), grad_up.astype(jnp.bfloat16)], axis=1)
+    part = lax.dot_general(grads, gate_up_ref[...], contract_last, preferred_element_type=jnp.float32)
+    expert = expert_ref[0]
+    routing = packed[:, 2 * width :].astype(jnp.float32)
+    lane = lax.broadcasted_iota(jnp.int32, routing.shape, 1)
+    weight = jnp.sum(
+        jnp.where((lane == expert) | (lane == expert + experts), routing, 0.0), axis=1, keepdims=True
+    )
+    part = (part * weight).astype(jnp.bfloat16)
+    columns = near_ref.shape[1] - width
+    column = lax.broadcasted_iota(jnp.int32, (packed.shape[0], columns), 1)
+    score_part = jnp.where(column == expert, scores, 0.0).astype(jnp.bfloat16)
+    near_ref[:, :width] = part[: 2 * rows]
+    near_ref[:, width:] = score_part[: 2 * rows]
+    far_ref[:, :width] = part[2 * rows :]
+    far_ref[:, width:] = score_part[2 * rows :]
+
+
+def expert_call(expert, own, first, rest, gate_up, down, experts):
+    rows = own.shape[0]
+    width, units = gate_up.shape[0], down.shape[0]
+    out = jax.ShapeDtypeStruct((2 * rows, width + padded(experts)), jnp.bfloat16)
+    vmem = pl.BlockSpec(memory_space=pltpu.VMEM)
+    return pl.pallas_call(
+        functools.partial(expert_kernel, experts),
+        in_specs=[pl.BlockSpec(memory_space=pltpu.SMEM)] + [vmem] * 5,
+        out_specs=(vmem, vmem),
+        out_shape=(out, out),
+        compiler_params=pltpu.CompilerParams(vmem_limit_bytes=40 * 2**20),
+        cost_estimate=pl.CostEstimate(
+            flops=2 * 4 * rows * width * units * 5, bytes_accessed=gate_up.size * 3, transcendentals=0
+        ),
+        name="expert",
+    )(expert, own, first, rest, gate_up, down)
+
+
+def finish_kernel(half_ref, own_ref, other_ref, ids_ref, grad_ref, score_ref):
+    rows, width = own_ref.shape[0], grad_ref.shape[1]
+    half = half_ref[0]
+    for ref, place in ((own_ref, half), (other_ref, 1 - half)):
+        block = pl.ds(pl.multiple_of(place * rows, rows), rows)
+        grad_ref[block, :] = ref[:, :width]
+        scores = ref[:, width:].astype(jnp.float32)
+        column = lax.broadcasted_iota(jnp.int32, scores.shape, 1)
+        ids = ids_ref[block, :]
+        place_of = lax.broadcasted_iota(jnp.int32, ids.shape, 1)
+        total = jnp.zeros(ids.shape, jnp.float32)
+        for k in range(ids.shape[1]):
+            one = jnp.sum(jnp.where(column == ids[:, k : k + 1], scores, 0.0), axis=1, keepdims=True)
+            total = jnp.where(place_of == k, one, total)
+        score_ref[block, :] = total
+
+
+def finish(half, own, other, expert_ids, width):
+    vmem = pl.BlockSpec(memory_space=pltpu.VMEM)
+    grad, score = pl.pallas_call(
+        finish_kernel,
+        in_specs=[pl.BlockSpec(memory_space=pltpu.SMEM)] + [vmem] * 3,
+        out_specs=(vmem, vmem),
+        out_shape=(
+            jax.ShapeDtypeStruct((expert_ids.shape[0], width), jnp.bfloat16),
+            jax.ShapeDtypeStruct(expert_ids.shape, jnp.float32),
+        ),
+        name="finish",
+    )(half, own, other, expert_ids)
+    return grad, score.astype(jnp.bfloat16)
+
+
+def added(*terms):
+    total = terms[0].astype(jnp.float32)
+    for term in terms[1:]:
+        total = total + term.astype(jnp.float32)
+    return total.astype(jnp.bfloat16)
+
+
+def dense_plan(tokens, cotangent, expert_ids, gate_weights, w_gate, w_up, w_down):
+    experts, halves = lax.axis_size("expert"), lax.axis_size("half")
+    levels = experts // 4
+    width = tokens.shape[1]
+    rows = tokens.shape[0] // 2
+    half = lax.axis_index("half").reshape(1).astype(jnp.int32)
+    expert = lax.axis_index("expert").reshape(1).astype(jnp.int32)
+    axes = ("expert", "half")
+
+    first_pairs = [(e * 2 + h, (e ^ (1 + h)) * 2 + h) for e in range(experts) for h in range(halves)]
+    second_pairs = [(e * 2 + h, (e ^ (2 - h)) * 2 + h) for e in range(experts) for h in range(halves)]
+    ring_pairs = [(e, (e + 4) % experts) for e in range(experts)]
+    swap_pairs = [(0, 1), (1, 0)]
+    to_first = lambda a: lax.ppermute(a, axes, first_pairs)
+    to_second = lambda a: lax.ppermute(a, axes, second_pairs)
+    along_ring = lambda a: lax.ppermute(a, "expert", ring_pairs)
+    swapped = lambda a: lax.ppermute(a, "half", swap_pairs)
+
+    own = pack(half, tokens, cotangent, expert_ids, gate_weights, experts)
+    gate_one, up_one, down_one = w_gate[0], w_up[0], w_down[0]
+    gate_up = jnp.concatenate([gate_one, swapped(gate_one), up_one, swapped(up_one)], axis=1)
+    down = jnp.concatenate([down_one, swapped(down_one)], axis=0)
+
+    planes = []
+    shard = own
+    for level in range(levels):
+        first = to_first(shard)
+        rest = to_second(jnp.concatenate([shard, first], axis=0))
+        planes.append((shard, first, rest))
+        if level < levels - 1:
+            shard = along_ring(shard)
+
+    sums = []
+    for shard, first, rest in planes:
+        near, far = expert_call(expert, shard, first, rest, gate_up, down, experts)
+        from_second = to_second(far)
+        from_first = to_first(added(near[rows:], from_second[rows:]))
+        sums.append((near[:rows], from_second[:rows], from_first))
+    carry = None
+    for level in list(range(1, levels)) + [0]:
+        terms = sums[level] if carry is None else sums[level] + (carry,)
+        carry = added(*terms)
+        if level:
+            carry = along_ring(carry)
+    return finish(half, carry, swapped(carry), expert_ids, width)
+
+
 def solution(mesh):
     placed = (
         P("expert", None),
@@ -89,6 +274,12 @@
         P("expert", None, "half"),
         P("expert", "half", None),
     )
+
+    def per_device(tokens, cotangent, expert_ids, *others):
+        experts, top = mesh.shape["expert"], expert_ids.shape[1]
+        dense = experts <= 2 * top and experts % 4 == 0 and mesh.shape["half"] == 2
+        return (dense_plan if dense else routed_plan)(tokens, cotangent, expert_ids, *others)
+
     return jax.shard_map(
         per_device,
         mesh=mesh,

time: 199 us -> 109 us (0.55)
  blocking collectives: 45.9 us -> 0 us
  Pallas kernels: 0 us -> 21.9 us
  local copies, waits for them, and re-layouts: 24.8 us -> 4.1 us
  waiting for transfers between devices: 71 us -> 52.7 us
  matrix products: 17 us -> 0 us
  between operations: 14 us -> 0.85 us
    all_to_all x3 -> x0, waiting for transfers between devices: 68.9 us -> none  [the longest x1 33.4 us: per_device(): lax.all_to_all(own_tokens, 'expert', split_axis=0, concat_axis=0, tiled=T...]
    ppermute x0 -> x26, waiting for transfers between devices: none -> 52.7 us  [the longest x6 32.2 us: dense_plan(): along_ring = lambda a: lax.ppermute(a, 'expert', ring_pairs)]
    all_to_all x1 -> x0, blocking collectives: 44.1 us -> none  [per_device(): lax.all_to_all(slot_part, 'expert', split_axis=0, concat_axis=0, tiled=True)]
    pallas_call x0 -> x6, Pallas kernels: none -> 21.9 us  [the longest x4 17.3 us: expert_call(): pl.pallas_call(functools.partial(expert_kernel, experts), in_specs=[pl.Bl...]
    ppermute x0 -> x26, starting transfers between devices: none -> 21 us  [the longest x8 10.2 us: dense_plan(): to_first = lambda a: lax.ppermute(a, axes, first_pairs)]
    all_to_all x3 -> x0, starting transfers between devices: 19.4 us -> none  [the longest x1 7.88 us: per_device(): lax.all_to_all(own_tokens, 'expert', split_axis=0, concat_axis=0, tiled=T...]
    gather x4 -> x0, local copies, waits for them, and re-layouts: 18.9 us -> none  [the longest x1 6.7 us: owner_sum(): picked = back.reshape(-1, width)[slot_index]]
    dot_general x6 -> x0, matrix products: 17 us -> none  [the longest x1 4.42 us: expert_terms(): jnp.einsum('ncd,fd->ncf', grads, down_one, preferred_element_type=jnp.flo...]
  transfers between devices with their start and end apart: 7 -> 26, of which waited for: 3 -> 13; matrix products, arithmetic and copies ran while one was open for 16% -> 5% of each run, Pallas kernels for 0% -> 16%
where the time goes in v1:
time: 109 us; the launch traced here: 107 us
  waiting for transfers between devices  52.7 us (48%)
  Pallas kernels  21.9 us (20%)
  starting transfers between devices  21 us (19%)
  other arithmetic  6.64 us (6%)
  local copies, waits for them, and re-layouts  4.1 us (4%)
    ppermute x6, waiting for transfers between devices, dense_plan(): along_ring = lambda a: lax.ppermute(a, 'expert', ring_pairs)  32.2 us
    pallas_call x4, Pallas kernels, expert_call(): pl.pallas_call(functools.partial(expert_kernel, experts), in_specs=[pl.Bl...  17.3 us
    ppermute x8, waiting for transfers between devices, dense_plan(): to_first = lambda a: lax.ppermute(a, axes, first_pairs)  13.5 us
    ppermute x8, starting transfers between devices, dense_plan(): to_first = lambda a: lax.ppermute(a, axes, first_pairs)  10.2 us
    ppermute x8, starting transfers between devices, dense_plan(): to_second = lambda a: lax.ppermute(a, axes, second_pairs)  6.97 us
    ppermute x8, waiting for transfers between devices, dense_plan(): to_second = lambda a: lax.ppermute(a, axes, second_pairs)  5.66 us
    unnamed x15, local copies, waits for them, and re-layouts  4.1 us
    ppermute x6, starting transfers between devices, dense_plan(): along_ring = lambda a: lax.ppermute(a, 'expert', ring_pairs)  3.2 us
  transfers between devices with their start and end apart: 26, of which 13 were waited for; matrix products, arithmetic and copies ran while one was open for 5% of the time, Pallas kernels for 16%

profile of v1, /device:TPU:0, one launch (start us, length us, event | category | flops | bytes accessed | tf_op | source)
XLA Modules:
  0.0 107.1 jit_solution(18360694520327036863)
XLA Ops:
  3.4 1.8 %pack.1.own_ref = bf16[32,4224]{1,0:T(8,128)(2,1)} custom-call(s32[1]{0:T(128)} %bitcast.half_ref, bf16[64,2048]{1,0:T(8,128)(2,1)} %tok_ref.1, bf16[64,2048]{1,0:T(8,128)(2,1)} %cot_ref.1, s32[64,8]{1,0:T(8,128)} %copy.9.ids_ref, f32[64,8]{1,0:T(8,128)} %copy.10.gw_ref), custom_call_target="tpu_custom_call" | custom-call | tf_op jit(solution)/shard_map/pack/pallas_call | solution.py:113
  5.2 3.0 %collective-permute-start.7 = (bf16[32,4224]{1,0:T(8,128)(2,1)}, bf16[32,4224]{1,0:T(8,128)(2,1)S(1)}, u32[]{:S(2)}, u32[]{:S(2)}) collective-permute-start(bf16[32,4224]{1,0:T(8,128)(2,1)} %pack.1.own_ref), channel_id=1, source_target_pairs={{0,8},{2,10},{4,12},{6,14},{8,16},{10,18},{12,20},{14,22},{16,24},... | collective-permute-start | bytes 811016 | tf_op jit(solution)/shard_map/ppermute | solution.py:235
  10.3 6.7 %collective-permute-done.7.own_ref = bf16[32,4224]{1,0:T(8,128)(2,1)S(1)} collective-permute-done((bf16[32,4224]{1,0:T(8,128)(2,1)}, bf16[32,4224]{1,0:T(8,128)(2,1)S(1)}, u32[]{:S(2)}, u32[]{:S(2)}) %collective-permute-start.7) | collective-permute-done | bytes 270368 | tf_op jit(solution)/shard_map/ppermute | solution.py:235
  17.0 1.5 %collective-permute-start.18 = (bf16[32,4224]{1,0:T(8,128)(2,1)S(1)}, bf16[32,4224]{1,0:T(8,128)(2,1)S(1)}, u32[]{:S(2)}, u32[]{:S(2)}) collective-permute-start(bf16[32,4224]{1,0:T(8,128)(2,1)S(1)} %collective-permute-done.7.own_ref), channel_id=1, source_target_pairs={{0,2},{1,5},{2,0},{3,7},{4,6},{5,1},{6,4},{7,3},{8,10},{9,13},{10,... | collective-permute-start | bytes 811016 | tf_op jit(solution)/shard_map/ppermute | solution.py:233
  19.5 7.9 %collective-permute-done.8.own_ref = bf16[32,4224]{1,0:T(8,128)(2,1)S(1)} collective-permute-done((bf16[32,4224]{1,0:T(8,128)(2,1)S(1)}, bf16[32,4224]{1,0:T(8,128)(2,1)S(1)}, u32[]{:S(2)}, u32[]{:S(2)}) %collective-permute-start.8) | collective-permute-done | bytes 270368 | tf_op jit(solution)/shard_map/ppermute | solution.py:235
  29.0 4.9 %collective-permute-done.14.first_ref = bf16[32,4224]{1,0:T(8,128)(2,1)S(1)} collective-permute-done((bf16[32,4224]{1,0:T(8,128)(2,1)S(1)}, bf16[32,4224]{1,0:T(8,128)(2,1)S(1)}, u32[]{:S(2)}, u32[]{:S(2)}) %collective-permute-start.14) | collective-permute-done | bytes 270368 | tf_op jit(solution)/shard_map/ppermute | solution.py:233
  34.8 2.4 %collective-permute-done.9.own_ref = bf16[32,4224]{1,0:T(8,128)(2,1)S(1)} collective-permute-done((bf16[32,4224]{1,0:T(8,128)(2,1)S(1)}, bf16[32,4224]{1,0:T(8,128)(2,1)S(1)}, u32[]{:S(2)}, u32[]{:S(2)}) %collective-permute-start.9) | collective-permute-done | bytes 270368 | tf_op jit(solution)/shard_map/ppermute | solution.py:235
  38.0 5.6 %collective-permute-done.10.first_ref = bf16[32,4224]{1,0:T(8,128)(2,1)S(1)} collective-permute-done((bf16[32,4224]{1,0:T(8,128)(2,1)S(1)}, bf16[32,4224]{1,0:T(8,128)(2,1)S(1)}, u32[]{:S(2)}, u32[]{:S(2)}) %collective-permute-start.10) | collective-permute-done | bytes 270368 | tf_op jit(solution)/shard_map/ppermute | solution.py:233
  44.2 1.6 %collective-permute-start.15 = (bf16[64,4224]{1,0:T(8,128)(2,1)S(1)}, bf16[64,4224]{1,0:T(8,128)(2,1)S(1)}, u32[]{:S(2)}, u32[]{:S(2)}) collective-permute-start(bf16[64,4224]{1,0:T(8,128)(2,1)S(1)} %pad_maximum_fusion.4), channel_id=1, source_target_pairs={{0,4},{1,3},{2,6},{3,1},{4,0},{5,7},{6,2},{7,5},{8,12},{9,11},{10,... | collective-permute-start | bytes 1622024 | tf_op jit(solution)/shard_map/ppermute | solution.py:234
  46.3 2.5 %pad_maximum_fusion.gate_up_ref = bf16[2048,1536]{1,0:T(8,128)(2,1)S(1)} fusion(bf16[2048,384]{1,0:T(8,128)(2,1)S(1)} %collective-permute-done.3, bf16[2048,384]{1,0:T(8,128)(2,1)S(1)} %bitcast.6, bf16[2048,384]{1,0:T(8,128)(2,1)} %collective-permute-done.2, bf16[2048,384]{1,0:T(8,128)(2,1)S(1)} %bitcast.8), kind=kLoop, calls=%fused_computation | loop fusion | flops 25165824 | bytes 12582912 | tf_op jit(solution)/shard_map/concatenate | solution.py:240
  48.9 1.8 %pad_maximum_fusion.1.down_ref = bf16[768,2048]{1,0:T(8,128)(2,1)S(1)} fusion(bf16[384,2048]{1,0:T(8,128)(2,1)} %collective-permute-done.4, bf16[384,2048]{1,0:T(8,128)(2,1)S(1)} %bitcast.10), kind=kLoop, calls=%fused_computation.1 | loop fusion | flops 6291456 | bytes 6291456 | tf_op jit(solution)/shard_map/concatenate | solution.py:241
  50.7 2.3 %collective-permute-done.19.rest_ref = bf16[64,4224]{1,0:T(8,128)(2,1)S(1)} collective-permute-done((bf16[64,4224]{1,0:T(8,128)(2,1)S(1)}, bf16[64,4224]{1,0:T(8,128)(2,1)S(1)}, u32[]{:S(2)}, u32[]{:S(2)}) %collective-permute-start.19) | collective-permute-done | bytes 540704 | tf_op jit(solution)/shard_map/ppermute | solution.py:234
  53.0 4.3 %expert.7 = (bf16[64,2176]{1,0:T(8,128)(2,1)S(1)}, bf16[64,2176]{1,0:T(8,128)(2,1)S(1)}) custom-call(s32[1]{0:T(128)} %bitcast.1.expert_ref, bf16[32,4224]{1,0:T(8,128)(2,1)S(1)} %collective-permute-done.7.own_ref, bf16[32,4224]{1,0:T(8,128)(2,1)S(1)} %collective-permute-done.18.first_ref, bf16[64,4224]{1,0:T(8,128)(2,1)S(1)} %collective-permute-done.19.rest_ref, ...), custom_call_target="tpu_custom_call" | custom-call | flops 2013265920 | bytes 9437184 | tf_op jit(solution)/shard_map/expert/pallas_call | solution.py:168
  58.8 4.3 %expert.6 = (bf16[64,2176]{1,0:T(8,128)(2,1)S(1)}, bf16[64,2176]{1,0:T(8,128)(2,1)S(1)}) custom-call(s32[1]{0:T(128)} %bitcast.1.expert_ref, bf16[32,4224]{1,0:T(8,128)(2,1)S(1)} %collective-permute-done.8.own_ref, bf16[32,4224]{1,0:T(8,128)(2,1)S(1)} %collective-permute-done.14.first_ref, bf16[64,4224]{1,0:T(8,128)(2,1)S(1)} %collective-permute-done.15.rest_ref, ...), custom_call_target="tpu_custom_call" | custom-call | flops 2013265920 | bytes 9437184 | tf_op jit(solution)/shard_map/expert/pallas_call | solution.py:168
  63.9 4.3 %expert.4 = (bf16[64,2176]{1,0:T(8,128)(2,1)S(1)}, bf16[64,2176]{1,0:T(8,128)(2,1)S(1)}) custom-call(s32[1]{0:T(128)} %bitcast.1.expert_ref, bf16[32,4224]{1,0:T(8,128)(2,1)S(1)} %copy-done, bf16[32,4224]{1,0:T(8,128)(2,1)S(1)} %collective-permute-done.first_ref, bf16[64,4224]{1,0:T(8,128)(2,1)S(1)} %collective-permute-done.1.rest_ref, ...), custom_call_target="tpu_custom_call" | custom-call | flops 2013265920 | bytes 9437184 | tf_op jit(solution)/shard_map/expert/pallas_call | solution.py:168
  69.6 4.3 %expert.5 = (bf16[64,2176]{1,0:T(8,128)(2,1)S(1)}, bf16[64,2176]{1,0:T(8,128)(2,1)S(1)}) custom-call(s32[1]{0:T(128)} %bitcast.1.expert_ref, bf16[32,4224]{1,0:T(8,128)(2,1)S(1)} %collective-permute-done.9.own_ref, bf16[32,4224]{1,0:T(8,128)(2,1)S(1)} %collective-permute-done.10.first_ref, bf16[64,4224]{1,0:T(8,128)(2,1)S(1)} %collective-permute-done.11.rest_ref, ...), custom_call_target="tpu_custom_call" | custom-call | flops 2013265920 | bytes 9437184 | tf_op jit(solution)/shard_map/expert/pallas_call | solution.py:168
  74.7 1.9 %collective-permute-start.21 = (bf16[32,2176]{1,0:T(8,128)(2,1)S(1)}, bf16[32,2176]{1,0:T(8,128)(2,1)S(1)}, u32[]{:S(2)}, u32[]{:S(2)}) collective-permute-start(bf16[32,2176]{1,0:T(8,128)(2,1)S(1)} %add_convert_fusion.4), channel_id=1, source_target_pairs={{0,2},{1,5},{2,0},{3,7},{4,6},{5,1},{6,4},{7,3},{8,10},{9,13},{10,... | collective-permute-start | bytes 417800 | tf_op jit(solution)/shard_map/ppermute | solution.py:233
  76.9 2.9 %collective-permute-done.21 = bf16[32,2176]{1,0:T(8,128)(2,1)S(1)} collective-permute-done((bf16[32,2176]{1,0:T(8,128)(2,1)S(1)}, bf16[32,2176]{1,0:T(8,128)(2,1)S(1)}, u32[]{:S(2)}, u32[]{:S(2)}) %collective-permute-start.21) | collective-permute-done | bytes 139296 | tf_op jit(solution)/shard_map/ppermute | solution.py:233
  80.0 2.5 %collective-permute-done.12 = bf16[64,2176]{1,0:T(8,128)(2,1)S(1)} collective-permute-done((bf16[64,2176]{1,0:T(8,128)(2,1)S(1)}, bf16[64,2176]{1,0:T(8,128)(2,1)S(1)}, u32[]{:S(2)}, u32[]{:S(2)}) %collective-permute-start.12) | collective-permute-done | bytes 278560 | tf_op jit(solution)/shard_map/ppermute | solution.py:234
  83.0 3.8 %collective-permute-done.22 = bf16[32,2176]{1,0:T(8,128)(2,1)S(1)} collective-permute-done((bf16[32,2176]{1,0:T(8,128)(2,1)S(1)}, bf16[32,2176]{1,0:T(8,128)(2,1)S(1)}, u32[]{:S(2)}, u32[]{:S(2)}) %collective-permute-start.22) | collective-permute-done | bytes 139296 | tf_op jit(solution)/shard_map/ppermute | solution.py:235
  87.0 2.3 %collective-permute-start.6 = (bf16[32,2176]{1,0:T(8,128)(2,1)S(1)}, bf16[32,2176]{1,0:T(8,128)(2,1)S(1)}, u32[]{:S(2)}, u32[]{:S(2)}) collective-permute-start(bf16[32,2176]{1,0:T(8,128)(2,1)S(1)} %add_convert_fusion.7), channel_id=1, source_target_pairs={{0,2},{1,5},{2,0},{3,7},{4,6},{5,1},{6,4},{7,3},{8,10},{9,13},{10,... | collective-permute-start | bytes 417800 | tf_op jit(solution)/shard_map/ppermute | solution.py:233
  89.3 4.5 %collective-permute-done.23 = bf16[32,2176]{1,0:T(8,128)(2,1)S(1)} collective-permute-done((bf16[32,2176]{1,0:T(8,128)(2,1)S(1)}, bf16[32,2176]{1,0:T(8,128)(2,1)S(1)}, u32[]{:S(2)}, u32[]{:S(2)}) %collective-permute-start.23) | collective-permute-done | bytes 139296 | tf_op jit(solution)/shard_map/ppermute | solution.py:235
  94.0 6.8 %collective-permute-done.24 = bf16[32,2176]{1,0:T(8,128)(2,1)S(1)} collective-permute-done((bf16[32,2176]{1,0:T(8,128)(2,1)S(1)}, bf16[32,2176]{1,0:T(8,128)(2,1)S(1)}, u32[]{:S(2)}, u32[]{:S(2)}) %collective-permute-start.24) | collective-permute-done | bytes 139296 | tf_op jit(solution)/shard_map/ppermute | solution.py:235
  103.0 2.8 %finish.1 = (bf16[64,2048]{1,0:T(8,128)(2,1)}, f32[64,8]{1,0:T(8,128)}) custom-call(s32[1]{0:T(128)} %bitcast.half_ref, bf16[32,2176]{1,0:T(8,128)(2,1)} %copy-done.4, bf16[32,2176]{1,0:T(8,128)(2,1)} %copy-done.5, s32[64,8]{1,0:T(8,128)} %copy.9.ids_ref), custom_call_target="tpu_custom_call" | custom-call | tf_op jit(solution)/shard_map/finish/pallas_call | solution.py:200
  (64 shorter events, 19.3 us)
Async XLA Ops:
  5.2 11.7 %collective-permute-start.7 = (bf16[32,4224]{1,0:T(8,128)(2,1)}, bf16[32,4224]{1,0:T(8,128)(2,1)S(1)}, u32[]{:S(2)}, u32[]{:S(2)}) collective-permute-start(bf16[32,4224]{1,0:T(8,128)(2,1)} %pack.1.own_ref), channel_id=1, source_target_pairs={{0,8},{2,10},{4,12},{6,14},{8,16},{10,18},{12,20},{14,22},{16,24},... | collective-permute-start | bytes 811016 | tf_op jit(solution)/shard_map/ppermute | solution.py:235
  8.3 10.2 %collective-permute-start = (bf16[32,4224]{1,0:T(8,128)(2,1)}, bf16[32,4224]{1,0:T(8,128)(2,1)S(1)}, u32[]{:S(2)}, u32[]{:S(2)}) collective-permute-start(bf16[32,4224]{1,0:T(8,128)(2,1)} %pack.1.own_ref), channel_id=1, source_target_pairs={{0,2},{1,5},{2,0},{3,7},{4,6},{5,1},{6,4},{7,3},{8,10},{9,13},{10,... | collective-permute-start | bytes 811016 | tf_op jit(solution)/shard_map/ppermute | solution.py:233
  9.8 34.5 %collective-permute-start.3 = (bf16[2048,384]{1,0:T(8,128)(2,1)}, bf16[2048,384]{1,0:T(8,128)(2,1)S(1)}, u32[]{:S(2)}, u32[]{:S(2)}) collective-permute-start(bf16[2048,384]{1,0:T(8,128)(2,1)} %bitcast.5), channel_id=1, source_target_pairs={{0,1},{1,0},{2,3},{3,2},{4,5},{5,4},{6,7},{7,6},{8,9},{9,8},{10,11... | collective-permute-start | bytes 4718600 | tf_op jit(solution)/shard_map/ppermute | solution.py:236
  9.8 36.1 %collective-permute-start.2 = (bf16[2048,384]{1,0:T(8,128)(2,1)}, bf16[2048,384]{1,0:T(8,128)(2,1)}, u32[]{:S(2)}, u32[]{:S(2)}) collective-permute-start(bf16[2048,384]{1,0:T(8,128)(2,1)} %bitcast.7), channel_id=1, source_target_pairs={{0,1},{1,0},{2,3},{3,2},{4,5},{5,4},{6,7},{7,6},{8,9},{9,8},{10,11... | collective-permute-start | bytes 4718600 | tf_op jit(solution)/shard_map/ppermute | solution.py:236
  10.3 38.6 %collective-permute-start.4 = (bf16[384,2048]{1,0:T(8,128)(2,1)}, bf16[384,2048]{1,0:T(8,128)(2,1)}, u32[]{:S(2)}, u32[]{:S(2)}) collective-permute-start(bf16[384,2048]{1,0:T(8,128)(2,1)} %bitcast.9), channel_id=1, source_target_pairs={{0,1},{1,0},{2,3},{3,2},{4,5},{5,4},{6,7},{7,6},{8,9},{9,8},{10,11... | collective-permute-start | bytes 4718600 | tf_op jit(solution)/shard_map/ppermute | solution.py:236
  17.0 12.0 %collective-permute-start.18 = (bf16[32,4224]{1,0:T(8,128)(2,1)S(1)}, bf16[32,4224]{1,0:T(8,128)(2,1)S(1)}, u32[]{:S(2)}, u32[]{:S(2)}) collective-permute-start(bf16[32,4224]{1,0:T(8,128)(2,1)S(1)} %collective-permute-done.7.own_ref), channel_id=1, source_target_pairs={{0,2},{1,5},{2,0},{3,7},{4,6},{5,1},{6,4},{7,3},{8,10},{9,13},{10,... | collective-permute-start | bytes 811016 | tf_op jit(solution)/shard_map/ppermute | solution.py:233
  18.5 9.0 %collective-permute-start.8 = (bf16[32,4224]{1,0:T(8,128)(2,1)S(1)}, bf16[32,4224]{1,0:T(8,128)(2,1)S(1)}, u32[]{:S(2)}, u32[]{:S(2)}) collective-permute-start(bf16[32,4224]{1,0:T(8,128)(2,1)S(1)} %collective-permute-done.7.own_ref), channel_id=1, source_target_pairs={{0,8},{2,10},{4,12},{6,14},{8,16},{10,18},{12,20},{14,22},{16,24},... | collective-permute-start | bytes 811016 | tf_op jit(solution)/shard_map/ppermute | solution.py:235
  27.4 6.5 %collective-permute-start.14 = (bf16[32,4224]{1,0:T(8,128)(2,1)S(1)}, bf16[32,4224]{1,0:T(8,128)(2,1)S(1)}, u32[]{:S(2)}, u32[]{:S(2)}) collective-permute-start(bf16[32,4224]{1,0:T(8,128)(2,1)S(1)} %collective-permute-done.8.own_ref), channel_id=1, source_target_pairs={{0,2},{1,5},{2,0},{3,7},{4,6},{5,1},{6,4},{7,3},{8,10},{9,13},{10,... | collective-permute-start | bytes 811016 | tf_op jit(solution)/shard_map/ppermute | solution.py:233
  28.9 8.3 %collective-permute-start.9 = (bf16[32,4224]{1,0:T(8,128)(2,1)S(1)}, bf16[32,4224]{1,0:T(8,128)(2,1)S(1)}, u32[]{:S(2)}, u32[]{:S(2)}) collective-permute-start(bf16[32,4224]{1,0:T(8,128)(2,1)S(1)} %collective-permute-done.8.own_ref), channel_id=1, source_target_pairs={{0,8},{2,10},{4,12},{6,14},{8,16},{10,18},{12,20},{14,22},{16,24},... | collective-permute-start | bytes 811016 | tf_op jit(solution)/shard_map/ppermute | solution.py:235
  33.9 30.0 %collective-permute-start.1 = (bf16[64,4224]{1,0:T(8,128)(2,1)S(1)}, bf16[64,4224]{1,0:T(8,128)(2,1)S(1)}, u32[]{:S(2)}, u32[]{:S(2)}) collective-permute-start(bf16[64,4224]{1,0:T(8,128)(2,1)S(1)} %pad_maximum_fusion.2), channel_id=1, source_target_pairs={{0,4},{1,3},{2,6},{3,1},{4,0},{5,7},{6,2},{7,5},{8,12},{9,11},{10,... | collective-permute-start | bytes 1622024 | tf_op jit(solution)/shard_map/ppermute | solution.py:234
  37.2 6.5 %collective-permute-start.10 = (bf16[32,4224]{1,0:T(8,128)(2,1)S(1)}, bf16[32,4224]{1,0:T(8,128)(2,1)S(1)}, u32[]{:S(2)}, u32[]{:S(2)}) collective-permute-start(bf16[32,4224]{1,0:T(8,128)(2,1)S(1)} %collective-permute-done.9.own_ref), channel_id=1, source_target_pairs={{0,2},{1,5},{2,0},{3,7},{4,6},{5,1},{6,4},{7,3},{8,10},{9,13},{10,... | collective-permute-start | bytes 811016 | tf_op jit(solution)/shard_map/ppermute | solution.py:233
  43.7 9.4 %collective-permute-start.19 = (bf16[64,4224]{1,0:T(8,128)(2,1)S(1)}, bf16[64,4224]{1,0:T(8,128)(2,1)S(1)}, u32[]{:S(2)}, u32[]{:S(2)}) collective-permute-start(bf16[64,4224]{1,0:T(8,128)(2,1)S(1)} %pad_maximum_fusion.5), channel_id=1, source_target_pairs={{0,4},{1,3},{2,6},{3,1},{4,0},{5,7},{6,2},{7,5},{8,12},{9,11},{10,... | collective-permute-start | bytes 1622024 | tf_op jit(solution)/shard_map/ppermute | solution.py:234
  44.2 14.6 %collective-permute-start.15 = (bf16[64,4224]{1,0:T(8,128)(2,1)S(1)}, bf16[64,4224]{1,0:T(8,128)(2,1)S(1)}, u32[]{:S(2)}, u32[]{:S(2)}) collective-permute-start(bf16[64,4224]{1,0:T(8,128)(2,1)S(1)} %pad_maximum_fusion.4), channel_id=1, source_target_pairs={{0,4},{1,3},{2,6},{3,1},{4,0},{5,7},{6,2},{7,5},{8,12},{9,11},{10,... | collective-permute-start | bytes 1622024 | tf_op jit(solution)/shard_map/ppermute | solution.py:234
  45.8 23.8 %collective-permute-start.11 = (bf16[64,4224]{1,0:T(8,128)(2,1)S(1)}, bf16[64,4224]{1,0:T(8,128)(2,1)S(1)}, u32[]{:S(2)}, u32[]{:S(2)}) collective-permute-start(bf16[64,4224]{1,0:T(8,128)(2,1)S(1)} %pad_maximum_fusion.3), channel_id=1, source_target_pairs={{0,4},{1,3},{2,6},{3,1},{4,0},{5,7},{6,2},{7,5},{8,12},{9,11},{10,... | collective-permute-start | bytes 1622024 | tf_op jit(solution)/shard_map/ppermute | solution.py:234
  57.4 17.3 %collective-permute-start.20 = (bf16[64,2176]{1,0:T(8,128)(2,1)S(1)}, bf16[64,2176]{1,0:T(8,128)(2,1)S(1)}, u32[]{:S(2)}, u32[]{:S(2)}) collective-permute-start(bf16[64,2176]{1,0:T(8,128)(2,1)S(1)} %get-tuple-element.19), channel_id=1, source_target_pairs={{0,4},{1,3},{2,6},{3,1},{4,0},{5,7},{6,2},{7,5},{8,12},{9,11},{10,... | collective-permute-start | bytes 835592 | tf_op jit(solution)/shard_map/ppermute | solution.py:234
  63.1 13.5 %collective-permute-start.16 = (bf16[64,2176]{1,0:T(8,128)(2,1)S(1)}, bf16[64,2176]{1,0:T(8,128)(2,1)S(1)}, u32[]{:S(2)}, u32[]{:S(2)}) collective-permute-start(bf16[64,2176]{1,0:T(8,128)(2,1)S(1)} %get-tuple-element.17), channel_id=1, source_target_pairs={{0,4},{1,3},{2,6},{3,1},{4,0},{5,7},{6,2},{7,5},{8,12},{9,11},{10,... | collective-permute-start | bytes 835592 | tf_op jit(solution)/shard_map/ppermute | solution.py:234
  68.2 18.8 %collective-permute-start.5 = (bf16[64,2176]{1,0:T(8,128)(2,1)S(1)}, bf16[64,2176]{1,0:T(8,128)(2,1)S(1)}, u32[]{:S(2)}, u32[]{:S(2)}) collective-permute-start(bf16[64,2176]{1,0:T(8,128)(2,1)S(1)} %get-tuple-element.13), channel_id=1, source_target_pairs={{0,4},{1,3},{2,6},{3,1},{4,0},{5,7},{6,2},{7,5},{8,12},{9,11},{10,... | collective-permute-start | bytes 835592 | tf_op jit(solution)/shard_map/ppermute | solution.py:234
  74.0 8.5 %collective-permute-start.12 = (bf16[64,2176]{1,0:T(8,128)(2,1)S(1)}, bf16[64,2176]{1,0:T(8,128)(2,1)S(1)}, u32[]{:S(2)}, u32[]{:S(2)}) collective-permute-start(bf16[64,2176]{1,0:T(8,128)(2,1)S(1)} %get-tuple-element.15), channel_id=1, source_target_pairs={{0,4},{1,3},{2,6},{3,1},{4,0},{5,7},{6,2},{7,5},{8,12},{9,11},{10,... | collective-permute-start | bytes 835592 | tf_op jit(solution)/shard_map/ppermute | solution.py:234
  76.7 6.3 %collective-permute-start.17 = (bf16[32,2176]{1,0:T(8,128)(2,1)S(1)}, bf16[32,2176]{1,0:T(8,128)(2,1)S(1)}, u32[]{:S(2)}, u32[]{:S(2)}) collective-permute-start(bf16[32,2176]{1,0:T(8,128)(2,1)S(1)} %add_convert_fusion.5), channel_id=1, source_target_pairs={{0,2},{1,5},{2,0},{3,7},{4,6},{5,1},{6,4},{7,3},{8,10},{9,13},{10,... | collective-permute-start | bytes 417800 | tf_op jit(solution)/shard_map/ppermute | solution.py:233
  79.9 6.9 %collective-permute-start.22 = (bf16[32,2176]{1,0:T(8,128)(2,1)S(1)}, bf16[32,2176]{1,0:T(8,128)(2,1)S(1)}, u32[]{:S(2)}, u32[]{:S(2)}) collective-permute-start(bf16[32,2176]{1,0:T(8,128)(2,1)S(1)} %add_convert_fusion.3), channel_id=1, source_target_pairs={{0,8},{2,10},{4,12},{6,14},{8,16},{10,18},{12,20},{14,22},{16,24},... | collective-permute-start | bytes 417800 | tf_op jit(solution)/shard_map/ppermute | solution.py:235
  82.5 6.8 %collective-permute-start.13 = (bf16[32,2176]{1,0:T(8,128)(2,1)S(1)}, bf16[32,2176]{1,0:T(8,128)(2,1)S(1)}, u32[]{:S(2)}, u32[]{:S(2)}) collective-permute-start(bf16[32,2176]{1,0:T(8,128)(2,1)S(1)} %add_convert_fusion.6), channel_id=1, source_target_pairs={{0,2},{1,5},{2,0},{3,7},{4,6},{5,1},{6,4},{7,3},{8,10},{9,13},{10,... | collective-permute-start | bytes 417800 | tf_op jit(solution)/shard_map/ppermute | solution.py:233
  86.9 6.9 %collective-permute-start.23 = (bf16[32,2176]{1,0:T(8,128)(2,1)S(1)}, bf16[32,2176]{1,0:T(8,128)(2,1)S(1)}, u32[]{:S(2)}, u32[]{:S(2)}) collective-permute-start(bf16[32,2176]{1,0:T(8,128)(2,1)S(1)} %add_convert_fusion.2), channel_id=1, source_target_pairs={{0,8},{2,10},{4,12},{6,14},{8,16},{10,18},{12,20},{14,22},{16,24},... | collective-permute-start | bytes 417800 | tf_op jit(solution)/shard_map/ppermute | solution.py:235
  87.0 6.9 %collective-permute-start.6 = (bf16[32,2176]{1,0:T(8,128)(2,1)S(1)}, bf16[32,2176]{1,0:T(8,128)(2,1)S(1)}, u32[]{:S(2)}, u32[]{:S(2)}) collective-permute-start(bf16[32,2176]{1,0:T(8,128)(2,1)S(1)} %add_convert_fusion.7), channel_id=1, source_target_pairs={{0,2},{1,5},{2,0},{3,7},{4,6},{5,1},{6,4},{7,3},{8,10},{9,13},{10,... | collective-permute-start | bytes 417800 | tf_op jit(solution)/shard_map/ppermute | solution.py:233
  93.9 6.9 %collective-permute-start.24 = (bf16[32,2176]{1,0:T(8,128)(2,1)S(1)}, bf16[32,2176]{1,0:T(8,128)(2,1)S(1)}, u32[]{:S(2)}, u32[]{:S(2)}) collective-permute-start(bf16[32,2176]{1,0:T(8,128)(2,1)S(1)} %add_convert_fusion.1), channel_id=1, source_target_pairs={{0,8},{2,10},{4,12},{6,14},{8,16},{10,18},{12,20},{14,22},{16,24},... | collective-permute-start | bytes 417800 | tf_op jit(solution)/shard_map/ppermute | solution.py:235
  (8 other events, 73.5 us)

commit v2 on v1

--- a/solution.py
+++ b/solution.py
@@ -8,6 +8,9 @@
 from jax.sharding import PartitionSpec as P
 
 LANES = 128
+LAG = 10000000000
+EFLOPS = 5000000000
+CONTRACT_LAST = (((1,), (1,)), ((), ()))
 
 
 def expert_terms(rows, grads, gate_one, up_one, down_one):
@@ -93,23 +96,26 @@
     rows, width = tok_ref.shape
     out_ref[:, 0:width] = tok_ref[...]
     out_ref[:, width : 2 * width] = cot_ref[...]
-    lane = lax.broadcasted_iota(jnp.int32, (rows, out_ref.shape[1] - 2 * width), 1)
-    total = jnp.zeros(lane.shape, jnp.float32)
-    weights = gw_ref[...]
-    high = weights.astype(jnp.bfloat16).astype(jnp.float32)
-    low = weights - high
-    ids = ids_ref[...]
-    for k in range(ids.shape[1]):
-        one = ids[:, k : k + 1]
-        total = jnp.where(lane == one, high[:, k : k + 1], total)
-        total = jnp.where(lane == one + experts, low[:, k : k + 1], total)
-    out_ref[:, 2 * width :] = total.astype(jnp.bfloat16)
+    top, count = ids_ref.shape
+    slot = lax.broadcasted_iota(jnp.int32, (out_ref.shape[1] - 2 * width, count), 0)
+    total = jnp.zeros(slot.shape, jnp.float32)
+    for k in range(top):
+        one, weight = ids_ref[k : k + 1, :], gw_ref[k : k + 1, :]
+        high = weight.astype(jnp.bfloat16).astype(jnp.float32)
+        total = jnp.where(slot == one, high, total)
+        total = jnp.where(slot == one + experts, weight - high, total)
+    row = lax.broadcasted_iota(jnp.int32, (rows, count), 0) + half_ref[0] * rows
+    pick = (row == lax.broadcasted_iota(jnp.int32, (rows, count), 1)).astype(jnp.bfloat16)
+    out_ref[:, 2 * width :] = lax.dot_general(
+        pick, total.astype(jnp.bfloat16), CONTRACT_LAST, preferred_element_type=jnp.float32
+    ).astype(jnp.bfloat16)
 
 
 def pack(half, tokens, cotangent, expert_ids, gate_weights, experts):
     tok_count, width = tokens.shape
     rows, top = tok_count // 2, expert_ids.shape[1]
     own = lambda i, half: (half[0], 0)
+    whole = lambda i, half: (0, 0)
     return pl.pallas_call(
         functools.partial(pack_kernel, experts),
         grid_spec=pltpu.PrefetchScalarGridSpec(
@@ -118,24 +124,24 @@
             in_specs=[
                 pl.BlockSpec((rows, width), own),
                 pl.BlockSpec((rows, width), own),
-                pl.BlockSpec((rows, top), own),
-                pl.BlockSpec((rows, top), own),
+                pl.BlockSpec((top, tok_count), whole),
+                pl.BlockSpec((top, tok_count), whole),
             ],
-            out_specs=pl.BlockSpec((rows, 2 * width + padded(2 * experts)), lambda i, half: (0, 0)),
+            out_specs=pl.BlockSpec((rows, 2 * width + padded(2 * experts)), whole),
         ),
         out_shape=jax.ShapeDtypeStruct((rows, 2 * width + padded(2 * experts)), jnp.bfloat16),
         name="pack",
-    )(half, tokens, cotangent, expert_ids, gate_weights)
-
-
-def expert_kernel(experts, expert_ref, own_ref, first_ref, rest_ref, gate_up_ref, down_ref, near_ref, far_ref):
-    rows = own_ref.shape[0]
+    )(half, tokens, cotangent, expert_ids.T, gate_weights.T)
+
+
+def expert_kernel(experts, expert_ref, gate_up_ref, down_ref, *refs):
+    shard_refs, out_refs = refs[: 2 * len(refs) // 3], refs[2 * len(refs) // 3 :]
+    rows = 2 * shard_refs[0].shape[0]
     width, units = gate_up_ref.shape[0], down_ref.shape[0]
-    contract_last = (((1,), (1,)), ((), ()))
-    packed = jnp.concatenate([own_ref[...], first_ref[...], rest_ref[...]], axis=0)
+    packed = jnp.concatenate([ref[...] for ref in shard_refs], axis=0)
     pre = jnp.dot(packed[:, :width], gate_up_ref[...], preferred_element_type=jnp.float32)
     grad_hidden = lax.dot_general(
-        packed[:, width : 2 * width], down_ref[...], contract_last, preferred_element_type=jnp.float32
+        packed[:, width : 2 * width], down_ref[...], CONTRACT_LAST, preferred_element_type=jnp.float32
     )
     gate_pre, up_pre = pre[:, :units], pre[:, units:]
     sigmoid_gate = 1.0 / (1.0 + jnp.exp(-gate_pre))
@@ -143,7 +149,7 @@
     scores = jnp.sum(grad_up * up_pre, axis=1, keepdims=True)
     grad_gate = grad_hidden * up_pre * sigmoid_gate * (1.0 + gate_pre * (1.0 - sigmoid_gate))
     grads = jnp.concatenate([grad_gate.astype(jnp.bfloat16), grad_up.astype(jnp.bfloat16)], axis=1)
-    part = lax.dot_general(grads, gate_up_ref[...], contract_last, preferred_element_type=jnp.float32)
+    part = lax.dot_general(grads, gate_up_ref[...], CONTRACT_LAST, preferred_element_type=jnp.float32)
     expert = expert_ref[0]
     routing = packed[:, 2 * width :].astype(jnp.float32)
     lane = lax.broadcasted_iota(jnp.int32, routing.shape, 1)
@@ -151,48 +157,64 @@
         jnp.where((lane == expert) | (lane == expert + experts), routing, 0.0), axis=1, keepdims=True
     )
     part = (part * weight).astype(jnp.bfloat16)
-    columns = near_ref.shape[1] - width
-    column = lax.broadcasted_iota(jnp.int32, (packed.shape[0], columns), 1)
+    column = lax.broadcasted_iota(jnp.int32, (packed.shape[0], out_refs[0].shape[1] - width), 1)
     score_part = jnp.where(column == expert, scores, 0.0).astype(jnp.bfloat16)
-    near_ref[:, :width] = part[: 2 * rows]
-    near_ref[:, width:] = score_part[: 2 * rows]
-    far_ref[:, :width] = part[2 * rows :]
-    far_ref[:, width:] = score_part[2 * rows :]
-
-
-def expert_call(expert, own, first, rest, gate_up, down, experts):
-    rows = own.shape[0]
+    for i, ref in enumerate(out_refs):
+        ref[:, :width] = part[i * rows : (i + 1) * rows]
+        ref[:, width:] = score_part[i * rows : (i + 1) * rows]
+
+
+def expert_call(expert, gate_up, down, experts, *shards):
+    rows = shards[0].shape[0]
     width, units = gate_up.shape[0], down.shape[0]
-    out = jax.ShapeDtypeStruct((2 * rows, width + padded(experts)), jnp.bfloat16)
+    outs = len(shards) // 2
     vmem = pl.BlockSpec(memory_space=pltpu.VMEM)
     return pl.pallas_call(
         functools.partial(expert_kernel, experts),
-        in_specs=[pl.BlockSpec(memory_space=pltpu.SMEM)] + [vmem] * 5,
-        out_specs=(vmem, vmem),
-        out_shape=(out, out),
+        in_specs=[pl.BlockSpec(memory_space=pltpu.SMEM)] + [vmem] * (2 + len(shards)),
+        out_specs=[vmem] * outs,
+        out_shape=[jax.ShapeDtypeStruct((2 * rows, width + padded(experts)), jnp.bfloat16)] * outs,
         compiler_params=pltpu.CompilerParams(vmem_limit_bytes=40 * 2**20),
-        cost_estimate=pl.CostEstimate(
-            flops=2 * 4 * rows * width * units * 5, bytes_accessed=gate_up.size * 3, transcendentals=0
-        ),
+        cost_estimate=pl.CostEstimate(flops=EFLOPS, bytes_accessed=1, transcendentals=0),
         name="expert",
-    )(expert, own, first, rest, gate_up, down)
+    )(expert, gate_up, down, *shards)
+
+
+def tie(*arrays, cost=1):
+    return pl.pallas_call(
+        lambda *refs: None,
+        in_specs=[pl.BlockSpec(memory_space=pl.ANY)] * len(arrays),
+        out_specs=[pl.BlockSpec(memory_space=pl.ANY)] * len(arrays),
+        out_shape=[jax.ShapeDtypeStruct(a.shape, a.dtype) for a in arrays],
+        input_output_aliases={i: i for i in range(len(arrays))},
+        compiler_params=pltpu.CompilerParams(vmem_limit_bytes=2**18),
+        cost_estimate=pl.CostEstimate(flops=cost, bytes_accessed=1, transcendentals=0),
+        name="tie",
+    )(*arrays)
 
 
 def finish_kernel(half_ref, own_ref, other_ref, ids_ref, grad_ref, score_ref):
     rows, width = own_ref.shape[0], grad_ref.shape[1]
     half = half_ref[0]
+    columns = own_ref.shape[1] - width
+    pair = lax.broadcasted_iota(jnp.int32, (columns, columns), 0)
+    same = (pair == lax.broadcasted_iota(jnp.int32, (columns, columns), 1)).astype(jnp.bfloat16)
+    scores = jnp.zeros((columns, 2 * rows), jnp.float32)
     for ref, place in ((own_ref, half), (other_ref, 1 - half)):
-        block = pl.ds(pl.multiple_of(place * rows, rows), rows)
-        grad_ref[block, :] = ref[:, :width]
-        scores = ref[:, width:].astype(jnp.float32)
-        column = lax.broadcasted_iota(jnp.int32, scores.shape, 1)
-        ids = ids_ref[block, :]
-        place_of = lax.broadcasted_iota(jnp.int32, ids.shape, 1)
-        total = jnp.zeros(ids.shape, jnp.float32)
-        for k in range(ids.shape[1]):
-            one = jnp.sum(jnp.where(column == ids[:, k : k + 1], scores, 0.0), axis=1, keepdims=True)
-            total = jnp.where(place_of == k, one, total)
-        score_ref[block, :] = total
+        grad_ref[pl.ds(pl.multiple_of(place * rows, rows), rows), :] = ref[:, :width]
+        row = lax.broadcasted_iota(jnp.int32, (2 * rows, rows), 0) - place * rows
+        spot = (row == lax.broadcasted_iota(jnp.int32, (2 * rows, rows), 1)).astype(jnp.bfloat16)
+        turned = lax.dot_general(same, ref[:, width:], CONTRACT_LAST, preferred_element_type=jnp.float32)
+        scores += lax.dot_general(
+            turned.astype(jnp.bfloat16), spot, CONTRACT_LAST, preferred_element_type=jnp.float32
+        )
+    expert = lax.broadcasted_iota(jnp.int32, scores.shape, 0)
+    place_of = lax.broadcasted_iota(jnp.int32, ids_ref.shape, 0)
+    total = jnp.zeros(ids_ref.shape, jnp.float32)
+    for k in range(ids_ref.shape[0]):
+        one = jnp.sum(jnp.where(expert == ids_ref[k : k + 1, :], scores, 0.0), axis=0, keepdims=True)
+        total = jnp.where(place_of == k, one, total)
+    score_ref[...] = total.astype(jnp.bfloat16)
 
 
 def finish(half, own, other, expert_ids, width):
@@ -203,11 +225,12 @@
         out_specs=(vmem, vmem),
         out_shape=(
             jax.ShapeDtypeStruct((expert_ids.shape[0], width), jnp.bfloat16),
-            jax.ShapeDtypeStruct(expert_ids.shape, jnp.float32),
+            jax.ShapeDtypeStruct(expert_ids.shape[::-1], jnp.bfloat16),
         ),
+        compiler_params=pltpu.CompilerParams(vmem_limit_bytes=4 * 2**20),
         name="finish",
-    )(half, own, other, expert_ids)
-    return grad, score.astype(jnp.bfloat16)
+    )(half, own, other, expert_ids.T)
+    return grad, score.T
 
 
 def added(*terms):
@@ -228,11 +251,9 @@
 
     first_pairs = [(e * 2 + h, (e ^ (1 + h)) * 2 + h) for e in range(experts) for h in range(halves)]
     second_pairs = [(e * 2 + h, (e ^ (2 - h)) * 2 + h) for e in range(experts) for h in range(halves)]
-    ring_pairs = [(e, (e + 4) % experts) for e in range(experts)]
     swap_pairs = [(0, 1), (1, 0)]
     to_first = lambda a: lax.ppermute(a, axes, first_pairs)
     to_second = lambda a: lax.ppermute(a, axes, second_pairs)
-    along_ring = lambda a: lax.ppermute(a, "expert", ring_pairs)
     swapped = lambda a: lax.ppermute(a, "half", swap_pairs)
 
     own = pack(half, tokens, cotangent, expert_ids, gate_weights, experts)
@@ -240,27 +261,48 @@
     gate_up = jnp.concatenate([gate_one, swapped(gate_one), up_one, swapped(up_one)], axis=1)
     down = jnp.concatenate([down_one, swapped(down_one)], axis=0)
 
-    planes = []
-    shard = own
+    shifted = lambda a, by: lax.ppermute(a, "expert", [(e, (e + 4 * by) % experts) for e in range(experts)])
+    shards, firsts, seconds, boths = [own], [], [], []
     for level in range(levels):
-        first = to_first(shard)
-        rest = to_second(jnp.concatenate([shard, first], axis=0))
-        planes.append((shard, first, rest))
-        if level < levels - 1:
-            shard = along_ring(shard)
-
-    sums = []
-    for shard, first, rest in planes:
-        near, far = expert_call(expert, shard, first, rest, gate_up, down, experts)
+        firsts.append(to_first(shards[level]))
+        seconds.append(to_second(shards[level]))
+        if level == levels - 1:
+            boths.append(shifted(boths[0], level))
+            break
+        following = shifted(shards[level], 1)
+        held = [following, firsts[level]]
+        if level > 1:
+            held += tie(seconds[level - 1], boths[level - 2], cost=LAG)
+        elif level > 0:
+            held.append(seconds[level - 1])
+        if level == levels - 2:
+            held += [gate_up, down]
+        held = tie(*held)
+        following, firsts[level] = held[:2]
+        if level > 0:
+            seconds[level - 1] = held[2]
+        if level > 1:
+            boths[level - 2] = held[3]
+        if level == levels - 2:
+            gate_up, down = held[-2:]
+        shards.append(following)
+        boths.append(to_second(firsts[level]))
+
+    total, results, previous = [], {}, None
+    for batch in ((1,0),(2,),(3,)):
+        planes = [[shards[i], firsts[i], seconds[i], boths[i]] for i in batch]
+        if previous is not None:
+            results[previous][1], planes[0][0] = tie(results[previous][1], planes[0][0])
+        outs = expert_call(expert, gate_up, down, experts, *sum(planes, []))
+        for i, level in enumerate(batch):
+            results[level] = list(outs[2 * i : 2 * i + 2])
+        previous = batch[0]
+    for level, (near, far) in results.items():
         from_second = to_second(far)
         from_first = to_first(added(near[rows:], from_second[rows:]))
-        sums.append((near[:rows], from_second[:rows], from_first))
-    carry = None
-    for level in list(range(1, levels)) + [0]:
-        terms = sums[level] if carry is None else sums[level] + (carry,)
-        carry = added(*terms)
-        if level:
-            carry = along_ring(carry)
+        terms = (near[:rows], from_second[:rows], from_first)
+        total += [shifted(added(*terms), levels - level)] if level else terms
+    carry = added(*total)
     return finish(half, carry, swapped(carry), expert_ids, width)
 
 
@@ -277,7 +319,7 @@
 
     def per_device(tokens, cotangent, expert_ids, *others):
         experts, top = mesh.shape["expert"], expert_ids.shape[1]
-        dense = experts <= 2 * top and experts % 4 == 0 and mesh.shape["half"] == 2
+        dense = 12 <= experts <= 2 * top and experts % 4 == 0 and mesh.shape["half"] == 2
         return (dense_plan if dense else routed_plan)(tokens, cotangent, expert_ids, *others)
 
     return jax.shard_map(

time: 109 us -> 85.8 us (0.79); the launches traced: 107 us -> 85.6 us
  waiting for transfers between devices: 52.7 us -> 31.2 us
  starting transfers between devices: 21 us -> 33.7 us
  Pallas kernels: 21.9 us -> 16.5 us
  local copies, waits for them, and re-layouts: 4.1 us -> 0.02 us
  other arithmetic: 6.64 us -> 3.32 us
    ppermute x6 -> x7, waiting for transfers between devices: 32.2 us -> 15.7 us  [dense_plan(): lax.ppermute(a, 'expert', [(e, (e + 4 * by) % experts) for e in range(exp...]
    ppermute x8 -> x11, starting transfers between devices: 6.97 us -> 14 us  [dense_plan(): to_second = lambda a: lax.ppermute(a, axes, second_pairs)]
    ppermute x6 -> x7, starting transfers between devices: 3.2 us -> 9.77 us  [dense_plan(): lax.ppermute(a, 'expert', [(e, (e + 4 * by) % experts) for e in range(exp...]
    ppermute x8, waiting for transfers between devices: 13.5 us -> 9.09 us  [dense_plan(): to_first = lambda a: lax.ppermute(a, axes, first_pairs)]
    unnamed x15 -> x10, local copies, waits for them, and re-layouts: 4.1 us -> 0.02 us
    pallas_call x4 -> x3, Pallas kernels: 17.3 us -> 13.7 us  [expert_call(): pl.pallas_call(functools.partial(expert_kernel, experts), in_specs=[pl.Bl...]
    pallas_call x1, Pallas kernels: 2.76 us -> 0.93 us  [finish(): pl.pallas_call(finish_kernel, in_specs=[pl.BlockSpec(memory_space=pltpu.S...]
    concatenate x1, other arithmetic: 1.81 us -> 0.37 us  [dense_plan(): down = jnp.concatenate([down_one, swapped(down_one)], axis=0)]
  transfers between devices with their start and end apart: 26 -> 30, of which waited for: 13 -> 11; matrix products, arithmetic and copies ran while one was open for 5% -> 4% of each run, Pallas kernels for 16% -> 16%
where the time goes in v2:
time: 85.8 us; the launch traced here: 85.6 us
  starting transfers between devices  33.7 us (39%)
  waiting for transfers between devices  31.2 us (36%)
  Pallas kernels  16.5 us (19%)
  other arithmetic  3.32 us (4%)
    ppermute x7, waiting for transfers between devices, dense_plan(): lax.ppermute(a, 'expert', [(e, (e + 4 * by) % experts) for e in range(exp...  15.7 us
    ppermute x11, starting transfers between devices, dense_plan(): to_second = lambda a: lax.ppermute(a, axes, second_pairs)  14 us
    pallas_call x3, Pallas kernels, expert_call(): pl.pallas_call(functools.partial(expert_kernel, experts), in_specs=[pl.Bl...  13.7 us
    ppermute x7, starting transfers between devices, dense_plan(): lax.ppermute(a, 'expert', [(e, (e + 4 * by) % experts) for e in range(exp...  9.77 us
    ppermute x8, starting transfers between devices, dense_plan(): to_first = lambda a: lax.ppermute(a, axes, first_pairs)  9.4 us
    ppermute x8, waiting for transfers between devices, dense_plan(): to_first = lambda a: lax.ppermute(a, axes, first_pairs)  9.09 us
    ppermute x11, waiting for transfers between devices, dense_plan(): to_second = lambda a: lax.ppermute(a, axes, second_pairs)  4.97 us
    concatenate x1, other arithmetic, dense_plan(): jnp.concatenate([gate_one, swapped(gate_one), up_one, swapped(up_one)], a...  2.53 us
  transfers between devices with their start and end apart: 30, of which 11 were waited for; matrix products, arithmetic and copies ran while one was open for 4% of the time, Pallas kernels for 16%

profile of v2, /device:TPU:0, one launch (start us, length us, event | category | flops | bytes accessed | tf_op | source)
XLA Modules:
  0.0 85.6 jit_solution(4637732760851383700)
XLA Ops:
  0.6 1.9 %pack.1.refs_4_ = bf16[32,4224]{1,0:T(8,128)(2,1)} custom-call(s32[1]{0:T(128)} %bitcast.half_ref, bf16[64,2048]{1,0:T(8,128)(2,1)} %tok_ref.1, bf16[64,2048]{1,0:T(8,128)(2,1)} %cot_ref.1, s32[8,64]{1,0:T(8,128)} %bitcast.8, f32[8,64]{1,0:T(8,128)} %bitcast.16), custom_call_target="tpu_custom_call" | custom-call | tf_op jit(solution)/shard_map/pack/pallas_call | solution.py:119
  2.5 3.0 %collective-permute-start = (bf16[32,4224]{1,0:T(8,128)(2,1)}, bf16[32,4224]{1,0:T(8,128)(2,1)S(1)}, u32[]{:S(2)}, u32[]{:S(2)}) collective-permute-start(bf16[32,4224]{1,0:T(8,128)(2,1)} %pack.1.refs_4_), channel_id=1, source_target_pairs={{0,8},{2,10},{4,12},{6,14},{8,16},{10,18},{12,20},{14,22},{16,24},... | collective-permute-start | bytes 811016 | tf_op jit(solution)/shard_map/ppermute | solution.py:264
  5.5 1.5 %collective-permute-start.1 = (bf16[32,4224]{1,0:T(8,128)(2,1)}, bf16[32,4224]{1,0:T(8,128)(2,1)S(1)}, u32[]{:S(2)}, u32[]{:S(2)}) collective-permute-start(bf16[32,4224]{1,0:T(8,128)(2,1)} %pack.1.refs_4_), channel_id=1, source_target_pairs={{0,2},{1,5},{2,0},{3,7},{4,6},{5,1},{6,4},{7,3},{8,10},{9,13},{10,... | collective-permute-start | bytes 811016 | tf_op jit(solution)/shard_map/ppermute | solution.py:255
  7.5 1.5 %collective-permute-start.4 = (bf16[32,4224]{1,0:T(8,128)(2,1)}, bf16[32,4224]{1,0:T(8,128)(2,1)S(1)}, u32[]{:S(2)}, u32[]{:S(2)}) collective-permute-start(bf16[32,4224]{1,0:T(8,128)(2,1)} %pack.1.refs_4_), channel_id=1, source_target_pairs={{0,4},{1,3},{2,6},{3,1},{4,0},{5,7},{6,2},{7,5},{8,12},{9,11},{10,... | collective-permute-start | bytes 811016 | tf_op jit(solution)/shard_map/ppermute | solution.py:256
  9.1 5.2 %collective-permute-done.refs_0_ = bf16[32,4224]{1,0:T(8,128)(2,1)S(1)} collective-permute-done((bf16[32,4224]{1,0:T(8,128)(2,1)}, bf16[32,4224]{1,0:T(8,128)(2,1)S(1)}, u32[]{:S(2)}, u32[]{:S(2)}) %collective-permute-start) | collective-permute-done | bytes 270368 | tf_op jit(solution)/shard_map/ppermute | solution.py:264
  15.6 2.2 %collective-permute-start.3 = (bf16[32,4224]{1,0:T(8,128)(2,1)S(1)}, bf16[32,4224]{1,0:T(8,128)(2,1)S(1)}, u32[]{:S(2)}, u32[]{:S(2)}) collective-permute-start(bf16[32,4224]{1,0:T(8,128)(2,1)S(1)} %get-tuple-element.29.refs_0_), channel_id=1, source_target_pairs={{0,2},{1,5},{2,0},{3,7},{4,6},{5,1},{6,4},{7,3},{8,10},{9,13},{10,... | collective-permute-start | bytes 811016 | tf_op jit(solution)/shard_map/ppermute | solution.py:255
  17.8 1.8 %collective-permute-start.7 = (bf16[32,4224]{1,0:T(8,128)(2,1)S(1)}, bf16[32,4224]{1,0:T(8,128)(2,1)S(1)}, u32[]{:S(2)}, u32[]{:S(2)}) collective-permute-start(bf16[32,4224]{1,0:T(8,128)(2,1)S(1)} %get-tuple-element.29.refs_0_), channel_id=1, source_target_pairs={{0,4},{1,3},{2,6},{3,1},{4,0},{5,7},{6,2},{7,5},{8,12},{9,11},{10,... | collective-permute-start | bytes 811016 | tf_op jit(solution)/shard_map/ppermute | solution.py:256
  19.6 4.1 %collective-permute-done.2.refs_0_ = bf16[32,4224]{1,0:T(8,128)(2,1)S(1)} collective-permute-done((bf16[32,4224]{1,0:T(8,128)(2,1)S(1)}, bf16[32,4224]{1,0:T(8,128)(2,1)S(1)}, u32[]{:S(2)}, u32[]{:S(2)}) %collective-permute-start.2) | collective-permute-done | bytes 270368 | tf_op jit(solution)/shard_map/ppermute | solution.py:264
  25.0 1.9 %collective-permute-start.5 = (bf16[32,4224]{1,0:T(8,128)(2,1)S(1)}, bf16[32,4224]{1,0:T(8,128)(2,1)S(1)}, u32[]{:S(2)}, u32[]{:S(2)}) collective-permute-start(bf16[32,4224]{1,0:T(8,128)(2,1)S(1)} %get-tuple-element.30.refs_1_), channel_id=1, source_target_pairs={{0,8},{2,10},{4,12},{6,14},{8,16},{10,18},{12,20},{14,22},{16,24},... | collective-permute-start | bytes 811016 | tf_op jit(solution)/shard_map/ppermute | solution.py:264
  26.9 3.3 %collective-permute-done.8.refs_1_ = bf16[32,4224]{1,0:T(8,128)(2,1)S(1)} collective-permute-done((bf16[32,4224]{1,0:T(8,128)(2,1)S(1)}, bf16[32,4224]{1,0:T(8,128)(2,1)S(1)}, u32[]{:S(2)}, u32[]{:S(2)}) %collective-permute-start.8) | collective-permute-done | bytes 270368 | tf_op jit(solution)/shard_map/ppermute | solution.py:256
  31.4 1.5 %collective-permute-start.18 = (bf16[32,4224]{1,0:T(8,128)(2,1)S(1)}, bf16[32,4224]{1,0:T(8,128)(2,1)S(1)}, u32[]{:S(2)}, u32[]{:S(2)}) collective-permute-start(bf16[32,4224]{1,0:T(8,128)(2,1)S(1)} %get-tuple-element.30.refs_1_), channel_id=1, source_target_pairs={{0,4},{1,3},{2,6},{3,1},{4,0},{5,7},{6,2},{7,5},{8,12},{9,11},{10,... | collective-permute-start | bytes 811016 | tf_op jit(solution)/shard_map/ppermute | solution.py:256
  33.5 2.5 %pad_maximum_fusion.refs_4_ = bf16[2048,1536]{1,0:T(8,128)(2,1)S(1)} fusion(bf16[2048,384]{1,0:T(8,128)(2,1)S(1)} %collective-permute-done.10, bf16[2048,384]{1,0:T(8,128)(2,1)S(1)} %bitcast.11, bf16[2048,384]{1,0:T(8,128)(2,1)} %collective-permute-done.9, bf16[2048,384]{1,0:T(8,128)(2,1)S(1)} %bitcast.13), kind=kLoop, calls=%fused_computation | loop fusion | flops 25165824 | bytes 12582912 | tf_op jit(solution)/shard_map/concatenate | solution.py:261
  36.4 3.2 %collective-permute-done.6.refs_1_ = bf16[32,4224]{1,0:T(8,128)(2,1)S(1)} collective-permute-done((bf16[32,4224]{1,0:T(8,128)(2,1)S(1)}, bf16[32,4224]{1,0:T(8,128)(2,1)S(1)}, u32[]{:S(2)}, u32[]{:S(2)}) %collective-permute-start.6) | collective-permute-done | bytes 270368 | tf_op jit(solution)/shard_map/ppermute | solution.py:255
  40.8 1.5 %collective-permute-start.24 = (bf16[32,4224]{1,0:T(8,128)(2,1)S(1)}, bf16[32,4224]{1,0:T(8,128)(2,1)S(1)}, u32[]{:S(2)}, u32[]{:S(2)}) collective-permute-start(bf16[32,4224]{1,0:T(8,128)(2,1)S(1)} %get-tuple-element.49.refs_1_), channel_id=1, source_target_pairs={{0,4},{1,3},{2,6},{3,1},{4,0},{5,7},{6,2},{7,5},{8,12},{9,11},{10,... | collective-permute-start | bytes 811016 | tf_op jit(solution)/shard_map/ppermute | solution.py:256
  43.4 5.0 %expert.3 = (bf16[64,2176]{1,0:T(8,128)(2,1)S(1)}, bf16[64,2176]{1,0:T(8,128)(2,1)S(1)}, bf16[64,2176]{1,0:T(8,128)(2,1)S(1)}, bf16[64,2176]{1,0:T(8,128)(2,1)S(1)}) custom-call(s32[1]{0:T(128)} %bitcast.1.expert_ref, bf16[2048,1536]{1,0:T(8,128)(2,1)S(1)} %get-tuple-element.34.gate_up_ref, bf16[768,2048]{1,0:T(8,128)(2,1)S(1)} %get-tuple-element.35.down_ref, ...), custom_call_target="tpu_custom_call" | custom-call | flops 5000000000 | bytes 1 | tf_op jit(solution)/shard_map/expert/pallas_call | solution.py:172
  48.5 1.8 %collective-permute-start.13 = (bf16[64,2176]{1,0:T(8,128)(2,1)S(1)}, bf16[64,2176]{1,0:T(8,128)(2,1)S(1)}, u32[]{:S(2)}, u32[]{:S(2)}) collective-permute-start(bf16[64,2176]{1,0:T(8,128)(2,1)S(1)} %get-tuple-element.42), channel_id=1, source_target_pairs={{0,4},{1,3},{2,6},{3,1},{4,0},{5,7},{6,2},{7,5},{8,12},{9,11},{10,... | collective-permute-start | bytes 835592 | tf_op jit(solution)/shard_map/ppermute | solution.py:256
  51.7 4.3 %expert.4 = (bf16[64,2176]{1,0:T(8,128)(2,1)S(1)}, bf16[64,2176]{1,0:T(8,128)(2,1)S(1)}) custom-call(s32[1]{0:T(128)} %bitcast.1.expert_ref, bf16[2048,1536]{1,0:T(8,128)(2,1)S(1)} %get-tuple-element.34.gate_up_ref, bf16[768,2048]{1,0:T(8,128)(2,1)S(1)} %get-tuple-element.35.down_ref, bf16[32,4224]{1,0:T(8,128)(2,1)S(1)} %get-tuple-element.45.refs_0_, ...), custom_call_target="tpu_custom_call" | custom-call | flops 5000000000 | bytes 1 | tf_op jit(solution)/shard_map/expert/pallas_call | solution.py:172
  56.8 4.3 %expert.5 = (bf16[64,2176]{1,0:T(8,128)(2,1)S(1)}, bf16[64,2176]{1,0:T(8,128)(2,1)S(1)}) custom-call(s32[1]{0:T(128)} %bitcast.1.expert_ref, bf16[2048,1536]{1,0:T(8,128)(2,1)S(1)} %get-tuple-element.34.gate_up_ref, bf16[768,2048]{1,0:T(8,128)(2,1)S(1)} %get-tuple-element.35.down_ref, bf16[32,4224]{1,0:T(8,128)(2,1)S(1)} %get-tuple-element.51.refs_0_, ...), custom_call_target="tpu_custom_call" | custom-call | flops 5000000000 | bytes 1 | tf_op jit(solution)/shard_map/expert/pallas_call | solution.py:172
  61.2 1.4 %collective-permute-start.26 = (bf16[64,2176]{1,0:T(8,128)(2,1)S(1)}, bf16[64,2176]{1,0:T(8,128)(2,1)S(1)}, u32[]{:S(2)}, u32[]{:S(2)}) collective-permute-start(bf16[64,2176]{1,0:T(8,128)(2,1)S(1)} %get-tuple-element.53), channel_id=1, source_target_pairs={{0,4},{1,3},{2,6},{3,1},{4,0},{5,7},{6,2},{7,5},{8,12},{9,11},{10,... | collective-permute-start | bytes 835592 | tf_op jit(solution)/shard_map/ppermute | solution.py:256
  63.3 1.6 %collective-permute-start.17 = (bf16[32,2176]{1,0:T(8,128)(2,1)S(1)}, bf16[32,2176]{1,0:T(8,128)(2,1)S(1)}, u32[]{:S(2)}, u32[]{:S(2)}) collective-permute-start(bf16[32,2176]{1,0:T(8,128)(2,1)S(1)} %add_convert_fusion.5), channel_id=1, source_target_pairs={{0,2},{1,5},{2,0},{3,7},{4,6},{5,1},{6,4},{7,3},{8,10},{9,13},{10,... | collective-permute-start | bytes 417800 | tf_op jit(solution)/shard_map/ppermute | solution.py:255
  64.8 2.9 %collective-permute-done.14 = bf16[32,2176]{1,0:T(8,128)(2,1)S(1)} collective-permute-done((bf16[32,2176]{1,0:T(8,128)(2,1)S(1)}, bf16[32,2176]{1,0:T(8,128)(2,1)S(1)}, u32[]{:S(2)}, u32[]{:S(2)}) %collective-permute-start.14) | collective-permute-done | bytes 139296 | tf_op jit(solution)/shard_map/ppermute | solution.py:255
  71.0 2.9 %collective-permute-done.21 = bf16[32,2176]{1,0:T(8,128)(2,1)S(1)} collective-permute-done((bf16[32,2176]{1,0:T(8,128)(2,1)S(1)}, bf16[32,2176]{1,0:T(8,128)(2,1)S(1)}, u32[]{:S(2)}, u32[]{:S(2)}) %collective-permute-start.21) | collective-permute-done | bytes 139296 | tf_op jit(solution)/shard_map/ppermute | solution.py:255
  74.0 1.5 %collective-permute-start.22 = (bf16[32,2176]{1,0:T(8,128)(2,1)S(1)}, bf16[32,2176]{1,0:T(8,128)(2,1)S(1)}, u32[]{:S(2)}, u32[]{:S(2)}) collective-permute-start(bf16[32,2176]{1,0:T(8,128)(2,1)S(1)} %add_convert_fusion.3), channel_id=1, source_target_pairs={{0,16},{2,18},{4,20},{6,22},{8,24},{10,26},{12,28},{14,30},{16,0},... | collective-permute-start | bytes 417800 | tf_op jit(solution)/shard_map/ppermute | solution.py:264
  76.7 6.4 %collective-permute-done.22 = bf16[32,2176]{1,0:T(8,128)(2,1)S(1)} collective-permute-done((bf16[32,2176]{1,0:T(8,128)(2,1)S(1)}, bf16[32,2176]{1,0:T(8,128)(2,1)S(1)}, u32[]{:S(2)}, u32[]{:S(2)}) %collective-permute-start.22) | collective-permute-done | bytes 139296 | tf_op jit(solution)/shard_map/ppermute | solution.py:264
  (67 shorter events, 17.4 us)
Async XLA Ops:
  2.5 11.7 %collective-permute-start = (bf16[32,4224]{1,0:T(8,128)(2,1)}, bf16[32,4224]{1,0:T(8,128)(2,1)S(1)}, u32[]{:S(2)}, u32[]{:S(2)}) collective-permute-start(bf16[32,4224]{1,0:T(8,128)(2,1)} %pack.1.refs_4_), channel_id=1, source_target_pairs={{0,8},{2,10},{4,12},{6,14},{8,16},{10,18},{12,20},{14,22},{16,24},... | collective-permute-start | bytes 811016 | tf_op jit(solution)/shard_map/ppermute | solution.py:264
  5.5 8.7 %collective-permute-start.1 = (bf16[32,4224]{1,0:T(8,128)(2,1)}, bf16[32,4224]{1,0:T(8,128)(2,1)S(1)}, u32[]{:S(2)}, u32[]{:S(2)}) collective-permute-start(bf16[32,4224]{1,0:T(8,128)(2,1)} %pack.1.refs_4_), channel_id=1, source_target_pairs={{0,2},{1,5},{2,0},{3,7},{4,6},{5,1},{6,4},{7,3},{8,10},{9,13},{10,... | collective-permute-start | bytes 811016 | tf_op jit(solution)/shard_map/ppermute | solution.py:255
  7.0 24.4 %collective-permute-start.10 = (bf16[2048,384]{1,0:T(8,128)(2,1)}, bf16[2048,384]{1,0:T(8,128)(2,1)S(1)}, u32[]{:S(2)}, u32[]{:S(2)}) collective-permute-start(bf16[2048,384]{1,0:T(8,128)(2,1)} %bitcast.10), channel_id=1, source_target_pairs={{0,1},{1,0},{2,3},{3,2},{4,5},{5,4},{6,7},{7,6},{8,9},{9,8},{10,11... | collective-permute-start | bytes 4718600 | tf_op jit(solution)/shard_map/ppermute | solution.py:257
  7.0 25.9 %collective-permute-start.9 = (bf16[2048,384]{1,0:T(8,128)(2,1)}, bf16[2048,384]{1,0:T(8,128)(2,1)}, u32[]{:S(2)}, u32[]{:S(2)}) collective-permute-start(bf16[2048,384]{1,0:T(8,128)(2,1)} %bitcast.12), channel_id=1, source_target_pairs={{0,1},{1,0},{2,3},{3,2},{4,5},{5,4},{6,7},{7,6},{8,9},{9,8},{10,11... | collective-permute-start | bytes 4718600 | tf_op jit(solution)/shard_map/ppermute | solution.py:257
  7.5 10.3 %collective-permute-start.4 = (bf16[32,4224]{1,0:T(8,128)(2,1)}, bf16[32,4224]{1,0:T(8,128)(2,1)S(1)}, u32[]{:S(2)}, u32[]{:S(2)}) collective-permute-start(bf16[32,4224]{1,0:T(8,128)(2,1)} %pack.1.refs_4_), channel_id=1, source_target_pairs={{0,4},{1,3},{2,6},{3,1},{4,0},{5,7},{6,2},{7,5},{8,12},{9,11},{10,... | collective-permute-start | bytes 811016 | tf_op jit(solution)/shard_map/ppermute | solution.py:256
  14.3 9.5 %collective-permute-start.2 = (bf16[32,4224]{1,0:T(8,128)(2,1)S(1)}, bf16[32,4224]{1,0:T(8,128)(2,1)S(1)}, u32[]{:S(2)}, u32[]{:S(2)}) collective-permute-start(bf16[32,4224]{1,0:T(8,128)(2,1)S(1)} %get-tuple-element.29.refs_0_), channel_id=1, source_target_pairs={{0,8},{2,10},{4,12},{6,14},{8,16},{10,18},{12,20},{14,22},{16,24},... | collective-permute-start | bytes 811016 | tf_op jit(solution)/shard_map/ppermute | solution.py:264
  15.6 9.4 %collective-permute-start.3 = (bf16[32,4224]{1,0:T(8,128)(2,1)S(1)}, bf16[32,4224]{1,0:T(8,128)(2,1)S(1)}, u32[]{:S(2)}, u32[]{:S(2)}) collective-permute-start(bf16[32,4224]{1,0:T(8,128)(2,1)S(1)} %get-tuple-element.29.refs_0_), channel_id=1, source_target_pairs={{0,2},{1,5},{2,0},{3,7},{4,6},{5,1},{6,4},{7,3},{8,10},{9,13},{10,... | collective-permute-start | bytes 811016 | tf_op jit(solution)/shard_map/ppermute | solution.py:255
  25.0 11.0 %collective-permute-start.11 = (bf16[384,2048]{1,0:T(8,128)(2,1)}, bf16[384,2048]{1,0:T(8,128)(2,1)S(1)}, u32[]{:S(2)}, u32[]{:S(2)}) collective-permute-start(bf16[384,2048]{1,0:T(8,128)(2,1)} %bitcast.14), channel_id=1, source_target_pairs={{0,1},{1,0},{2,3},{3,2},{4,5},{5,4},{6,7},{7,6},{8,9},{9,8},{10,11... | collective-permute-start | bytes 4718600 | tf_op jit(solution)/shard_map/ppermute | solution.py:257
  25.0 11.4 %collective-permute-start.5 = (bf16[32,4224]{1,0:T(8,128)(2,1)S(1)}, bf16[32,4224]{1,0:T(8,128)(2,1)S(1)}, u32[]{:S(2)}, u32[]{:S(2)}) collective-permute-start(bf16[32,4224]{1,0:T(8,128)(2,1)S(1)} %get-tuple-element.30.refs_1_), channel_id=1, source_target_pairs={{0,8},{2,10},{4,12},{6,14},{8,16},{10,18},{12,20},{14,22},{16,24},... | collective-permute-start | bytes 811016 | tf_op jit(solution)/shard_map/ppermute | solution.py:264
  30.2 9.4 %collective-permute-start.6 = (bf16[32,4224]{1,0:T(8,128)(2,1)S(1)}, bf16[32,4224]{1,0:T(8,128)(2,1)S(1)}, u32[]{:S(2)}, u32[]{:S(2)}) collective-permute-start(bf16[32,4224]{1,0:T(8,128)(2,1)S(1)} %get-tuple-element.30.refs_1_), channel_id=1, source_target_pairs={{0,2},{1,5},{2,0},{3,7},{4,6},{5,1},{6,4},{7,3},{8,10},{9,13},{10,... | collective-permute-start | bytes 811016 | tf_op jit(solution)/shard_map/ppermute | solution.py:255
  31.4 17.1 %collective-permute-start.18 = (bf16[32,4224]{1,0:T(8,128)(2,1)S(1)}, bf16[32,4224]{1,0:T(8,128)(2,1)S(1)}, u32[]{:S(2)}, u32[]{:S(2)}) collective-permute-start(bf16[32,4224]{1,0:T(8,128)(2,1)S(1)} %get-tuple-element.30.refs_1_), channel_id=1, source_target_pairs={{0,4},{1,3},{2,6},{3,1},{4,0},{5,7},{6,2},{7,5},{8,12},{9,11},{10,... | collective-permute-start | bytes 811016 | tf_op jit(solution)/shard_map/ppermute | solution.py:256
  33.0 10.5 %collective-permute-start.12 = (bf16[32,4224]{1,0:T(8,128)(2,1)S(1)}, bf16[32,4224]{1,0:T(8,128)(2,1)S(1)}, u32[]{:S(2)}, u32[]{:S(2)}) collective-permute-start(bf16[32,4224]{1,0:T(8,128)(2,1)S(1)} %get-tuple-element.36.refs_1_), channel_id=1, source_target_pairs={{0,4},{1,3},{2,6},{3,1},{4,0},{5,7},{6,2},{7,5},{8,12},{9,11},{10,... | collective-permute-start | bytes 811016 | tf_op jit(solution)/shard_map/ppermute | solution.py:256
  39.6 16.5 %collective-permute-start.23 = (bf16[32,4224]{1,0:T(8,128)(2,1)S(1)}, bf16[32,4224]{1,0:T(8,128)(2,1)S(1)}, u32[]{:S(2)}, u32[]{:S(2)}) collective-permute-start(bf16[32,4224]{1,0:T(8,128)(2,1)S(1)} %get-tuple-element.49.refs_1_), channel_id=1, source_target_pairs={{0,2},{1,5},{2,0},{3,7},{4,6},{5,1},{6,4},{7,3},{8,10},{9,13},{10,... | collective-permute-start | bytes 811016 | tf_op jit(solution)/shard_map/ppermute | solution.py:255
  40.8 15.2 %collective-permute-start.24 = (bf16[32,4224]{1,0:T(8,128)(2,1)S(1)}, bf16[32,4224]{1,0:T(8,128)(2,1)S(1)}, u32[]{:S(2)}, u32[]{:S(2)}) collective-permute-start(bf16[32,4224]{1,0:T(8,128)(2,1)S(1)} %get-tuple-element.49.refs_1_), channel_id=1, source_target_pairs={{0,4},{1,3},{2,6},{3,1},{4,0},{5,7},{6,2},{7,5},{8,12},{9,11},{10,... | collective-permute-start | bytes 811016 | tf_op jit(solution)/shard_map/ppermute | solution.py:256
  42.4 8.0 %collective-permute-start.19 = (bf16[32,4224]{1,0:T(8,128)(2,1)S(1)}, bf16[32,4224]{1,0:T(8,128)(2,1)S(1)}, u32[]{:S(2)}, u32[]{:S(2)}) collective-permute-start(bf16[32,4224]{1,0:T(8,128)(2,1)S(1)} %get-tuple-element.46.refs_1_), channel_id=1, source_target_pairs={{0,4},{1,3},{2,6},{3,1},{4,0},{5,7},{6,2},{7,5},{8,12},{9,11},{10,... | collective-permute-start | bytes 811016 | tf_op jit(solution)/shard_map/ppermute | solution.py:256
  43.4 13.4 %collective-permute-start.25 = (bf16[32,4224]{1,0:T(8,128)(2,1)S(1)}, bf16[32,4224]{1,0:T(8,128)(2,1)S(1)}, u32[]{:S(2)}, u32[]{:S(2)}) collective-permute-start(bf16[32,4224]{1,0:T(8,128)(2,1)S(1)} %get-tuple-element.39.refs_7_), channel_id=1, source_target_pairs={{0,24},{2,26},{4,28},{6,30},{8,0},{10,2},{12,4},{14,6},{16,8},{18,... | collective-permute-start | bytes 811016 | tf_op jit(solution)/shard_map/ppermute | solution.py:264
  48.5 14.1 %collective-permute-start.13 = (bf16[64,2176]{1,0:T(8,128)(2,1)S(1)}, bf16[64,2176]{1,0:T(8,128)(2,1)S(1)}, u32[]{:S(2)}, u32[]{:S(2)}) collective-permute-start(bf16[64,2176]{1,0:T(8,128)(2,1)S(1)} %get-tuple-element.42), channel_id=1, source_target_pairs={{0,4},{1,3},{2,6},{3,1},{4,0},{5,7},{6,2},{7,5},{8,12},{9,11},{10,... | collective-permute-start | bytes 835592 | tf_op jit(solution)/shard_map/ppermute | solution.py:256
  50.4 12.9 %collective-permute-start.16 = (bf16[64,2176]{1,0:T(8,128)(2,1)S(1)}, bf16[64,2176]{1,0:T(8,128)(2,1)S(1)}, u32[]{:S(2)}, u32[]{:S(2)}) collective-permute-start(bf16[64,2176]{1,0:T(8,128)(2,1)S(1)} %get-tuple-element.44), channel_id=1, source_target_pairs={{0,4},{1,3},{2,6},{3,1},{4,0},{5,7},{6,2},{7,5},{8,12},{9,11},{10,... | collective-permute-start | bytes 835592 | tf_op jit(solution)/shard_map/ppermute | solution.py:256
  56.1 12.7 %collective-permute-start.20 = (bf16[64,2176]{1,0:T(8,128)(2,1)S(1)}, bf16[64,2176]{1,0:T(8,128)(2,1)S(1)}, u32[]{:S(2)}, u32[]{:S(2)}) collective-permute-start(bf16[64,2176]{1,0:T(8,128)(2,1)S(1)} %get-tuple-element.50), channel_id=1, source_target_pairs={{0,4},{1,3},{2,6},{3,1},{4,0},{5,7},{6,2},{7,5},{8,12},{9,11},{10,... | collective-permute-start | bytes 835592 | tf_op jit(solution)/shard_map/ppermute | solution.py:256
  61.2 9.3 %collective-permute-start.26 = (bf16[64,2176]{1,0:T(8,128)(2,1)S(1)}, bf16[64,2176]{1,0:T(8,128)(2,1)S(1)}, u32[]{:S(2)}, u32[]{:S(2)}) collective-permute-start(bf16[64,2176]{1,0:T(8,128)(2,1)S(1)} %get-tuple-element.53), channel_id=1, source_target_pairs={{0,4},{1,3},{2,6},{3,1},{4,0},{5,7},{6,2},{7,5},{8,12},{9,11},{10,... | collective-permute-start | bytes 835592 | tf_op jit(solution)/shard_map/ppermute | solution.py:256
  63.3 13.4 %collective-permute-start.17 = (bf16[32,2176]{1,0:T(8,128)(2,1)S(1)}, bf16[32,2176]{1,0:T(8,128)(2,1)S(1)}, u32[]{:S(2)}, u32[]{:S(2)}) collective-permute-start(bf16[32,2176]{1,0:T(8,128)(2,1)S(1)} %add_convert_fusion.5), channel_id=1, source_target_pairs={{0,2},{1,5},{2,0},{3,7},{4,6},{5,1},{6,4},{7,3},{8,10},{9,13},{10,... | collective-permute-start | bytes 417800 | tf_op jit(solution)/shard_map/ppermute | solution.py:255
  67.8 8.9 %collective-permute-start.15 = (bf16[32,2176]{1,0:T(8,128)(2,1)S(1)}, bf16[32,2176]{1,0:T(8,128)(2,1)S(1)}, u32[]{:S(2)}, u32[]{:S(2)}) collective-permute-start(bf16[32,2176]{1,0:T(8,128)(2,1)S(1)} %add_convert_fusion.6), channel_id=1, source_target_pairs={{0,24},{2,26},{4,28},{6,30},{8,0},{10,2},{12,4},{14,6},{16,8},{18,... | collective-permute-start | bytes 417800 | tf_op jit(solution)/shard_map/ppermute | solution.py:264
  74.0 9.1 %collective-permute-start.22 = (bf16[32,2176]{1,0:T(8,128)(2,1)S(1)}, bf16[32,2176]{1,0:T(8,128)(2,1)S(1)}, u32[]{:S(2)}, u32[]{:S(2)}) collective-permute-start(bf16[32,2176]{1,0:T(8,128)(2,1)S(1)} %add_convert_fusion.3), channel_id=1, source_target_pairs={{0,16},{2,18},{4,20},{6,22},{8,24},{10,26},{12,28},{14,30},{16,0},... | collective-permute-start | bytes 417800 | tf_op jit(solution)/shard_map/ppermute | solution.py:264
  75.7 7.5 %collective-permute-start.28 = (bf16[32,2176]{1,0:T(8,128)(2,1)S(1)}, bf16[32,2176]{1,0:T(8,128)(2,1)S(1)}, u32[]{:S(2)}, u32[]{:S(2)}) collective-permute-start(bf16[32,2176]{1,0:T(8,128)(2,1)S(1)} %add_convert_fusion.1), channel_id=1, source_target_pairs={{0,8},{2,10},{4,12},{6,14},{8,16},{10,18},{12,20},{14,22},{16,24},... | collective-permute-start | bytes 417800 | tf_op jit(solution)/shard_map/ppermute | solution.py:264
  (11 other events, 85.3 us)

commit v3 on v2

--- a/solution.py
+++ b/solution.py
@@ -8,8 +8,10 @@
 from jax.sharding import PartitionSpec as P
 
 LANES = 128
+VM = 16
+PREP = 4 * 10**9
 LAG = 10000000000
-EFLOPS = 5000000000
+EFLOPS = 5 * 10**9
 CONTRACT_LAST = (((1,), (1,)), ((), ()))
 
 
@@ -134,22 +136,20 @@
     )(half, tokens, cotangent, expert_ids.T, gate_weights.T)
 
 
-def expert_kernel(experts, expert_ref, gate_up_ref, down_ref, *refs):
+def expert_kernel(experts, expert_ref, gate_up_ref, gate_up_t_ref, down_t_ref, *refs):
     shard_refs, out_refs = refs[: 2 * len(refs) // 3], refs[2 * len(refs) // 3 :]
     rows = 2 * shard_refs[0].shape[0]
-    width, units = gate_up_ref.shape[0], down_ref.shape[0]
+    width, units = down_t_ref.shape
     packed = jnp.concatenate([ref[...] for ref in shard_refs], axis=0)
     pre = jnp.dot(packed[:, :width], gate_up_ref[...], preferred_element_type=jnp.float32)
-    grad_hidden = lax.dot_general(
-        packed[:, width : 2 * width], down_ref[...], CONTRACT_LAST, preferred_element_type=jnp.float32
-    )
+    grad_hidden = jnp.dot(packed[:, width : 2 * width], down_t_ref[...], preferred_element_type=jnp.float32)
     gate_pre, up_pre = pre[:, :units], pre[:, units:]
     sigmoid_gate = 1.0 / (1.0 + jnp.exp(-gate_pre))
     grad_up = grad_hidden * gate_pre * sigmoid_gate
     scores = jnp.sum(grad_up * up_pre, axis=1, keepdims=True)
     grad_gate = grad_hidden * up_pre * sigmoid_gate * (1.0 + gate_pre * (1.0 - sigmoid_gate))
     grads = jnp.concatenate([grad_gate.astype(jnp.bfloat16), grad_up.astype(jnp.bfloat16)], axis=1)
-    part = lax.dot_general(grads, gate_up_ref[...], CONTRACT_LAST, preferred_element_type=jnp.float32)
+    part = jnp.dot(grads, gate_up_t_ref[...], preferred_element_type=jnp.float32)
     expert = expert_ref[0]
     routing = packed[:, 2 * width :].astype(jnp.float32)
     lane = lax.broadcasted_iota(jnp.int32, routing.shape, 1)
@@ -164,20 +164,62 @@
         ref[:, width:] = score_part[i * rows : (i + 1) * rows]
 
 
-def expert_call(expert, gate_up, down, experts, *shards):
+def layout_kernel(own_refs, other_refs, joined_ref, turned_ref):
+    units = own_refs[0].shape[1]
+    for i, ref in enumerate((own_refs[0], other_refs[0], own_refs[1], other_refs[1])):
+        joined_ref[:, i * units : (i + 1) * units] = ref[...]
+        turned_ref[i * units : (i + 1) * units, :] = ref[...].T
+
+
+def turn_kernel(own_ref, other_ref, turned_ref):
+    units = own_ref.shape[0]
+    turned_ref[:, :units] = own_ref[...].T
+    turned_ref[:, units:] = other_ref[...].T
+
+
+def lay_out(gate_one, gate_other, up_one, up_other, down_one, down_other):
+    width, units = gate_one.shape
+    vmem = pl.BlockSpec(memory_space=pltpu.VMEM)
+    params = pltpu.CompilerParams(vmem_limit_bytes=VM * 2**20)
+    cost = pl.CostEstimate(flops=PREP, bytes_accessed=1, transcendentals=0)
+    joined, turned = pl.pallas_call(
+        lambda a, b, c, d, e, f: layout_kernel((a, c), (b, d), e, f),
+        in_specs=[vmem] * 4,
+        out_specs=[vmem] * 2,
+        out_shape=[
+            jax.ShapeDtypeStruct((width, 4 * units), jnp.bfloat16),
+            jax.ShapeDtypeStruct((4 * units, width), jnp.bfloat16),
+        ],
+        compiler_params=params,
+        cost_estimate=cost,
+        name="layout",
+    )(gate_one, gate_other, up_one, up_other)
+    down = pl.pallas_call(
+        turn_kernel,
+        in_specs=[vmem] * 2,
+        out_specs=vmem,
+        out_shape=jax.ShapeDtypeStruct((width, 2 * units), jnp.bfloat16),
+        compiler_params=params,
+        cost_estimate=cost,
+        name="turn",
+    )(down_one, down_other)
+    return joined, turned, down
+
+
+def expert_call(expert, weights, experts, *shards):
     rows = shards[0].shape[0]
-    width, units = gate_up.shape[0], down.shape[0]
+    width = weights[0].shape[0]
     outs = len(shards) // 2
     vmem = pl.BlockSpec(memory_space=pltpu.VMEM)
     return pl.pallas_call(
         functools.partial(expert_kernel, experts),
-        in_specs=[pl.BlockSpec(memory_space=pltpu.SMEM)] + [vmem] * (2 + len(shards)),
+        in_specs=[pl.BlockSpec(memory_space=pltpu.SMEM)] + [vmem] * (3 + len(shards)),
         out_specs=[vmem] * outs,
         out_shape=[jax.ShapeDtypeStruct((2 * rows, width + padded(experts)), jnp.bfloat16)] * outs,
-        compiler_params=pltpu.CompilerParams(vmem_limit_bytes=40 * 2**20),
+        compiler_params=pltpu.CompilerParams(vmem_limit_bytes=VM * 2**20),
         cost_estimate=pl.CostEstimate(flops=EFLOPS, bytes_accessed=1, transcendentals=0),
         name="expert",
-    )(expert, gate_up, down, *shards)
+    )(expert, *weights, *shards)
 
 
 def tie(*arrays, cost=1):
@@ -258,8 +300,7 @@
 
     own = pack(half, tokens, cotangent, expert_ids, gate_weights, experts)
     gate_one, up_one, down_one = w_gate[0], w_up[0], w_down[0]
-    gate_up = jnp.concatenate([gate_one, swapped(gate_one), up_one, swapped(up_one)], axis=1)
-    down = jnp.concatenate([down_one, swapped(down_one)], axis=0)
+    weights = lay_out(gate_one, swapped(gate_one), up_one, swapped(up_one), down_one, swapped(down_one))
 
     shifted = lambda a, by: lax.ppermute(a, "expert", [(e, (e + 4 * by) % experts) for e in range(experts)])
     shards, firsts, seconds, boths = [own], [], [], []
@@ -276,7 +317,7 @@
         elif level > 0:
             held.append(seconds[level - 1])
         if level == levels - 2:
-            held += [gate_up, down]
+            held += weights
         held = tie(*held)
         following, firsts[level] = held[:2]
         if level > 0:
@@ -284,16 +325,16 @@
         if level > 1:
             boths[level - 2] = held[3]
         if level == levels - 2:
-            gate_up, down = held[-2:]
+            weights = held[-3:]
         shards.append(following)
         boths.append(to_second(firsts[level]))
 
     total, results, previous = [], {}, None
-    for batch in ((1,0),(2,),(3,)):
+    for batch in [(1, 0)] + [(level,) for level in range(2, levels)]:
         planes = [[shards[i], firsts[i], seconds[i], boths[i]] for i in batch]
         if previous is not None:
             results[previous][1], planes[0][0] = tie(results[previous][1], planes[0][0])
-        outs = expert_call(expert, gate_up, down, experts, *sum(planes, []))
+        outs = expert_call(expert, weights, experts, *sum(planes, []))
         for i, level in enumerate(batch):
             results[level] = list(outs[2 * i : 2 * i + 2])
         previous = batch[0]

time: 85.8 us -> 82.8 us (0.965)
  waiting for transfers between devices: 31.2 us -> 28 us
  other arithmetic: 3.32 us -> 0.41 us
  Pallas kernels: 16.5 us -> 18.6 us
  starting transfers between devices: 33.7 us -> 34.8 us
    pallas_call x0 -> x2, Pallas kernels: none -> 5.06 us  [the longest x1 4.19 us: lay_out(): pl.pallas_call(lambda a, b, c, d, e, f: layout_kernel((a, c), (b, d), e,...]
    ppermute x11, waiting for transfers between devices: 4.97 us -> 0.49 us  [dense_plan(): to_second = lambda a: lax.ppermute(a, axes, second_pairs)]
    pallas_call x3, Pallas kernels: 13.7 us -> 10.8 us  [expert_call(): pl.pallas_call(functools.partial(expert_kernel, experts), in_specs=[pl.Bl...]
    concatenate x2 -> x0, other arithmetic: 2.9 us -> none  [the longest x1 2.53 us: dense_plan(): jnp.concatenate([gate_one, swapped(gate_one), up_one, swapped(up_one)], a...]
    ppermute x8, starting transfers between devices: 9.4 us -> 11.9 us  [dense_plan(): to_first = lambda a: lax.ppermute(a, axes, first_pairs)]
    ppermute x11, starting transfers between devices: 14 us -> 12 us  [dense_plan(): to_second = lambda a: lax.ppermute(a, axes, second_pairs)]
    ppermute x7, waiting for transfers between devices: 15.7 us -> 17.7 us  [dense_plan(): lax.ppermute(a, 'expert', [(e, (e + 4 * by) % experts) for e in range(exp...]
    ppermute x7, starting transfers between devices: 9.77 us -> 10.8 us  [dense_plan(): lax.ppermute(a, 'expert', [(e, (e + 4 * by) % experts) for e in range(exp...]
  transfers between devices with their start and end apart: 30 -> 30, of which waited for: 11 -> 11; matrix products, arithmetic and copies ran while one was open for 4% -> 0% of each run, Pallas kernels for 16% -> 19%
where the time goes in v3:
time: 82.8 us; the launch traced here: 82.7 us
  starting transfers between devices  34.8 us (42%)
  waiting for transfers between devices  28 us (34%)
  Pallas kernels  18.6 us (22%)
    ppermute x7, waiting for transfers between devices, dense_plan(): lax.ppermute(a, 'expert', [(e, (e + 4 * by) % experts) for e in range(exp...  17.7 us
    ppermute x11, starting transfers between devices, dense_plan(): to_second = lambda a: lax.ppermute(a, axes, second_pairs)  12 us
    ppermute x8, starting transfers between devices, dense_plan(): to_first = lambda a: lax.ppermute(a, axes, first_pairs)  11.9 us
    ppermute x7, starting transfers between devices, dense_plan(): lax.ppermute(a, 'expert', [(e, (e + 4 * by) % experts) for e in range(exp...  10.8 us
    pallas_call x3, Pallas kernels, expert_call(): pl.pallas_call(functools.partial(expert_kernel, experts), in_specs=[pl.Bl...  10.8 us
    ppermute x8, waiting for transfers between devices, dense_plan(): to_first = lambda a: lax.ppermute(a, axes, first_pairs)  8.51 us
    pallas_call x1, Pallas kernels, lay_out(): pl.pallas_call(lambda a, b, c, d, e, f: layout_kernel((a, c), (b, d), e,...  4.19 us
    pallas_call x1, Pallas kernels, pack(): pl.pallas_call(functools.partial(pack_kernel, experts), grid_spec=pltpu.P...  1.89 us
  transfers between devices with their start and end apart: 30, of which 11 were waited for; matrix products, arithmetic and copies ran while one was open for 0% of the time, Pallas kernels for 19%

profile of v3, /device:TPU:0, one launch (start us, length us, event | category | flops | bytes accessed | tf_op | source)
XLA Modules:
  0.0 82.7 jit_solution(60014460533839959)
XLA Ops:
  0.6 1.9 %pack.1.refs_4_ = bf16[32,4224]{1,0:T(8,128)(2,1)} custom-call(s32[1]{0:T(128)} %bitcast.half_ref, bf16[64,2048]{1,0:T(8,128)(2,1)} %tok_ref.1, bf16[64,2048]{1,0:T(8,128)(2,1)} %cot_ref.1, s32[8,64]{1,0:T(8,128)} %bitcast.8, f32[8,64]{1,0:T(8,128)} %bitcast.16), custom_call_target="tpu_custom_call" | custom-call | tf_op jit(solution)/shard_map/pack/pallas_call | solution.py:121
  2.5 3.0 %collective-permute-start = (bf16[32,4224]{1,0:T(8,128)(2,1)}, bf16[32,4224]{1,0:T(8,128)(2,1)S(1)}, u32[]{:S(2)}, u32[]{:S(2)}) collective-permute-start(bf16[32,4224]{1,0:T(8,128)(2,1)} %pack.1.refs_4_), channel_id=1, source_target_pairs={{0,8},{2,10},{4,12},{6,14},{8,16},{10,18},{12,20},{14,22},{16,24},... | collective-permute-start | bytes 811016 | tf_op jit(solution)/shard_map/ppermute | solution.py:305
  5.6 1.5 %collective-permute-start.1 = (bf16[32,4224]{1,0:T(8,128)(2,1)}, bf16[32,4224]{1,0:T(8,128)(2,1)S(1)}, u32[]{:S(2)}, u32[]{:S(2)}) collective-permute-start(bf16[32,4224]{1,0:T(8,128)(2,1)} %pack.1.refs_4_), channel_id=1, source_target_pairs={{0,2},{1,5},{2,0},{3,7},{4,6},{5,1},{6,4},{7,3},{8,10},{9,13},{10,... | collective-permute-start | bytes 811016 | tf_op jit(solution)/shard_map/ppermute | solution.py:297
  7.0 1.5 %collective-permute-start.4 = (bf16[32,4224]{1,0:T(8,128)(2,1)}, bf16[32,4224]{1,0:T(8,128)(2,1)S(1)}, u32[]{:S(2)}, u32[]{:S(2)}) collective-permute-start(bf16[32,4224]{1,0:T(8,128)(2,1)} %pack.1.refs_4_), channel_id=1, source_target_pairs={{0,4},{1,3},{2,6},{3,1},{4,0},{5,7},{6,2},{7,5},{8,12},{9,11},{10,... | collective-permute-start | bytes 811016 | tf_op jit(solution)/shard_map/ppermute | solution.py:298
  8.6 5.7 %collective-permute-done.refs_0_ = bf16[32,4224]{1,0:T(8,128)(2,1)S(1)} collective-permute-done((bf16[32,4224]{1,0:T(8,128)(2,1)}, bf16[32,4224]{1,0:T(8,128)(2,1)S(1)}, u32[]{:S(2)}, u32[]{:S(2)}) %collective-permute-start) | collective-permute-done | bytes 270368 | tf_op jit(solution)/shard_map/ppermute | solution.py:305
  15.7 2.4 %collective-permute-start.3 = (bf16[32,4224]{1,0:T(8,128)(2,1)S(1)}, bf16[32,4224]{1,0:T(8,128)(2,1)S(1)}, u32[]{:S(2)}, u32[]{:S(2)}) collective-permute-start(bf16[32,4224]{1,0:T(8,128)(2,1)S(1)} %get-tuple-element.32.refs_0_), channel_id=1, source_target_pairs={{0,2},{1,5},{2,0},{3,7},{4,6},{5,1},{6,4},{7,3},{8,10},{9,13},{10,... | collective-permute-start | bytes 811016 | tf_op jit(solution)/shard_map/ppermute | solution.py:297
  18.1 1.5 %collective-permute-start.7 = (bf16[32,4224]{1,0:T(8,128)(2,1)S(1)}, bf16[32,4224]{1,0:T(8,128)(2,1)S(1)}, u32[]{:S(2)}, u32[]{:S(2)}) collective-permute-start(bf16[32,4224]{1,0:T(8,128)(2,1)S(1)} %get-tuple-element.32.refs_0_), channel_id=1, source_target_pairs={{0,4},{1,3},{2,6},{3,1},{4,0},{5,7},{6,2},{7,5},{8,12},{9,11},{10,... | collective-permute-start | bytes 811016 | tf_op jit(solution)/shard_map/ppermute | solution.py:298
  20.1 3.6 %collective-permute-done.2.refs_0_ = bf16[32,4224]{1,0:T(8,128)(2,1)S(1)} collective-permute-done((bf16[32,4224]{1,0:T(8,128)(2,1)S(1)}, bf16[32,4224]{1,0:T(8,128)(2,1)S(1)}, u32[]{:S(2)}, u32[]{:S(2)}) %collective-permute-start.2) | collective-permute-done | bytes 270368 | tf_op jit(solution)/shard_map/ppermute | solution.py:305
  23.7 1.8 %collective-permute-done.3.refs_1_ = bf16[32,4224]{1,0:T(8,128)(2,1)S(1)} collective-permute-done((bf16[32,4224]{1,0:T(8,128)(2,1)S(1)}, bf16[32,4224]{1,0:T(8,128)(2,1)S(1)}, u32[]{:S(2)}, u32[]{:S(2)}) %collective-permute-start.3) | collective-permute-done | bytes 270368 | tf_op jit(solution)/shard_map/ppermute | solution.py:297
  30.0 1.8 %collective-permute-start.12 = (bf16[32,4224]{1,0:T(8,128)(2,1)S(1)}, bf16[32,4224]{1,0:T(8,128)(2,1)S(1)}, u32[]{:S(2)}, u32[]{:S(2)}) collective-permute-start(bf16[32,4224]{1,0:T(8,128)(2,1)S(1)} %get-tuple-element.42.refs_1_), channel_id=1, source_target_pairs={{0,4},{1,3},{2,6},{3,1},{4,0},{5,7},{6,2},{7,5},{8,12},{9,11},{10,... | collective-permute-start | bytes 811016 | tf_op jit(solution)/shard_map/ppermute | solution.py:298
  31.8 4.2 %layout.1 = (bf16[2048,1536]{1,0:T(8,128)(2,1)S(1)}, bf16[1536,2048]{1,0:T(8,128)(2,1)S(1)}) custom-call(bf16[2048,384]{1,0:T(8,128)(2,1)S(1)} %bitcast.13, bf16[2048,384]{1,0:T(8,128)(2,1)} %collective-permute-done.9.b, bf16[2048,384]{1,0:T(8,128)(2,1)S(1)} %bitcast.15, bf16[2048,384]{1,0:T(8,128)(2,1)} %collective-permute-done.10.d), custom_call_target="tpu_custom_call" | custom-call | flops 4000000000 | bytes 1 | tf_op jit(solution)/shard_map/layout/pallas_call | solution.py:185
  38.6 1.6 %collective-permute-start.19 = (bf16[32,4224]{1,0:T(8,128)(2,1)S(1)}, bf16[32,4224]{1,0:T(8,128)(2,1)S(1)}, u32[]{:S(2)}, u32[]{:S(2)}) collective-permute-start(bf16[32,4224]{1,0:T(8,128)(2,1)S(1)} %get-tuple-element.52.refs_1_), channel_id=1, source_target_pairs={{0,4},{1,3},{2,6},{3,1},{4,0},{5,7},{6,2},{7,5},{8,12},{9,11},{10,... | collective-permute-start | bytes 811016 | tf_op jit(solution)/shard_map/ppermute | solution.py:298
  40.2 2.4 %collective-permute-start.25 = (bf16[32,4224]{1,0:T(8,128)(2,1)S(1)}, bf16[32,4224]{1,0:T(8,128)(2,1)S(1)}, u32[]{:S(2)}, u32[]{:S(2)}) collective-permute-start(bf16[32,4224]{1,0:T(8,128)(2,1)S(1)} %get-tuple-element.45.refs_7_), channel_id=1, source_target_pairs={{0,24},{2,26},{4,28},{6,30},{8,0},{10,2},{12,4},{14,6},{16,8},{18,... | collective-permute-start | bytes 811016 | tf_op jit(solution)/shard_map/ppermute | solution.py:305
  42.6 5.1 %expert.3 = (bf16[64,2176]{1,0:T(8,128)(2,1)S(1)}, bf16[64,2176]{1,0:T(8,128)(2,1)S(1)}, bf16[64,2176]{1,0:T(8,128)(2,1)S(1)}, bf16[64,2176]{1,0:T(8,128)(2,1)S(1)}) custom-call(s32[1]{0:T(128)} %bitcast.1.expert_ref, bf16[2048,1536]{1,0:T(8,128)(2,1)S(1)} %get-tuple-element.39.gate_up_ref, bf16[1536,2048]{1,0:T(8,128)(2,1)S(1)} %get-tuple-element.40.gate_up_t_ref, ...), custom_call_target="tpu_custom_call" | custom-call | flops 5000000000 | bytes 1 | tf_op jit(solution)/shard_map/expert/pallas_call | solution.py:214
  48.3 1.6 %collective-permute-start.16 = (bf16[64,2176]{1,0:T(8,128)(2,1)S(1)}, bf16[64,2176]{1,0:T(8,128)(2,1)S(1)}, u32[]{:S(2)}, u32[]{:S(2)}) collective-permute-start(bf16[64,2176]{1,0:T(8,128)(2,1)S(1)} %get-tuple-element.50), channel_id=1, source_target_pairs={{0,4},{1,3},{2,6},{3,1},{4,0},{5,7},{6,2},{7,5},{8,12},{9,11},{10,... | collective-permute-start | bytes 835592 | tf_op jit(solution)/shard_map/ppermute | solution.py:298
  49.9 2.8 %expert.4 = (bf16[64,2176]{1,0:T(8,128)(2,1)S(1)}, bf16[64,2176]{1,0:T(8,128)(2,1)S(1)}) custom-call(s32[1]{0:T(128)} %bitcast.1.expert_ref, bf16[2048,1536]{1,0:T(8,128)(2,1)S(1)} %get-tuple-element.39.gate_up_ref, bf16[1536,2048]{1,0:T(8,128)(2,1)S(1)} %get-tuple-element.40.gate_up_t_ref, bf16[2048,768]{1,0:T(8,128)(2,1)S(1)} %get-tuple-element.41.down_t_ref, ...), custom_call_target="tpu_custom_call" | custom-call | flops 5000000000 | bytes 1 | tf_op jit(solution)/shard_map/expert/pallas_call | solution.py:214
  53.2 2.8 %expert.5 = (bf16[64,2176]{1,0:T(8,128)(2,1)S(1)}, bf16[64,2176]{1,0:T(8,128)(2,1)S(1)}) custom-call(s32[1]{0:T(128)} %bitcast.1.expert_ref, bf16[2048,1536]{1,0:T(8,128)(2,1)S(1)} %get-tuple-element.39.gate_up_ref, bf16[1536,2048]{1,0:T(8,128)(2,1)S(1)} %get-tuple-element.40.gate_up_t_ref, bf16[2048,768]{1,0:T(8,128)(2,1)S(1)} %get-tuple-element.41.down_t_ref, ...), custom_call_target="tpu_custom_call" | custom-call | flops 5000000000 | bytes 1 | tf_op jit(solution)/shard_map/expert/pallas_call | solution.py:214
  56.0 1.7 %collective-permute-start.26 = (bf16[64,2176]{1,0:T(8,128)(2,1)S(1)}, bf16[64,2176]{1,0:T(8,128)(2,1)S(1)}, u32[]{:S(2)}, u32[]{:S(2)}) collective-permute-start(bf16[64,2176]{1,0:T(8,128)(2,1)S(1)} %get-tuple-element.59), channel_id=1, source_target_pairs={{0,4},{1,3},{2,6},{3,1},{4,0},{5,7},{6,2},{7,5},{8,12},{9,11},{10,... | collective-permute-start | bytes 835592 | tf_op jit(solution)/shard_map/ppermute | solution.py:298
  57.7 1.7 %collective-permute-start.14 = (bf16[32,2176]{1,0:T(8,128)(2,1)S(1)}, bf16[32,2176]{1,0:T(8,128)(2,1)S(1)}, u32[]{:S(2)}, u32[]{:S(2)}) collective-permute-start(bf16[32,2176]{1,0:T(8,128)(2,1)S(1)} %add_convert_fusion.7), channel_id=1, source_target_pairs={{0,2},{1,5},{2,0},{3,7},{4,6},{5,1},{6,4},{7,3},{8,10},{9,13},{10,... | collective-permute-start | bytes 417800 | tf_op jit(solution)/shard_map/ppermute | solution.py:297
  59.9 2.9 %collective-permute-done.14 = bf16[32,2176]{1,0:T(8,128)(2,1)S(1)} collective-permute-done((bf16[32,2176]{1,0:T(8,128)(2,1)S(1)}, bf16[32,2176]{1,0:T(8,128)(2,1)S(1)}, u32[]{:S(2)}, u32[]{:S(2)}) %collective-permute-start.14) | collective-permute-done | bytes 139296 | tf_op jit(solution)/shard_map/ppermute | solution.py:297
  62.9 2.1 %collective-permute-start.15 = (bf16[32,2176]{1,0:T(8,128)(2,1)S(1)}, bf16[32,2176]{1,0:T(8,128)(2,1)S(1)}, u32[]{:S(2)}, u32[]{:S(2)}) collective-permute-start(bf16[32,2176]{1,0:T(8,128)(2,1)S(1)} %add_convert_fusion.6), channel_id=1, source_target_pairs={{0,24},{2,26},{4,28},{6,30},{8,0},{10,2},{12,4},{14,6},{16,8},{18,... | collective-permute-start | bytes 417800 | tf_op jit(solution)/shard_map/ppermute | solution.py:305
  66.5 2.0 %collective-permute-start.27 = (bf16[32,2176]{1,0:T(8,128)(2,1)S(1)}, bf16[32,2176]{1,0:T(8,128)(2,1)S(1)}, u32[]{:S(2)}, u32[]{:S(2)}) collective-permute-start(bf16[32,2176]{1,0:T(8,128)(2,1)S(1)} %add_convert_fusion.2), channel_id=1, source_target_pairs={{0,2},{1,5},{2,0},{3,7},{4,6},{5,1},{6,4},{7,3},{8,10},{9,13},{10,... | collective-permute-start | bytes 417800 | tf_op jit(solution)/shard_map/ppermute | solution.py:297
  68.4 1.8 %collective-permute-done.21 = bf16[32,2176]{1,0:T(8,128)(2,1)S(1)} collective-permute-done((bf16[32,2176]{1,0:T(8,128)(2,1)S(1)}, bf16[32,2176]{1,0:T(8,128)(2,1)S(1)}, u32[]{:S(2)}, u32[]{:S(2)}) %collective-permute-start.21) | collective-permute-done | bytes 139296 | tf_op jit(solution)/shard_map/ppermute | solution.py:297
  72.0 8.2 %collective-permute-done.22 = bf16[32,2176]{1,0:T(8,128)(2,1)S(1)} collective-permute-done((bf16[32,2176]{1,0:T(8,128)(2,1)S(1)}, bf16[32,2176]{1,0:T(8,128)(2,1)S(1)}, u32[]{:S(2)}, u32[]{:S(2)}) %collective-permute-start.22) | collective-permute-done | bytes 139296 | tf_op jit(solution)/shard_map/ppermute | solution.py:305
  (67 shorter events, 16.3 us)
Async XLA Ops:
  2.5 11.7 %collective-permute-start = (bf16[32,4224]{1,0:T(8,128)(2,1)}, bf16[32,4224]{1,0:T(8,128)(2,1)S(1)}, u32[]{:S(2)}, u32[]{:S(2)}) collective-permute-start(bf16[32,4224]{1,0:T(8,128)(2,1)} %pack.1.refs_4_), channel_id=1, source_target_pairs={{0,8},{2,10},{4,12},{6,14},{8,16},{10,18},{12,20},{14,22},{16,24},... | collective-permute-start | bytes 811016 | tf_op jit(solution)/shard_map/ppermute | solution.py:305
  5.6 8.7 %collective-permute-start.1 = (bf16[32,4224]{1,0:T(8,128)(2,1)}, bf16[32,4224]{1,0:T(8,128)(2,1)S(1)}, u32[]{:S(2)}, u32[]{:S(2)}) collective-permute-start(bf16[32,4224]{1,0:T(8,128)(2,1)} %pack.1.refs_4_), channel_id=1, source_target_pairs={{0,2},{1,5},{2,0},{3,7},{4,6},{5,1},{6,4},{7,3},{8,10},{9,13},{10,... | collective-permute-start | bytes 811016 | tf_op jit(solution)/shard_map/ppermute | solution.py:297
  7.0 21.7 %collective-permute-start.11 = (bf16[384,2048]{1,0:T(8,128)(2,1)}, bf16[384,2048]{1,0:T(8,128)(2,1)S(1)}, u32[]{:S(2)}, u32[]{:S(2)}) collective-permute-start(bf16[384,2048]{1,0:T(8,128)(2,1)} %bitcast.10), channel_id=1, source_target_pairs={{0,1},{1,0},{2,3},{3,2},{4,5},{5,4},{6,7},{7,6},{8,9},{9,8},{10,11... | collective-permute-start | bytes 4718600 | tf_op jit(solution)/shard_map/ppermute | solution.py:299
  7.0 12.6 %collective-permute-start.4 = (bf16[32,4224]{1,0:T(8,128)(2,1)}, bf16[32,4224]{1,0:T(8,128)(2,1)S(1)}, u32[]{:S(2)}, u32[]{:S(2)}) collective-permute-start(bf16[32,4224]{1,0:T(8,128)(2,1)} %pack.1.refs_4_), channel_id=1, source_target_pairs={{0,4},{1,3},{2,6},{3,1},{4,0},{5,7},{6,2},{7,5},{8,12},{9,11},{10,... | collective-permute-start | bytes 811016 | tf_op jit(solution)/shard_map/ppermute | solution.py:298
  14.3 9.5 %collective-permute-start.2 = (bf16[32,4224]{1,0:T(8,128)(2,1)S(1)}, bf16[32,4224]{1,0:T(8,128)(2,1)S(1)}, u32[]{:S(2)}, u32[]{:S(2)}) collective-permute-start(bf16[32,4224]{1,0:T(8,128)(2,1)S(1)} %get-tuple-element.32.refs_0_), channel_id=1, source_target_pairs={{0,8},{2,10},{4,12},{6,14},{8,16},{10,18},{12,20},{14,22},{16,24},... | collective-permute-start | bytes 811016 | tf_op jit(solution)/shard_map/ppermute | solution.py:305
  15.7 9.8 %collective-permute-start.3 = (bf16[32,4224]{1,0:T(8,128)(2,1)S(1)}, bf16[32,4224]{1,0:T(8,128)(2,1)S(1)}, u32[]{:S(2)}, u32[]{:S(2)}) collective-permute-start(bf16[32,4224]{1,0:T(8,128)(2,1)S(1)} %get-tuple-element.32.refs_0_), channel_id=1, source_target_pairs={{0,2},{1,5},{2,0},{3,7},{4,6},{5,1},{6,4},{7,3},{8,10},{9,13},{10,... | collective-permute-start | bytes 811016 | tf_op jit(solution)/shard_map/ppermute | solution.py:297
  18.1 7.4 %collective-permute-start.7 = (bf16[32,4224]{1,0:T(8,128)(2,1)S(1)}, bf16[32,4224]{1,0:T(8,128)(2,1)S(1)}, u32[]{:S(2)}, u32[]{:S(2)}) collective-permute-start(bf16[32,4224]{1,0:T(8,128)(2,1)S(1)} %get-tuple-element.32.refs_0_), channel_id=1, source_target_pairs={{0,4},{1,3},{2,6},{3,1},{4,0},{5,7},{6,2},{7,5},{8,12},{9,11},{10,... | collective-permute-start | bytes 811016 | tf_op jit(solution)/shard_map/ppermute | solution.py:298
  19.6 7.8 %collective-permute-start.8 = (bf16[32,4224]{1,0:T(8,128)(2,1)S(1)}, bf16[32,4224]{1,0:T(8,128)(2,1)S(1)}, u32[]{:S(2)}, u32[]{:S(2)}) collective-permute-start(bf16[32,4224]{1,0:T(8,128)(2,1)S(1)} %get-tuple-element.34.refs_5_), channel_id=1, source_target_pairs={{0,4},{1,3},{2,6},{3,1},{4,0},{5,7},{6,2},{7,5},{8,12},{9,11},{10,... | collective-permute-start | bytes 811016 | tf_op jit(solution)/shard_map/ppermute | solution.py:298
  25.5 10.7 %collective-permute-start.5 = (bf16[32,4224]{1,0:T(8,128)(2,1)S(1)}, bf16[32,4224]{1,0:T(8,128)(2,1)S(1)}, u32[]{:S(2)}, u32[]{:S(2)}) collective-permute-start(bf16[32,4224]{1,0:T(8,128)(2,1)S(1)} %get-tuple-element.33.refs_1_), channel_id=1, source_target_pairs={{0,8},{2,10},{4,12},{6,14},{8,16},{10,18},{12,20},{14,22},{16,24},... | collective-permute-start | bytes 811016 | tf_op jit(solution)/shard_map/ppermute | solution.py:305
  27.5 9.4 %collective-permute-start.6 = (bf16[32,4224]{1,0:T(8,128)(2,1)S(1)}, bf16[32,4224]{1,0:T(8,128)(2,1)S(1)}, u32[]{:S(2)}, u32[]{:S(2)}) collective-permute-start(bf16[32,4224]{1,0:T(8,128)(2,1)S(1)} %get-tuple-element.33.refs_1_), channel_id=1, source_target_pairs={{0,2},{1,5},{2,0},{3,7},{4,6},{5,1},{6,4},{7,3},{8,10},{9,13},{10,... | collective-permute-start | bytes 811016 | tf_op jit(solution)/shard_map/ppermute | solution.py:297
  28.8 19.0 %collective-permute-start.18 = (bf16[32,4224]{1,0:T(8,128)(2,1)S(1)}, bf16[32,4224]{1,0:T(8,128)(2,1)S(1)}, u32[]{:S(2)}, u32[]{:S(2)}) collective-permute-start(bf16[32,4224]{1,0:T(8,128)(2,1)S(1)} %get-tuple-element.33.refs_1_), channel_id=1, source_target_pairs={{0,4},{1,3},{2,6},{3,1},{4,0},{5,7},{6,2},{7,5},{8,12},{9,11},{10,... | collective-permute-start | bytes 811016 | tf_op jit(solution)/shard_map/ppermute | solution.py:298
  30.0 10.2 %collective-permute-start.12 = (bf16[32,4224]{1,0:T(8,128)(2,1)S(1)}, bf16[32,4224]{1,0:T(8,128)(2,1)S(1)}, u32[]{:S(2)}, u32[]{:S(2)}) collective-permute-start(bf16[32,4224]{1,0:T(8,128)(2,1)S(1)} %get-tuple-element.42.refs_1_), channel_id=1, source_target_pairs={{0,4},{1,3},{2,6},{3,1},{4,0},{5,7},{6,2},{7,5},{8,12},{9,11},{10,... | collective-permute-start | bytes 811016 | tf_op jit(solution)/shard_map/ppermute | solution.py:298
  36.8 15.8 %collective-permute-start.23 = (bf16[32,4224]{1,0:T(8,128)(2,1)S(1)}, bf16[32,4224]{1,0:T(8,128)(2,1)S(1)}, u32[]{:S(2)}, u32[]{:S(2)}) collective-permute-start(bf16[32,4224]{1,0:T(8,128)(2,1)S(1)} %get-tuple-element.55.refs_1_), channel_id=1, source_target_pairs={{0,2},{1,5},{2,0},{3,7},{4,6},{5,1},{6,4},{7,3},{8,10},{9,13},{10,... | collective-permute-start | bytes 811016 | tf_op jit(solution)/shard_map/ppermute | solution.py:297
  38.1 14.5 %collective-permute-start.24 = (bf16[32,4224]{1,0:T(8,128)(2,1)S(1)}, bf16[32,4224]{1,0:T(8,128)(2,1)S(1)}, u32[]{:S(2)}, u32[]{:S(2)}) collective-permute-start(bf16[32,4224]{1,0:T(8,128)(2,1)S(1)} %get-tuple-element.55.refs_1_), channel_id=1, source_target_pairs={{0,4},{1,3},{2,6},{3,1},{4,0},{5,7},{6,2},{7,5},{8,12},{9,11},{10,... | collective-permute-start | bytes 811016 | tf_op jit(solution)/shard_map/ppermute | solution.py:298
  38.6 9.7 %collective-permute-start.19 = (bf16[32,4224]{1,0:T(8,128)(2,1)S(1)}, bf16[32,4224]{1,0:T(8,128)(2,1)S(1)}, u32[]{:S(2)}, u32[]{:S(2)}) collective-permute-start(bf16[32,4224]{1,0:T(8,128)(2,1)S(1)} %get-tuple-element.52.refs_1_), channel_id=1, source_target_pairs={{0,4},{1,3},{2,6},{3,1},{4,0},{5,7},{6,2},{7,5},{8,12},{9,11},{10,... | collective-permute-start | bytes 811016 | tf_op jit(solution)/shard_map/ppermute | solution.py:298
  40.2 13.0 %collective-permute-start.25 = (bf16[32,4224]{1,0:T(8,128)(2,1)S(1)}, bf16[32,4224]{1,0:T(8,128)(2,1)S(1)}, u32[]{:S(2)}, u32[]{:S(2)}) collective-permute-start(bf16[32,4224]{1,0:T(8,128)(2,1)S(1)} %get-tuple-element.45.refs_7_), channel_id=1, source_target_pairs={{0,24},{2,26},{4,28},{6,30},{8,0},{10,2},{12,4},{14,6},{16,8},{18,... | collective-permute-start | bytes 811016 | tf_op jit(solution)/shard_map/ppermute | solution.py:305
  47.8 9.9 %collective-permute-start.13 = (bf16[64,2176]{1,0:T(8,128)(2,1)S(1)}, bf16[64,2176]{1,0:T(8,128)(2,1)S(1)}, u32[]{:S(2)}, u32[]{:S(2)}) collective-permute-start(bf16[64,2176]{1,0:T(8,128)(2,1)S(1)} %get-tuple-element.48), channel_id=1, source_target_pairs={{0,4},{1,3},{2,6},{3,1},{4,0},{5,7},{6,2},{7,5},{8,12},{9,11},{10,... | collective-permute-start | bytes 835592 | tf_op jit(solution)/shard_map/ppermute | solution.py:298
  48.3 11.2 %collective-permute-start.16 = (bf16[64,2176]{1,0:T(8,128)(2,1)S(1)}, bf16[64,2176]{1,0:T(8,128)(2,1)S(1)}, u32[]{:S(2)}, u32[]{:S(2)}) collective-permute-start(bf16[64,2176]{1,0:T(8,128)(2,1)S(1)} %get-tuple-element.50), channel_id=1, source_target_pairs={{0,4},{1,3},{2,6},{3,1},{4,0},{5,7},{6,2},{7,5},{8,12},{9,11},{10,... | collective-permute-start | bytes 835592 | tf_op jit(solution)/shard_map/ppermute | solution.py:298
  52.7 12.4 %collective-permute-start.20 = (bf16[64,2176]{1,0:T(8,128)(2,1)S(1)}, bf16[64,2176]{1,0:T(8,128)(2,1)S(1)}, u32[]{:S(2)}, u32[]{:S(2)}) collective-permute-start(bf16[64,2176]{1,0:T(8,128)(2,1)S(1)} %get-tuple-element.56), channel_id=1, source_target_pairs={{0,4},{1,3},{2,6},{3,1},{4,0},{5,7},{6,2},{7,5},{8,12},{9,11},{10,... | collective-permute-start | bytes 835592 | tf_op jit(solution)/shard_map/ppermute | solution.py:298
  56.0 10.4 %collective-permute-start.26 = (bf16[64,2176]{1,0:T(8,128)(2,1)S(1)}, bf16[64,2176]{1,0:T(8,128)(2,1)S(1)}, u32[]{:S(2)}, u32[]{:S(2)}) collective-permute-start(bf16[64,2176]{1,0:T(8,128)(2,1)S(1)} %get-tuple-element.59), channel_id=1, source_target_pairs={{0,4},{1,3},{2,6},{3,1},{4,0},{5,7},{6,2},{7,5},{8,12},{9,11},{10,... | collective-permute-start | bytes 835592 | tf_op jit(solution)/shard_map/ppermute | solution.py:298
  59.5 12.5 %collective-permute-start.17 = (bf16[32,2176]{1,0:T(8,128)(2,1)S(1)}, bf16[32,2176]{1,0:T(8,128)(2,1)S(1)}, u32[]{:S(2)}, u32[]{:S(2)}) collective-permute-start(bf16[32,2176]{1,0:T(8,128)(2,1)S(1)} %add_convert_fusion.5), channel_id=1, source_target_pairs={{0,2},{1,5},{2,0},{3,7},{4,6},{5,1},{6,4},{7,3},{8,10},{9,13},{10,... | collective-permute-start | bytes 417800 | tf_op jit(solution)/shard_map/ppermute | solution.py:297
  62.9 9.1 %collective-permute-start.15 = (bf16[32,2176]{1,0:T(8,128)(2,1)S(1)}, bf16[32,2176]{1,0:T(8,128)(2,1)S(1)}, u32[]{:S(2)}, u32[]{:S(2)}) collective-permute-start(bf16[32,2176]{1,0:T(8,128)(2,1)S(1)} %add_convert_fusion.6), channel_id=1, source_target_pairs={{0,24},{2,26},{4,28},{6,30},{8,0},{10,2},{12,4},{14,6},{16,8},{18,... | collective-permute-start | bytes 417800 | tf_op jit(solution)/shard_map/ppermute | solution.py:305
  70.3 9.9 %collective-permute-start.22 = (bf16[32,2176]{1,0:T(8,128)(2,1)S(1)}, bf16[32,2176]{1,0:T(8,128)(2,1)S(1)}, u32[]{:S(2)}, u32[]{:S(2)}) collective-permute-start(bf16[32,2176]{1,0:T(8,128)(2,1)S(1)} %add_convert_fusion.3), channel_id=1, source_target_pairs={{0,16},{2,18},{4,20},{6,22},{8,24},{10,26},{12,28},{14,30},{16,0},... | collective-permute-start | bytes 417800 | tf_op jit(solution)/shard_map/ppermute | solution.py:305
  71.8 8.4 %collective-permute-start.28 = (bf16[32,2176]{1,0:T(8,128)(2,1)S(1)}, bf16[32,2176]{1,0:T(8,128)(2,1)S(1)}, u32[]{:S(2)}, u32[]{:S(2)}) collective-permute-start(bf16[32,2176]{1,0:T(8,128)(2,1)S(1)} %add_convert_fusion.1), channel_id=1, source_target_pairs={{0,8},{2,10},{4,12},{6,14},{8,16},{10,18},{12,20},{14,22},{16,24},... | collective-permute-start | bytes 417800 | tf_op jit(solution)/shard_map/ppermute | solution.py:305
  (11 other events, 70.7 us)

commit v4 on v3

--- a/solution.py
+++ b/solution.py
@@ -11,7 +11,7 @@
 VM = 16
 PREP = 4 * 10**9
 LAG = 10000000000
-EFLOPS = 5 * 10**9
+EFLOPS = 6 * 10**9
 CONTRACT_LAST = (((1,), (1,)), ((), ()))
 
 
@@ -222,17 +222,17 @@
     )(expert, *weights, *shards)
 
 
-def tie(*arrays, cost=1):
+def tie(*arrays, cost=1, after=()):
     return pl.pallas_call(
         lambda *refs: None,
-        in_specs=[pl.BlockSpec(memory_space=pl.ANY)] * len(arrays),
+        in_specs=[pl.BlockSpec(memory_space=pl.ANY)] * (len(arrays) + len(after)),
         out_specs=[pl.BlockSpec(memory_space=pl.ANY)] * len(arrays),
         out_shape=[jax.ShapeDtypeStruct(a.shape, a.dtype) for a in arrays],
         input_output_aliases={i: i for i in range(len(arrays))},
         compiler_params=pltpu.CompilerParams(vmem_limit_bytes=2**18),
         cost_estimate=pl.CostEstimate(flops=cost, bytes_accessed=1, transcendentals=0),
         name="tie",
-    )(*arrays)
+    )(*arrays, *after)
 
 
 def finish_kernel(half_ref, own_ref, other_ref, ids_ref, grad_ref, score_ref):
@@ -338,10 +338,17 @@
         for i, level in enumerate(batch):
             results[level] = list(outs[2 * i : 2 * i + 2])
         previous = batch[0]
+    from_second = {level: to_second(far) for level, (near, far) in results.items()}
+    from_first = {}
+    for level in [level for level in results if level not in (0, 2)]:
+        near, far = results[level]
+        from_first[level] = to_first(added(near[rows:], from_second[level][rows:]))
+    passed = added(results[2][0][rows:], from_second[2][rows:])
+    from_first[2] = to_first(passed)
+    from_first[1], from_second[0] = tie(from_first[1], from_second[0], cost=1, after=(passed,))
+    from_first[0] = to_first(added(results[0][0][rows:], from_second[0][rows:]))
     for level, (near, far) in results.items():
-        from_second = to_second(far)
-        from_first = to_first(added(near[rows:], from_second[rows:]))
-        terms = (near[:rows], from_second[:rows], from_first)
+        terms = (near[:rows], from_second[level][:rows], from_first[level])
         total += [shifted(added(*terms), levels - level)] if level else terms
     carry = added(*total)
     return finish(half, carry, swapped(carry), expert_ids, width)
@@ -360,7 +367,7 @@
 
     def per_device(tokens, cotangent, expert_ids, *others):
         experts, top = mesh.shape["expert"], expert_ids.shape[1]
-        dense = 12 <= experts <= 2 * top and experts % 4 == 0 and mesh.shape["half"] == 2
+        dense = experts // 4 > 2 and experts <= 2 * top and experts % 4 == 0 and mesh.shape["half"] == 2
         return (dense_plan if dense else routed_plan)(tokens, cotangent, expert_ids, *others)
 
     return jax.shard_map(

time: 82.8 us -> 81.5 us (0.984)
  waiting for transfers between devices: 28 us -> 24.7 us
  starting transfers between devices: 34.8 us -> 36.7 us
    ppermute x8, waiting for transfers between devices: 8.51 us -> 5.56 us  [dense_plan(): to_first = lambda a: lax.ppermute(a, axes, first_pairs)]
    ppermute x7, waiting for transfers between devices: 17.7 us -> 15 us  [dense_plan(): lax.ppermute(a, 'expert', [(e, (e + 4 * by) % experts) for e in range(exp...]
    ppermute x11, waiting for transfers between devices: 0.49 us -> 2.82 us  [dense_plan(): to_second = lambda a: lax.ppermute(a, axes, second_pairs)]
    ppermute x8, starting transfers between devices: 11.9 us -> 14.1 us  [dense_plan(): to_first = lambda a: lax.ppermute(a, axes, first_pairs)]
  transfers between devices with their start and end apart: 30 -> 30, of which waited for: 11 -> 10; matrix products, arithmetic and copies ran while one was open for 0% -> 0% of each run, Pallas kernels for 19% -> 19%
where the time goes in v4:
time: 81.5 us; the launch traced here: 81.3 us
  starting transfers between devices  36.7 us (45%)
  waiting for transfers between devices  24.7 us (30%)
  Pallas kernels  18.7 us (23%)
  between operations  0.82 us (1%)
    ppermute x7, waiting for transfers between devices, dense_plan(): lax.ppermute(a, 'expert', [(e, (e + 4 * by) % experts) for e in range(exp...  15 us
    ppermute x8, starting transfers between devices, dense_plan(): to_first = lambda a: lax.ppermute(a, axes, first_pairs)  14.1 us
    ppermute x11, starting transfers between devices, dense_plan(): to_second = lambda a: lax.ppermute(a, axes, second_pairs)  12 us
    pallas_call x3, Pallas kernels, expert_call(): pl.pallas_call(functools.partial(expert_kernel, experts), in_specs=[pl.Bl...  10.8 us
    ppermute x7, starting transfers between devices, dense_plan(): lax.ppermute(a, 'expert', [(e, (e + 4 * by) % experts) for e in range(exp...  10.6 us
    ppermute x8, waiting for transfers between devices, dense_plan(): to_first = lambda a: lax.ppermute(a, axes, first_pairs)  5.56 us
    pallas_call x1, Pallas kernels, lay_out(): pl.pallas_call(lambda a, b, c, d, e, f: layout_kernel((a, c), (b, d), e,...  4.19 us
    ppermute x11, waiting for transfers between devices, dense_plan(): to_second = lambda a: lax.ppermute(a, axes, second_pairs)  2.82 us
  transfers between devices with their start and end apart: 30, of which 10 were waited for; matrix products, arithmetic and copies ran while one was open for 0% of the time, Pallas kernels for 19%

profile of v4, /device:TPU:0, one launch (start us, length us, event | category | flops | bytes accessed | tf_op | source)
XLA Modules:
  0.0 81.3 jit_solution(2434191198064469356)
XLA Ops:
  0.6 1.9 %pack.1.refs_4_ = bf16[32,4224]{1,0:T(8,128)(2,1)} custom-call(s32[1]{0:T(128)} %bitcast.half_ref, bf16[64,2048]{1,0:T(8,128)(2,1)} %tok_ref.1, bf16[64,2048]{1,0:T(8,128)(2,1)} %cot_ref.1, s32[8,64]{1,0:T(8,128)} %bitcast.8, f32[8,64]{1,0:T(8,128)} %bitcast.16), custom_call_target="tpu_custom_call" | custom-call | tf_op jit(solution)/shard_map/pack/pallas_call | solution.py:121
  2.5 3.0 %collective-permute-start = (bf16[32,4224]{1,0:T(8,128)(2,1)}, bf16[32,4224]{1,0:T(8,128)(2,1)S(1)}, u32[]{:S(2)}, u32[]{:S(2)}) collective-permute-start(bf16[32,4224]{1,0:T(8,128)(2,1)} %pack.1.refs_4_), channel_id=1, source_target_pairs={{0,8},{2,10},{4,12},{6,14},{8,16},{10,18},{12,20},{14,22},{16,24},... | collective-permute-start | bytes 811016 | tf_op jit(solution)/shard_map/ppermute | solution.py:305
  7.1 1.5 %collective-permute-start.4 = (bf16[32,4224]{1,0:T(8,128)(2,1)}, bf16[32,4224]{1,0:T(8,128)(2,1)S(1)}, u32[]{:S(2)}, u32[]{:S(2)}) collective-permute-start(bf16[32,4224]{1,0:T(8,128)(2,1)} %pack.1.refs_4_), channel_id=1, source_target_pairs={{0,4},{1,3},{2,6},{3,1},{4,0},{5,7},{6,2},{7,5},{8,12},{9,11},{10,... | collective-permute-start | bytes 811016 | tf_op jit(solution)/shard_map/ppermute | solution.py:298
  8.6 5.7 %collective-permute-done.refs_0_ = bf16[32,4224]{1,0:T(8,128)(2,1)S(1)} collective-permute-done((bf16[32,4224]{1,0:T(8,128)(2,1)}, bf16[32,4224]{1,0:T(8,128)(2,1)S(1)}, u32[]{:S(2)}, u32[]{:S(2)}) %collective-permute-start) | collective-permute-done | bytes 270368 | tf_op jit(solution)/shard_map/ppermute | solution.py:305
  15.8 2.4 %collective-permute-start.3 = (bf16[32,4224]{1,0:T(8,128)(2,1)S(1)}, bf16[32,4224]{1,0:T(8,128)(2,1)S(1)}, u32[]{:S(2)}, u32[]{:S(2)}) collective-permute-start(bf16[32,4224]{1,0:T(8,128)(2,1)S(1)} %get-tuple-element.34.refs_0_), channel_id=1, source_target_pairs={{0,2},{1,5},{2,0},{3,7},{4,6},{5,1},{6,4},{7,3},{8,10},{9,13},{10,... | collective-permute-start | bytes 811016 | tf_op jit(solution)/shard_map/ppermute | solution.py:297
  18.1 1.5 %collective-permute-start.7 = (bf16[32,4224]{1,0:T(8,128)(2,1)S(1)}, bf16[32,4224]{1,0:T(8,128)(2,1)S(1)}, u32[]{:S(2)}, u32[]{:S(2)}) collective-permute-start(bf16[32,4224]{1,0:T(8,128)(2,1)S(1)} %get-tuple-element.34.refs_0_), channel_id=1, source_target_pairs={{0,4},{1,3},{2,6},{3,1},{4,0},{5,7},{6,2},{7,5},{8,12},{9,11},{10,... | collective-permute-start | bytes 811016 | tf_op jit(solution)/shard_map/ppermute | solution.py:298
  20.2 3.6 %collective-permute-done.2.refs_0_ = bf16[32,4224]{1,0:T(8,128)(2,1)S(1)} collective-permute-done((bf16[32,4224]{1,0:T(8,128)(2,1)S(1)}, bf16[32,4224]{1,0:T(8,128)(2,1)S(1)}, u32[]{:S(2)}, u32[]{:S(2)}) %collective-permute-start.2) | collective-permute-done | bytes 270368 | tf_op jit(solution)/shard_map/ppermute | solution.py:305
  23.8 1.8 %collective-permute-done.3.refs_1_ = bf16[32,4224]{1,0:T(8,128)(2,1)S(1)} collective-permute-done((bf16[32,4224]{1,0:T(8,128)(2,1)S(1)}, bf16[32,4224]{1,0:T(8,128)(2,1)S(1)}, u32[]{:S(2)}, u32[]{:S(2)}) %collective-permute-start.3) | collective-permute-done | bytes 270368 | tf_op jit(solution)/shard_map/ppermute | solution.py:297
  30.0 1.8 %collective-permute-start.12 = (bf16[32,4224]{1,0:T(8,128)(2,1)S(1)}, bf16[32,4224]{1,0:T(8,128)(2,1)S(1)}, u32[]{:S(2)}, u32[]{:S(2)}) collective-permute-start(bf16[32,4224]{1,0:T(8,128)(2,1)S(1)} %get-tuple-element.44.refs_1_), channel_id=1, source_target_pairs={{0,4},{1,3},{2,6},{3,1},{4,0},{5,7},{6,2},{7,5},{8,12},{9,11},{10,... | collective-permute-start | bytes 811016 | tf_op jit(solution)/shard_map/ppermute | solution.py:298
  31.8 4.2 %layout.1 = (bf16[2048,1536]{1,0:T(8,128)(2,1)S(1)}, bf16[1536,2048]{1,0:T(8,128)(2,1)S(1)}) custom-call(bf16[2048,384]{1,0:T(8,128)(2,1)S(1)} %bitcast.13, bf16[2048,384]{1,0:T(8,128)(2,1)} %collective-permute-done.9.b, bf16[2048,384]{1,0:T(8,128)(2,1)S(1)} %bitcast.15, bf16[2048,384]{1,0:T(8,128)(2,1)} %collective-permute-done.10.d), custom_call_target="tpu_custom_call" | custom-call | flops 4000000000 | bytes 1 | tf_op jit(solution)/shard_map/layout/pallas_call | solution.py:185
  38.6 1.6 %collective-permute-start.17 = (bf16[32,4224]{1,0:T(8,128)(2,1)S(1)}, bf16[32,4224]{1,0:T(8,128)(2,1)S(1)}, u32[]{:S(2)}, u32[]{:S(2)}) collective-permute-start(bf16[32,4224]{1,0:T(8,128)(2,1)S(1)} %get-tuple-element.53.refs_1_), channel_id=1, source_target_pairs={{0,4},{1,3},{2,6},{3,1},{4,0},{5,7},{6,2},{7,5},{8,12},{9,11},{10,... | collective-permute-start | bytes 811016 | tf_op jit(solution)/shard_map/ppermute | solution.py:298
  40.2 2.4 %collective-permute-start.25 = (bf16[32,4224]{1,0:T(8,128)(2,1)S(1)}, bf16[32,4224]{1,0:T(8,128)(2,1)S(1)}, u32[]{:S(2)}, u32[]{:S(2)}) collective-permute-start(bf16[32,4224]{1,0:T(8,128)(2,1)S(1)} %get-tuple-element.47.refs_7_), channel_id=1, source_target_pairs={{0,24},{2,26},{4,28},{6,30},{8,0},{10,2},{12,4},{14,6},{16,8},{18,... | collective-permute-start | bytes 811016 | tf_op jit(solution)/shard_map/ppermute | solution.py:305
  42.6 5.1 %expert.3 = (bf16[64,2176]{1,0:T(8,128)(2,1)S(1)}, bf16[64,2176]{1,0:T(8,128)(2,1)S(1)}, bf16[64,2176]{1,0:T(8,128)(2,1)S(1)}, bf16[64,2176]{1,0:T(8,128)(2,1)S(1)}) custom-call(s32[1]{0:T(128)} %bitcast.1.expert_ref, bf16[2048,1536]{1,0:T(8,128)(2,1)S(1)} %get-tuple-element.41.gate_up_ref, bf16[1536,2048]{1,0:T(8,128)(2,1)S(1)} %get-tuple-element.42.gate_up_t_ref, ...), custom_call_target="tpu_custom_call" | custom-call | flops 6000000000 | bytes 1 | tf_op jit(solution)/shard_map/expert/pallas_call | solution.py:214
  48.3 1.6 %collective-permute-start.15 = (bf16[64,2176]{1,0:T(8,128)(2,1)S(1)}, bf16[64,2176]{1,0:T(8,128)(2,1)S(1)}, u32[]{:S(2)}, u32[]{:S(2)}) collective-permute-start(bf16[64,2176]{1,0:T(8,128)(2,1)S(1)} %get-tuple-element.51), channel_id=1, source_target_pairs={{0,4},{1,3},{2,6},{3,1},{4,0},{5,7},{6,2},{7,5},{8,12},{9,11},{10,... | collective-permute-start | bytes 835592 | tf_op jit(solution)/shard_map/ppermute | solution.py:298
  49.9 2.8 %expert.4 = (bf16[64,2176]{1,0:T(8,128)(2,1)S(1)}, bf16[64,2176]{1,0:T(8,128)(2,1)S(1)}) custom-call(s32[1]{0:T(128)} %bitcast.1.expert_ref, bf16[2048,1536]{1,0:T(8,128)(2,1)S(1)} %get-tuple-element.41.gate_up_ref, bf16[1536,2048]{1,0:T(8,128)(2,1)S(1)} %get-tuple-element.42.gate_up_t_ref, bf16[2048,768]{1,0:T(8,128)(2,1)S(1)} %get-tuple-element.43.down_t_ref, ...), custom_call_target="tpu_custom_call" | custom-call | flops 6000000000 | bytes 1 | tf_op jit(solution)/shard_map/expert/pallas_call | solution.py:214
  53.2 2.8 %expert.5 = (bf16[64,2176]{1,0:T(8,128)(2,1)S(1)}, bf16[64,2176]{1,0:T(8,128)(2,1)S(1)}) custom-call(s32[1]{0:T(128)} %bitcast.1.expert_ref, bf16[2048,1536]{1,0:T(8,128)(2,1)S(1)} %get-tuple-element.41.gate_up_ref, bf16[1536,2048]{1,0:T(8,128)(2,1)S(1)} %get-tuple-element.42.gate_up_t_ref, bf16[2048,768]{1,0:T(8,128)(2,1)S(1)} %get-tuple-element.43.down_t_ref, ...), custom_call_target="tpu_custom_call" | custom-call | flops 6000000000 | bytes 1 | tf_op jit(solution)/shard_map/expert/pallas_call | solution.py:214
  56.1 1.6 %collective-permute-start.26 = (bf16[64,2176]{1,0:T(8,128)(2,1)S(1)}, bf16[64,2176]{1,0:T(8,128)(2,1)S(1)}, u32[]{:S(2)}, u32[]{:S(2)}) collective-permute-start(bf16[64,2176]{1,0:T(8,128)(2,1)S(1)} %get-tuple-element.63), channel_id=1, source_target_pairs={{0,4},{1,3},{2,6},{3,1},{4,0},{5,7},{6,2},{7,5},{8,12},{9,11},{10,... | collective-permute-start | bytes 835592 | tf_op jit(solution)/shard_map/ppermute | solution.py:298
  57.7 1.7 %collective-permute-start.14 = (bf16[32,2176]{1,0:T(8,128)(2,1)S(1)}, bf16[32,2176]{1,0:T(8,128)(2,1)S(1)}, u32[]{:S(2)}, u32[]{:S(2)}) collective-permute-start(bf16[32,2176]{1,0:T(8,128)(2,1)S(1)} %add_convert_fusion.7), channel_id=1, source_target_pairs={{0,2},{1,5},{2,0},{3,7},{4,6},{5,1},{6,4},{7,3},{8,10},{9,13},{10,... | collective-permute-start | bytes 417800 | tf_op jit(solution)/shard_map/ppermute | solution.py:297
  59.5 2.3 %collective-permute-done.18 = bf16[64,2176]{1,0:T(8,128)(2,1)S(1)} collective-permute-done((bf16[64,2176]{1,0:T(8,128)(2,1)S(1)}, bf16[64,2176]{1,0:T(8,128)(2,1)S(1)}, u32[]{:S(2)}, u32[]{:S(2)}) %collective-permute-start.18) | collective-permute-done | bytes 278560 | tf_op jit(solution)/shard_map/ppermute | solution.py:298
  61.8 2.6 %collective-permute-start.21 = (bf16[32,2176]{1,0:T(8,128)(2,1)S(1)}, bf16[32,2176]{1,0:T(8,128)(2,1)S(1)}, u32[]{:S(2)}, u32[]{:S(2)}) collective-permute-start(bf16[32,2176]{1,0:T(8,128)(2,1)S(1)} %add_convert_fusion.6.refs_2_), channel_id=1, source_target_pairs={{0,2},{1,5},{2,0},{3,7},{4,6},{5,1},{6,4},{7,3},{8,10},{9,13},{10,... | collective-permute-start | bytes 417800 | tf_op jit(solution)/shard_map/ppermute | solution.py:297
  66.5 2.0 %collective-permute-start.27 = (bf16[32,2176]{1,0:T(8,128)(2,1)S(1)}, bf16[32,2176]{1,0:T(8,128)(2,1)S(1)}, u32[]{:S(2)}, u32[]{:S(2)}) collective-permute-start(bf16[32,2176]{1,0:T(8,128)(2,1)S(1)} %add_convert_fusion.2), channel_id=1, source_target_pairs={{0,2},{1,5},{2,0},{3,7},{4,6},{5,1},{6,4},{7,3},{8,10},{9,13},{10,... | collective-permute-start | bytes 417800 | tf_op jit(solution)/shard_map/ppermute | solution.py:297
  68.6 3.2 %collective-permute-done.27 = bf16[32,2176]{1,0:T(8,128)(2,1)S(1)} collective-permute-done((bf16[32,2176]{1,0:T(8,128)(2,1)S(1)}, bf16[32,2176]{1,0:T(8,128)(2,1)S(1)}, u32[]{:S(2)}, u32[]{:S(2)}) %collective-permute-start.27) | collective-permute-done | bytes 139296 | tf_op jit(solution)/shard_map/ppermute | solution.py:297
  71.8 1.6 %collective-permute-start.28 = (bf16[32,2176]{1,0:T(8,128)(2,1)S(1)}, bf16[32,2176]{1,0:T(8,128)(2,1)S(1)}, u32[]{:S(2)}, u32[]{:S(2)}) collective-permute-start(bf16[32,2176]{1,0:T(8,128)(2,1)S(1)} %add_convert_fusion.1), channel_id=1, source_target_pairs={{0,8},{2,10},{4,12},{6,14},{8,16},{10,18},{12,20},{14,22},{16,24},... | collective-permute-start | bytes 417800 | tf_op jit(solution)/shard_map/ppermute | solution.py:305
  73.4 5.5 %collective-permute-done.22 = bf16[32,2176]{1,0:T(8,128)(2,1)S(1)} collective-permute-done((bf16[32,2176]{1,0:T(8,128)(2,1)S(1)}, bf16[32,2176]{1,0:T(8,128)(2,1)S(1)}, u32[]{:S(2)}, u32[]{:S(2)}) %collective-permute-start.22) | collective-permute-done | bytes 139296 | tf_op jit(solution)/shard_map/ppermute | solution.py:305
  (68 shorter events, 16.3 us)
Async XLA Ops:
  2.5 11.7 %collective-permute-start = (bf16[32,4224]{1,0:T(8,128)(2,1)}, bf16[32,4224]{1,0:T(8,128)(2,1)S(1)}, u32[]{:S(2)}, u32[]{:S(2)}) collective-permute-start(bf16[32,4224]{1,0:T(8,128)(2,1)} %pack.1.refs_4_), channel_id=1, source_target_pairs={{0,8},{2,10},{4,12},{6,14},{8,16},{10,18},{12,20},{14,22},{16,24},... | collective-permute-start | bytes 811016 | tf_op jit(solution)/shard_map/ppermute | solution.py:305
  5.6 8.7 %collective-permute-start.1 = (bf16[32,4224]{1,0:T(8,128)(2,1)}, bf16[32,4224]{1,0:T(8,128)(2,1)S(1)}, u32[]{:S(2)}, u32[]{:S(2)}) collective-permute-start(bf16[32,4224]{1,0:T(8,128)(2,1)} %pack.1.refs_4_), channel_id=1, source_target_pairs={{0,2},{1,5},{2,0},{3,7},{4,6},{5,1},{6,4},{7,3},{8,10},{9,13},{10,... | collective-permute-start | bytes 811016 | tf_op jit(solution)/shard_map/ppermute | solution.py:297
  7.1 21.7 %collective-permute-start.11 = (bf16[384,2048]{1,0:T(8,128)(2,1)}, bf16[384,2048]{1,0:T(8,128)(2,1)S(1)}, u32[]{:S(2)}, u32[]{:S(2)}) collective-permute-start(bf16[384,2048]{1,0:T(8,128)(2,1)} %bitcast.10), channel_id=1, source_target_pairs={{0,1},{1,0},{2,3},{3,2},{4,5},{5,4},{6,7},{7,6},{8,9},{9,8},{10,11... | collective-permute-start | bytes 4718600 | tf_op jit(solution)/shard_map/ppermute | solution.py:299
  7.1 12.6 %collective-permute-start.4 = (bf16[32,4224]{1,0:T(8,128)(2,1)}, bf16[32,4224]{1,0:T(8,128)(2,1)S(1)}, u32[]{:S(2)}, u32[]{:S(2)}) collective-permute-start(bf16[32,4224]{1,0:T(8,128)(2,1)} %pack.1.refs_4_), channel_id=1, source_target_pairs={{0,4},{1,3},{2,6},{3,1},{4,0},{5,7},{6,2},{7,5},{8,12},{9,11},{10,... | collective-permute-start | bytes 811016 | tf_op jit(solution)/shard_map/ppermute | solution.py:298
  14.3 9.5 %collective-permute-start.2 = (bf16[32,4224]{1,0:T(8,128)(2,1)S(1)}, bf16[32,4224]{1,0:T(8,128)(2,1)S(1)}, u32[]{:S(2)}, u32[]{:S(2)}) collective-permute-start(bf16[32,4224]{1,0:T(8,128)(2,1)S(1)} %get-tuple-element.34.refs_0_), channel_id=1, source_target_pairs={{0,8},{2,10},{4,12},{6,14},{8,16},{10,18},{12,20},{14,22},{16,24},... | collective-permute-start | bytes 811016 | tf_op jit(solution)/shard_map/ppermute | solution.py:305
  15.8 9.8 %collective-permute-start.3 = (bf16[32,4224]{1,0:T(8,128)(2,1)S(1)}, bf16[32,4224]{1,0:T(8,128)(2,1)S(1)}, u32[]{:S(2)}, u32[]{:S(2)}) collective-permute-start(bf16[32,4224]{1,0:T(8,128)(2,1)S(1)} %get-tuple-element.34.refs_0_), channel_id=1, source_target_pairs={{0,2},{1,5},{2,0},{3,7},{4,6},{5,1},{6,4},{7,3},{8,10},{9,13},{10,... | collective-permute-start | bytes 811016 | tf_op jit(solution)/shard_map/ppermute | solution.py:297
  18.1 7.4 %collective-permute-start.7 = (bf16[32,4224]{1,0:T(8,128)(2,1)S(1)}, bf16[32,4224]{1,0:T(8,128)(2,1)S(1)}, u32[]{:S(2)}, u32[]{:S(2)}) collective-permute-start(bf16[32,4224]{1,0:T(8,128)(2,1)S(1)} %get-tuple-element.34.refs_0_), channel_id=1, source_target_pairs={{0,4},{1,3},{2,6},{3,1},{4,0},{5,7},{6,2},{7,5},{8,12},{9,11},{10,... | collective-permute-start | bytes 811016 | tf_op jit(solution)/shard_map/ppermute | solution.py:298
  19.7 7.8 %collective-permute-start.8 = (bf16[32,4224]{1,0:T(8,128)(2,1)S(1)}, bf16[32,4224]{1,0:T(8,128)(2,1)S(1)}, u32[]{:S(2)}, u32[]{:S(2)}) collective-permute-start(bf16[32,4224]{1,0:T(8,128)(2,1)S(1)} %get-tuple-element.36.refs_5_), channel_id=1, source_target_pairs={{0,4},{1,3},{2,6},{3,1},{4,0},{5,7},{6,2},{7,5},{8,12},{9,11},{10,... | collective-permute-start | bytes 811016 | tf_op jit(solution)/shard_map/ppermute | solution.py:298
  25.5 10.7 %collective-permute-start.5 = (bf16[32,4224]{1,0:T(8,128)(2,1)S(1)}, bf16[32,4224]{1,0:T(8,128)(2,1)S(1)}, u32[]{:S(2)}, u32[]{:S(2)}) collective-permute-start(bf16[32,4224]{1,0:T(8,128)(2,1)S(1)} %get-tuple-element.35.refs_1_), channel_id=1, source_target_pairs={{0,8},{2,10},{4,12},{6,14},{8,16},{10,18},{12,20},{14,22},{16,24},... | collective-permute-start | bytes 811016 | tf_op jit(solution)/shard_map/ppermute | solution.py:305
  27.5 9.4 %collective-permute-start.6 = (bf16[32,4224]{1,0:T(8,128)(2,1)S(1)}, bf16[32,4224]{1,0:T(8,128)(2,1)S(1)}, u32[]{:S(2)}, u32[]{:S(2)}) collective-permute-start(bf16[32,4224]{1,0:T(8,128)(2,1)S(1)} %get-tuple-element.35.refs_1_), channel_id=1, source_target_pairs={{0,2},{1,5},{2,0},{3,7},{4,6},{5,1},{6,4},{7,3},{8,10},{9,13},{10,... | collective-permute-start | bytes 811016 | tf_op jit(solution)/shard_map/ppermute | solution.py:297
  28.8 19.0 %collective-permute-start.16 = (bf16[32,4224]{1,0:T(8,128)(2,1)S(1)}, bf16[32,4224]{1,0:T(8,128)(2,1)S(1)}, u32[]{:S(2)}, u32[]{:S(2)}) collective-permute-start(bf16[32,4224]{1,0:T(8,128)(2,1)S(1)} %get-tuple-element.35.refs_1_), channel_id=1, source_target_pairs={{0,4},{1,3},{2,6},{3,1},{4,0},{5,7},{6,2},{7,5},{8,12},{9,11},{10,... | collective-permute-start | bytes 811016 | tf_op jit(solution)/shard_map/ppermute | solution.py:298
  30.0 10.2 %collective-permute-start.12 = (bf16[32,4224]{1,0:T(8,128)(2,1)S(1)}, bf16[32,4224]{1,0:T(8,128)(2,1)S(1)}, u32[]{:S(2)}, u32[]{:S(2)}) collective-permute-start(bf16[32,4224]{1,0:T(8,128)(2,1)S(1)} %get-tuple-element.44.refs_1_), channel_id=1, source_target_pairs={{0,4},{1,3},{2,6},{3,1},{4,0},{5,7},{6,2},{7,5},{8,12},{9,11},{10,... | collective-permute-start | bytes 811016 | tf_op jit(solution)/shard_map/ppermute | solution.py:298
  36.9 15.8 %collective-permute-start.23 = (bf16[32,4224]{1,0:T(8,128)(2,1)S(1)}, bf16[32,4224]{1,0:T(8,128)(2,1)S(1)}, u32[]{:S(2)}, u32[]{:S(2)}) collective-permute-start(bf16[32,4224]{1,0:T(8,128)(2,1)S(1)} %get-tuple-element.56.refs_1_), channel_id=1, source_target_pairs={{0,2},{1,5},{2,0},{3,7},{4,6},{5,1},{6,4},{7,3},{8,10},{9,13},{10,... | collective-permute-start | bytes 811016 | tf_op jit(solution)/shard_map/ppermute | solution.py:297
  38.1 14.5 %collective-permute-start.24 = (bf16[32,4224]{1,0:T(8,128)(2,1)S(1)}, bf16[32,4224]{1,0:T(8,128)(2,1)S(1)}, u32[]{:S(2)}, u32[]{:S(2)}) collective-permute-start(bf16[32,4224]{1,0:T(8,128)(2,1)S(1)} %get-tuple-element.56.refs_1_), channel_id=1, source_target_pairs={{0,4},{1,3},{2,6},{3,1},{4,0},{5,7},{6,2},{7,5},{8,12},{9,11},{10,... | collective-permute-start | bytes 811016 | tf_op jit(solution)/shard_map/ppermute | solution.py:298
  38.6 9.7 %collective-permute-start.17 = (bf16[32,4224]{1,0:T(8,128)(2,1)S(1)}, bf16[32,4224]{1,0:T(8,128)(2,1)S(1)}, u32[]{:S(2)}, u32[]{:S(2)}) collective-permute-start(bf16[32,4224]{1,0:T(8,128)(2,1)S(1)} %get-tuple-element.53.refs_1_), channel_id=1, source_target_pairs={{0,4},{1,3},{2,6},{3,1},{4,0},{5,7},{6,2},{7,5},{8,12},{9,11},{10,... | collective-permute-start | bytes 811016 | tf_op jit(solution)/shard_map/ppermute | solution.py:298
  40.2 13.0 %collective-permute-start.25 = (bf16[32,4224]{1,0:T(8,128)(2,1)S(1)}, bf16[32,4224]{1,0:T(8,128)(2,1)S(1)}, u32[]{:S(2)}, u32[]{:S(2)}) collective-permute-start(bf16[32,4224]{1,0:T(8,128)(2,1)S(1)} %get-tuple-element.47.refs_7_), channel_id=1, source_target_pairs={{0,24},{2,26},{4,28},{6,30},{8,0},{10,2},{12,4},{14,6},{16,8},{18,... | collective-permute-start | bytes 811016 | tf_op jit(solution)/shard_map/ppermute | solution.py:305
  47.8 9.9 %collective-permute-start.13 = (bf16[64,2176]{1,0:T(8,128)(2,1)S(1)}, bf16[64,2176]{1,0:T(8,128)(2,1)S(1)}, u32[]{:S(2)}, u32[]{:S(2)}) collective-permute-start(bf16[64,2176]{1,0:T(8,128)(2,1)S(1)} %get-tuple-element.50), channel_id=1, source_target_pairs={{0,4},{1,3},{2,6},{3,1},{4,0},{5,7},{6,2},{7,5},{8,12},{9,11},{10,... | collective-permute-start | bytes 835592 | tf_op jit(solution)/shard_map/ppermute | solution.py:298
  48.3 16.2 %collective-permute-start.15 = (bf16[64,2176]{1,0:T(8,128)(2,1)S(1)}, bf16[64,2176]{1,0:T(8,128)(2,1)S(1)}, u32[]{:S(2)}, u32[]{:S(2)}) collective-permute-start(bf16[64,2176]{1,0:T(8,128)(2,1)S(1)} %get-tuple-element.51), channel_id=1, source_target_pairs={{0,4},{1,3},{2,6},{3,1},{4,0},{5,7},{6,2},{7,5},{8,12},{9,11},{10,... | collective-permute-start | bytes 835592 | tf_op jit(solution)/shard_map/ppermute | solution.py:298
  52.7 9.1 %collective-permute-start.18 = (bf16[64,2176]{1,0:T(8,128)(2,1)S(1)}, bf16[64,2176]{1,0:T(8,128)(2,1)S(1)}, u32[]{:S(2)}, u32[]{:S(2)}) collective-permute-start(bf16[64,2176]{1,0:T(8,128)(2,1)S(1)} %get-tuple-element.57), channel_id=1, source_target_pairs={{0,4},{1,3},{2,6},{3,1},{4,0},{5,7},{6,2},{7,5},{8,12},{9,11},{10,... | collective-permute-start | bytes 835592 | tf_op jit(solution)/shard_map/ppermute | solution.py:298
  56.1 10.4 %collective-permute-start.26 = (bf16[64,2176]{1,0:T(8,128)(2,1)S(1)}, bf16[64,2176]{1,0:T(8,128)(2,1)S(1)}, u32[]{:S(2)}, u32[]{:S(2)}) collective-permute-start(bf16[64,2176]{1,0:T(8,128)(2,1)S(1)} %get-tuple-element.63), channel_id=1, source_target_pairs={{0,4},{1,3},{2,6},{3,1},{4,0},{5,7},{6,2},{7,5},{8,12},{9,11},{10,... | collective-permute-start | bytes 835592 | tf_op jit(solution)/shard_map/ppermute | solution.py:298
  64.5 8.8 %collective-permute-start.19 = (bf16[32,2176]{1,0:T(8,128)(2,1)S(1)}, bf16[32,2176]{1,0:T(8,128)(2,1)S(1)}, u32[]{:S(2)}, u32[]{:S(2)}) collective-permute-start(bf16[32,2176]{1,0:T(8,128)(2,1)S(1)} %add_convert_fusion.5), channel_id=1, source_target_pairs={{0,24},{2,26},{4,28},{6,30},{8,0},{10,2},{12,4},{14,6},{16,8},{18,... | collective-permute-start | bytes 417800 | tf_op jit(solution)/shard_map/ppermute | solution.py:305
  65.1 8.3 %collective-permute-start.20 = (bf16[32,2176]{1,0:T(8,128)(2,1)S(1)}, bf16[32,2176]{1,0:T(8,128)(2,1)S(1)}, u32[]{:S(2)}, u32[]{:S(2)}) collective-permute-start(bf16[32,2176]{1,0:T(8,128)(2,1)S(1)} %add_convert_fusion.4), channel_id=1, source_target_pairs={{0,2},{1,5},{2,0},{3,7},{4,6},{5,1},{6,4},{7,3},{8,10},{9,13},{10,... | collective-permute-start | bytes 417800 | tf_op jit(solution)/shard_map/ppermute | solution.py:297
  68.5 10.3 %collective-permute-start.22 = (bf16[32,2176]{1,0:T(8,128)(2,1)S(1)}, bf16[32,2176]{1,0:T(8,128)(2,1)S(1)}, u32[]{:S(2)}, u32[]{:S(2)}) collective-permute-start(bf16[32,2176]{1,0:T(8,128)(2,1)S(1)} %add_convert_fusion.3), channel_id=1, source_target_pairs={{0,16},{2,18},{4,20},{6,22},{8,24},{10,26},{12,28},{14,30},{16,0},... | collective-permute-start | bytes 417800 | tf_op jit(solution)/shard_map/ppermute | solution.py:305
  71.8 7.1 %collective-permute-start.28 = (bf16[32,2176]{1,0:T(8,128)(2,1)S(1)}, bf16[32,2176]{1,0:T(8,128)(2,1)S(1)}, u32[]{:S(2)}, u32[]{:S(2)}) collective-permute-start(bf16[32,2176]{1,0:T(8,128)(2,1)S(1)} %add_convert_fusion.1), channel_id=1, source_target_pairs={{0,8},{2,10},{4,12},{6,14},{8,16},{10,18},{12,20},{14,22},{16,24},... | collective-permute-start | bytes 417800 | tf_op jit(solution)/shard_map/ppermute | solution.py:305
  (11 other events, 72.4 us)

commit v5 on v4

--- a/solution.py
+++ b/solution.py
@@ -136,32 +136,54 @@
     )(half, tokens, cotangent, expert_ids.T, gate_weights.T)
 
 
-def expert_kernel(experts, expert_ref, gate_up_ref, gate_up_t_ref, down_t_ref, *refs):
-    shard_refs, out_refs = refs[: 2 * len(refs) // 3], refs[2 * len(refs) // 3 :]
-    rows = 2 * shard_refs[0].shape[0]
+def plane_rows(experts, expert, gate_up_ref, gate_up_t_ref, down_t_ref, packed, out_refs):
+    rows = packed.shape[0] // 2
     width, units = down_t_ref.shape
-    packed = jnp.concatenate([ref[...] for ref in shard_refs], axis=0)
-    pre = jnp.dot(packed[:, :width], gate_up_ref[...], preferred_element_type=jnp.float32)
-    grad_hidden = jnp.dot(packed[:, width : 2 * width], down_t_ref[...], preferred_element_type=jnp.float32)
-    gate_pre, up_pre = pre[:, :units], pre[:, units:]
-    sigmoid_gate = 1.0 / (1.0 + jnp.exp(-gate_pre))
-    grad_up = grad_hidden * gate_pre * sigmoid_gate
-    scores = jnp.sum(grad_up * up_pre, axis=1, keepdims=True)
-    grad_gate = grad_hidden * up_pre * sigmoid_gate * (1.0 + gate_pre * (1.0 - sigmoid_gate))
-    grads = jnp.concatenate([grad_gate.astype(jnp.bfloat16), grad_up.astype(jnp.bfloat16)], axis=1)
-    part = jnp.dot(grads, gate_up_t_ref[...], preferred_element_type=jnp.float32)
-    expert = expert_ref[0]
     routing = packed[:, 2 * width :].astype(jnp.float32)
     lane = lax.broadcasted_iota(jnp.int32, routing.shape, 1)
     weight = jnp.sum(
         jnp.where((lane == expert) | (lane == expert + experts), routing, 0.0), axis=1, keepdims=True
     )
-    part = (part * weight).astype(jnp.bfloat16)
+    tokens, grads = packed[:, :width], packed[:, width : 2 * width]
+    scores, gate_parts, up_parts = 0.0, [], []
+    block = units
+    for start in range(0, units, block):
+        gate_pre = jnp.dot(tokens, gate_up_ref[:, start : start + block], preferred_element_type=jnp.float32)
+        up_pre = jnp.dot(
+            tokens, gate_up_ref[:, units + start : units + start + block], preferred_element_type=jnp.float32
+        )
+        grad_hidden = jnp.dot(grads, down_t_ref[:, start : start + block], preferred_element_type=jnp.float32)
+        sigmoid_gate = 1.0 / (1.0 + jnp.exp(-gate_pre))
+        grad_up = grad_hidden * gate_pre * sigmoid_gate
+        scores += jnp.sum(grad_up * up_pre, axis=1, keepdims=True)
+        grad_gate = grad_hidden * up_pre * sigmoid_gate * (1.0 + gate_pre * (1.0 - sigmoid_gate))
+        gate_parts.append(grad_gate.astype(jnp.bfloat16))
+        up_parts.append(grad_up.astype(jnp.bfloat16))
+    hidden = jnp.concatenate(gate_parts + up_parts, axis=1)
+    block = width
+    for start in range(0, width, block):
+        part = jnp.dot(hidden, gate_up_t_ref[:, start : start + block], preferred_element_type=jnp.float32)
+        part = (part * weight).astype(jnp.bfloat16)
+        for i, ref in enumerate(out_refs):
+            ref[:, start : start + block] = part[i * rows : (i + 1) * rows]
     column = lax.broadcasted_iota(jnp.int32, (packed.shape[0], out_refs[0].shape[1] - width), 1)
     score_part = jnp.where(column == expert, scores, 0.0).astype(jnp.bfloat16)
     for i, ref in enumerate(out_refs):
-        ref[:, :width] = part[i * rows : (i + 1) * rows]
         ref[:, width:] = score_part[i * rows : (i + 1) * rows]
+
+
+def expert_kernel(experts, expert_ref, gate_up_ref, gate_up_t_ref, down_t_ref, *refs):
+    shard_refs, out_refs = refs[: 2 * len(refs) // 3], refs[2 * len(refs) // 3 :]
+    for i in range(0, len(out_refs), 2):
+        plane_rows(
+            experts,
+            expert_ref[0],
+            gate_up_ref,
+            gate_up_t_ref,
+            down_t_ref,
+            jnp.concatenate([ref[...] for ref in shard_refs[2 * i : 2 * i + 4]], axis=0),
+            out_refs[i : i + 2],
+        )
 
 
 def layout_kernel(own_refs, other_refs, joined_ref, turned_ref):
@@ -302,7 +324,16 @@
     gate_one, up_one, down_one = w_gate[0], w_up[0], w_down[0]
     weights = lay_out(gate_one, swapped(gate_one), up_one, swapped(up_one), down_one, swapped(down_one))
 
-    shifted = lambda a, by: lax.ppermute(a, "expert", [(e, (e + 4 * by) % experts) for e in range(experts)])
+    ring = [*range(0, levels, 2), *reversed(range(1, levels, 2))]
+    shifted = lambda a, by: lax.ppermute(
+        a,
+        "expert",
+        [
+            (ring[i] * 4 + j, ring[(i + by) % levels] * 4 + j)
+            for i in range(levels)
+            for j in range(4)
+        ],
+    )
     shards, firsts, seconds, boths = [own], [], [], []
     for level in range(levels):
         firsts.append(to_first(shards[level]))

time: 81.5 us -> 79.3 us (0.973)
  starting transfers between devices: 36.7 us -> 34.7 us
    ppermute x8, waiting for transfers between devices: 5.56 us -> 13.3 us  [dense_plan(): to_first = lambda a: lax.ppermute(a, axes, first_pairs)]
    ppermute x7, waiting for transfers between devices: 15 us -> 7.51 us  [dense_plan(): lax.ppermute(a, 'expert', [(ring[i] * 4 + j, ring[(i + by) % levels] * 4...]
    ppermute x8, starting transfers between devices: 14.1 us -> 11.8 us  [dense_plan(): to_first = lambda a: lax.ppermute(a, axes, first_pairs)]
    ppermute x7, starting transfers between devices: 10.6 us -> 11.5 us  [dense_plan(): lax.ppermute(a, 'expert', [(ring[i] * 4 + j, ring[(i + by) % levels] * 4...]
  transfers between devices with their start and end apart: 30 -> 30, of which waited for: 10 -> 13; matrix products, arithmetic and copies ran while one was open for 0% -> 0% of each run, Pallas kernels for 19% -> 20%
where the time goes in v5:
time: 79.3 us; the launch traced here: 79.2 us
  starting transfers between devices  34.7 us (44%)
  waiting for transfers between devices  24.9 us (31%)
  Pallas kernels  18.3 us (23%)
  between operations  0.82 us (1%)
    ppermute x8, waiting for transfers between devices, dense_plan(): to_first = lambda a: lax.ppermute(a, axes, first_pairs)  13.3 us
    ppermute x8, starting transfers between devices, dense_plan(): to_first = lambda a: lax.ppermute(a, axes, first_pairs)  11.8 us
    ppermute x7, starting transfers between devices, dense_plan(): lax.ppermute(a, 'expert', [(ring[i] * 4 + j, ring[(i + by) % levels] * 4...  11.5 us
    ppermute x11, starting transfers between devices, dense_plan(): to_second = lambda a: lax.ppermute(a, axes, second_pairs)  11.4 us
    pallas_call x3, Pallas kernels, expert_call(): pl.pallas_call(functools.partial(expert_kernel, experts), in_specs=[pl.Bl...  10.4 us
    ppermute x7, waiting for transfers between devices, dense_plan(): lax.ppermute(a, 'expert', [(ring[i] * 4 + j, ring[(i + by) % levels] * 4...  7.51 us
    pallas_call x1, Pallas kernels, lay_out(): pl.pallas_call(lambda a, b, c, d, e, f: layout_kernel((a, c), (b, d), e,...  4.19 us
    ppermute x11, waiting for transfers between devices, dense_plan(): to_second = lambda a: lax.ppermute(a, axes, second_pairs)  2.74 us
  transfers between devices with their start and end apart: 30, of which 13 were waited for; matrix products, arithmetic and copies ran while one was open for 0% of the time, Pallas kernels for 20%

profile of v5, /device:TPU:0, one launch (start us, length us, event | category | flops | bytes accessed | tf_op | source)
XLA Modules:
  0.0 79.2 jit_solution(10724643849019580011)
XLA Ops:
  0.6 1.9 %pack.1.refs_4_ = bf16[32,4224]{1,0:T(8,128)(2,1)} custom-call(s32[1]{0:T(128)} %bitcast.half_ref, bf16[64,2048]{1,0:T(8,128)(2,1)} %tok_ref.1, bf16[64,2048]{1,0:T(8,128)(2,1)} %cot_ref.1, s32[8,64]{1,0:T(8,128)} %bitcast.8, f32[8,64]{1,0:T(8,128)} %bitcast.16), custom_call_target="tpu_custom_call" | custom-call | tf_op jit(solution)/shard_map/pack/pallas_call | solution.py:121
  2.5 4.0 %collective-permute-start = (bf16[32,4224]{1,0:T(8,128)(2,1)}, bf16[32,4224]{1,0:T(8,128)(2,1)S(1)}, u32[]{:S(2)}, u32[]{:S(2)}) collective-permute-start(bf16[32,4224]{1,0:T(8,128)(2,1)} %pack.1.refs_4_), channel_id=1, source_target_pairs={{0,16},{2,18},{4,20},{6,22},{16,24},{18,26},{20,28},{22,30},{24,8}... | collective-permute-start | bytes 811016 | tf_op jit(solution)/shard_map/ppermute | solution.py:328
  6.6 1.5 %collective-permute-start.1 = (bf16[32,4224]{1,0:T(8,128)(2,1)}, bf16[32,4224]{1,0:T(8,128)(2,1)S(1)}, u32[]{:S(2)}, u32[]{:S(2)}) collective-permute-start(bf16[32,4224]{1,0:T(8,128)(2,1)} %pack.1.refs_4_), channel_id=1, source_target_pairs={{0,2},{1,5},{2,0},{3,7},{4,6},{5,1},{6,4},{7,3},{8,10},{9,13},{10,... | collective-permute-start | bytes 811016 | tf_op jit(solution)/shard_map/ppermute | solution.py:319
  8.1 1.5 %collective-permute-start.4 = (bf16[32,4224]{1,0:T(8,128)(2,1)}, bf16[32,4224]{1,0:T(8,128)(2,1)S(1)}, u32[]{:S(2)}, u32[]{:S(2)}) collective-permute-start(bf16[32,4224]{1,0:T(8,128)(2,1)} %pack.1.refs_4_), channel_id=1, source_target_pairs={{0,4},{1,3},{2,6},{3,1},{4,0},{5,7},{6,2},{7,5},{8,12},{9,11},{10,... | collective-permute-start | bytes 811016 | tf_op jit(solution)/shard_map/ppermute | solution.py:320
  9.6 3.0 %collective-permute-done.refs_0_ = bf16[32,4224]{1,0:T(8,128)(2,1)S(1)} collective-permute-done((bf16[32,4224]{1,0:T(8,128)(2,1)}, bf16[32,4224]{1,0:T(8,128)(2,1)S(1)}, u32[]{:S(2)}, u32[]{:S(2)}) %collective-permute-start) | collective-permute-done | bytes 270368 | tf_op jit(solution)/shard_map/ppermute | solution.py:328
  12.6 2.5 %collective-permute-done.1.refs_1_ = bf16[32,4224]{1,0:T(8,128)(2,1)S(1)} collective-permute-done((bf16[32,4224]{1,0:T(8,128)(2,1)}, bf16[32,4224]{1,0:T(8,128)(2,1)S(1)}, u32[]{:S(2)}, u32[]{:S(2)}) %collective-permute-start.1) | collective-permute-done | bytes 270368 | tf_op jit(solution)/shard_map/ppermute | solution.py:319
  15.2 1.6 %collective-permute-start.2 = (bf16[32,4224]{1,0:T(8,128)(2,1)S(1)}, bf16[32,4224]{1,0:T(8,128)(2,1)S(1)}, u32[]{:S(2)}, u32[]{:S(2)}) collective-permute-start(bf16[32,4224]{1,0:T(8,128)(2,1)S(1)} %get-tuple-element.34.refs_0_), channel_id=1, source_target_pairs={{0,16},{2,18},{4,20},{6,22},{16,24},{18,26},{20,28},{22,30},{24,8}... | collective-permute-start | bytes 811016 | tf_op jit(solution)/shard_map/ppermute | solution.py:328
  16.8 2.4 %collective-permute-start.3 = (bf16[32,4224]{1,0:T(8,128)(2,1)S(1)}, bf16[32,4224]{1,0:T(8,128)(2,1)S(1)}, u32[]{:S(2)}, u32[]{:S(2)}) collective-permute-start(bf16[32,4224]{1,0:T(8,128)(2,1)S(1)} %get-tuple-element.34.refs_0_), channel_id=1, source_target_pairs={{0,2},{1,5},{2,0},{3,7},{4,6},{5,1},{6,4},{7,3},{8,10},{9,13},{10,... | collective-permute-start | bytes 811016 | tf_op jit(solution)/shard_map/ppermute | solution.py:319
  19.1 1.5 %collective-permute-start.7 = (bf16[32,4224]{1,0:T(8,128)(2,1)S(1)}, bf16[32,4224]{1,0:T(8,128)(2,1)S(1)}, u32[]{:S(2)}, u32[]{:S(2)}) collective-permute-start(bf16[32,4224]{1,0:T(8,128)(2,1)S(1)} %get-tuple-element.34.refs_0_), channel_id=1, source_target_pairs={{0,4},{1,3},{2,6},{3,1},{4,0},{5,7},{6,2},{7,5},{8,12},{9,11},{10,... | collective-permute-start | bytes 811016 | tf_op jit(solution)/shard_map/ppermute | solution.py:320
  21.7 4.9 %collective-permute-done.3.refs_1_ = bf16[32,4224]{1,0:T(8,128)(2,1)S(1)} collective-permute-done((bf16[32,4224]{1,0:T(8,128)(2,1)S(1)}, bf16[32,4224]{1,0:T(8,128)(2,1)S(1)}, u32[]{:S(2)}, u32[]{:S(2)}) %collective-permute-start.3) | collective-permute-done | bytes 270368 | tf_op jit(solution)/shard_map/ppermute | solution.py:319
  26.9 1.6 %collective-permute-done.8.refs_1_ = bf16[32,4224]{1,0:T(8,128)(2,1)S(1)} collective-permute-done((bf16[32,4224]{1,0:T(8,128)(2,1)S(1)}, bf16[32,4224]{1,0:T(8,128)(2,1)S(1)}, u32[]{:S(2)}, u32[]{:S(2)}) %collective-permute-start.8) | collective-permute-done | bytes 270368 | tf_op jit(solution)/shard_map/ppermute | solution.py:320
  32.0 4.2 %layout.1 = (bf16[2048,1536]{1,0:T(8,128)(2,1)S(1)}, bf16[1536,2048]{1,0:T(8,128)(2,1)S(1)}) custom-call(bf16[2048,384]{1,0:T(8,128)(2,1)S(1)} %bitcast.13, bf16[2048,384]{1,0:T(8,128)(2,1)} %collective-permute-done.9.b, bf16[2048,384]{1,0:T(8,128)(2,1)S(1)} %bitcast.15, bf16[2048,384]{1,0:T(8,128)(2,1)} %collective-permute-done.10.d), custom_call_target="tpu_custom_call" | custom-call | flops 4000000000 | bytes 1 | tf_op jit(solution)/shard_map/layout/pallas_call | solution.py:207
  36.2 1.6 %collective-permute-done.6.refs_1_ = bf16[32,4224]{1,0:T(8,128)(2,1)S(1)} collective-permute-done((bf16[32,4224]{1,0:T(8,128)(2,1)S(1)}, bf16[32,4224]{1,0:T(8,128)(2,1)S(1)}, u32[]{:S(2)}, u32[]{:S(2)}) %collective-permute-start.6) | collective-permute-done | bytes 270368 | tf_op jit(solution)/shard_map/ppermute | solution.py:319
  40.4 1.6 %collective-permute-start.25 = (bf16[32,4224]{1,0:T(8,128)(2,1)S(1)}, bf16[32,4224]{1,0:T(8,128)(2,1)S(1)}, u32[]{:S(2)}, u32[]{:S(2)}) collective-permute-start(bf16[32,4224]{1,0:T(8,128)(2,1)S(1)} %get-tuple-element.47.refs_7_), channel_id=1, source_target_pairs={{0,8},{2,10},{4,12},{6,14},{16,0},{18,2},{20,4},{22,6},{24,16},{26... | collective-permute-start | bytes 811016 | tf_op jit(solution)/shard_map/ppermute | solution.py:328
  42.0 4.8 %expert.3 = (bf16[64,2176]{1,0:T(8,128)(2,1)S(1)}, bf16[64,2176]{1,0:T(8,128)(2,1)S(1)}, bf16[64,2176]{1,0:T(8,128)(2,1)S(1)}, bf16[64,2176]{1,0:T(8,128)(2,1)S(1)}) custom-call(s32[1]{0:T(128)} %bitcast.1.expert_ref, bf16[2048,1536]{1,0:T(8,128)(2,1)S(1)} %get-tuple-element.41.gate_up_ref, bf16[1536,2048]{1,0:T(8,128)(2,1)S(1)} %get-tuple-element.42.gate_up_t_ref, ...), custom_call_target="tpu_custom_call" | custom-call | flops 6000000000 | bytes 1 | tf_op jit(solution)/shard_map/expert/pallas_call | solution.py:236
  48.9 2.8 %expert.4 = (bf16[64,2176]{1,0:T(8,128)(2,1)S(1)}, bf16[64,2176]{1,0:T(8,128)(2,1)S(1)}) custom-call(s32[1]{0:T(128)} %bitcast.1.expert_ref, bf16[2048,1536]{1,0:T(8,128)(2,1)S(1)} %get-tuple-element.41.gate_up_ref, bf16[1536,2048]{1,0:T(8,128)(2,1)S(1)} %get-tuple-element.42.gate_up_t_ref, bf16[2048,768]{1,0:T(8,128)(2,1)S(1)} %get-tuple-element.43.down_t_ref, ...), custom_call_target="tpu_custom_call" | custom-call | flops 6000000000 | bytes 1 | tf_op jit(solution)/shard_map/expert/pallas_call | solution.py:236
  52.6 2.8 %expert.5 = (bf16[64,2176]{1,0:T(8,128)(2,1)S(1)}, bf16[64,2176]{1,0:T(8,128)(2,1)S(1)}) custom-call(s32[1]{0:T(128)} %bitcast.1.expert_ref, bf16[2048,1536]{1,0:T(8,128)(2,1)S(1)} %get-tuple-element.41.gate_up_ref, bf16[1536,2048]{1,0:T(8,128)(2,1)S(1)} %get-tuple-element.42.gate_up_t_ref, bf16[2048,768]{1,0:T(8,128)(2,1)S(1)} %get-tuple-element.43.down_t_ref, ...), custom_call_target="tpu_custom_call" | custom-call | flops 6000000000 | bytes 1 | tf_op jit(solution)/shard_map/expert/pallas_call | solution.py:236
  56.8 2.0 %collective-permute-start.14 = (bf16[32,2176]{1,0:T(8,128)(2,1)S(1)}, bf16[32,2176]{1,0:T(8,128)(2,1)S(1)}, u32[]{:S(2)}, u32[]{:S(2)}) collective-permute-start(bf16[32,2176]{1,0:T(8,128)(2,1)S(1)} %add_convert_fusion.7), channel_id=1, source_target_pairs={{0,2},{1,5},{2,0},{3,7},{4,6},{5,1},{6,4},{7,3},{8,10},{9,13},{10,... | collective-permute-start | bytes 417800 | tf_op jit(solution)/shard_map/ppermute | solution.py:319
  59.4 2.2 %collective-permute-start.21 = (bf16[32,2176]{1,0:T(8,128)(2,1)S(1)}, bf16[32,2176]{1,0:T(8,128)(2,1)S(1)}, u32[]{:S(2)}, u32[]{:S(2)}) collective-permute-start(bf16[32,2176]{1,0:T(8,128)(2,1)S(1)} %add_convert_fusion.6.refs_2_), channel_id=1, source_target_pairs={{0,2},{1,5},{2,0},{3,7},{4,6},{5,1},{6,4},{7,3},{8,10},{9,13},{10,... | collective-permute-start | bytes 417800 | tf_op jit(solution)/shard_map/ppermute | solution.py:319
  64.1 1.6 %collective-permute-start.20 = (bf16[32,2176]{1,0:T(8,128)(2,1)S(1)}, bf16[32,2176]{1,0:T(8,128)(2,1)S(1)}, u32[]{:S(2)}, u32[]{:S(2)}) collective-permute-start(bf16[32,2176]{1,0:T(8,128)(2,1)S(1)} %add_convert_fusion.4), channel_id=1, source_target_pairs={{0,2},{1,5},{2,0},{3,7},{4,6},{5,1},{6,4},{7,3},{8,10},{9,13},{10,... | collective-permute-start | bytes 417800 | tf_op jit(solution)/shard_map/ppermute | solution.py:319
  67.8 3.0 %collective-permute-done.27 = bf16[32,2176]{1,0:T(8,128)(2,1)S(1)} collective-permute-done((bf16[32,2176]{1,0:T(8,128)(2,1)S(1)}, bf16[32,2176]{1,0:T(8,128)(2,1)S(1)}, u32[]{:S(2)}, u32[]{:S(2)}) %collective-permute-start.27) | collective-permute-done | bytes 139296 | tf_op jit(solution)/shard_map/ppermute | solution.py:319
  70.9 1.8 %collective-permute-start.28 = (bf16[32,2176]{1,0:T(8,128)(2,1)S(1)}, bf16[32,2176]{1,0:T(8,128)(2,1)S(1)}, u32[]{:S(2)}, u32[]{:S(2)}) collective-permute-start(bf16[32,2176]{1,0:T(8,128)(2,1)S(1)} %add_convert_fusion.1), channel_id=1, source_target_pairs={{0,16},{2,18},{4,20},{6,22},{16,24},{18,26},{20,28},{22,30},{24,8}... | collective-permute-start | bytes 417800 | tf_op jit(solution)/shard_map/ppermute | solution.py:328
  72.7 1.8 %collective-permute-done.22 = bf16[32,2176]{1,0:T(8,128)(2,1)S(1)} collective-permute-done((bf16[32,2176]{1,0:T(8,128)(2,1)S(1)}, bf16[32,2176]{1,0:T(8,128)(2,1)S(1)}, u32[]{:S(2)}, u32[]{:S(2)}) %collective-permute-start.22) | collective-permute-done | bytes 139296 | tf_op jit(solution)/shard_map/ppermute | solution.py:328
  74.5 2.1 %collective-permute-done.28 = bf16[32,2176]{1,0:T(8,128)(2,1)S(1)} collective-permute-done((bf16[32,2176]{1,0:T(8,128)(2,1)S(1)}, bf16[32,2176]{1,0:T(8,128)(2,1)S(1)}, u32[]{:S(2)}, u32[]{:S(2)}) %collective-permute-start.28) | collective-permute-done | bytes 139296 | tf_op jit(solution)/shard_map/ppermute | solution.py:328
  (68 shorter events, 19.5 us)
Async XLA Ops:
  2.5 10.1 %collective-permute-start = (bf16[32,4224]{1,0:T(8,128)(2,1)}, bf16[32,4224]{1,0:T(8,128)(2,1)S(1)}, u32[]{:S(2)}, u32[]{:S(2)}) collective-permute-start(bf16[32,4224]{1,0:T(8,128)(2,1)} %pack.1.refs_4_), channel_id=1, source_target_pairs={{0,16},{2,18},{4,20},{6,22},{16,24},{18,26},{20,28},{22,30},{24,8}... | collective-permute-start | bytes 811016 | tf_op jit(solution)/shard_map/ppermute | solution.py:328
  6.6 8.6 %collective-permute-start.1 = (bf16[32,4224]{1,0:T(8,128)(2,1)}, bf16[32,4224]{1,0:T(8,128)(2,1)S(1)}, u32[]{:S(2)}, u32[]{:S(2)}) collective-permute-start(bf16[32,4224]{1,0:T(8,128)(2,1)} %pack.1.refs_4_), channel_id=1, source_target_pairs={{0,2},{1,5},{2,0},{3,7},{4,6},{5,1},{6,4},{7,3},{8,10},{9,13},{10,... | collective-permute-start | bytes 811016 | tf_op jit(solution)/shard_map/ppermute | solution.py:319
  8.1 20.9 %collective-permute-start.11 = (bf16[384,2048]{1,0:T(8,128)(2,1)}, bf16[384,2048]{1,0:T(8,128)(2,1)S(1)}, u32[]{:S(2)}, u32[]{:S(2)}) collective-permute-start(bf16[384,2048]{1,0:T(8,128)(2,1)} %bitcast.10), channel_id=1, source_target_pairs={{0,1},{1,0},{2,3},{3,2},{4,5},{5,4},{6,7},{7,6},{8,9},{9,8},{10,11... | collective-permute-start | bytes 4718600 | tf_op jit(solution)/shard_map/ppermute | solution.py:321
  8.1 12.6 %collective-permute-start.4 = (bf16[32,4224]{1,0:T(8,128)(2,1)}, bf16[32,4224]{1,0:T(8,128)(2,1)S(1)}, u32[]{:S(2)}, u32[]{:S(2)}) collective-permute-start(bf16[32,4224]{1,0:T(8,128)(2,1)} %pack.1.refs_4_), channel_id=1, source_target_pairs={{0,4},{1,3},{2,6},{3,1},{4,0},{5,7},{6,2},{7,5},{8,12},{9,11},{10,... | collective-permute-start | bytes 811016 | tf_op jit(solution)/shard_map/ppermute | solution.py:320
  16.8 9.8 %collective-permute-start.3 = (bf16[32,4224]{1,0:T(8,128)(2,1)S(1)}, bf16[32,4224]{1,0:T(8,128)(2,1)S(1)}, u32[]{:S(2)}, u32[]{:S(2)}) collective-permute-start(bf16[32,4224]{1,0:T(8,128)(2,1)S(1)} %get-tuple-element.34.refs_0_), channel_id=1, source_target_pairs={{0,2},{1,5},{2,0},{3,7},{4,6},{5,1},{6,4},{7,3},{8,10},{9,13},{10,... | collective-permute-start | bytes 811016 | tf_op jit(solution)/shard_map/ppermute | solution.py:319
  19.1 7.4 %collective-permute-start.7 = (bf16[32,4224]{1,0:T(8,128)(2,1)S(1)}, bf16[32,4224]{1,0:T(8,128)(2,1)S(1)}, u32[]{:S(2)}, u32[]{:S(2)}) collective-permute-start(bf16[32,4224]{1,0:T(8,128)(2,1)S(1)} %get-tuple-element.34.refs_0_), channel_id=1, source_target_pairs={{0,4},{1,3},{2,6},{3,1},{4,0},{5,7},{6,2},{7,5},{8,12},{9,11},{10,... | collective-permute-start | bytes 811016 | tf_op jit(solution)/shard_map/ppermute | solution.py:320
  20.7 7.8 %collective-permute-start.8 = (bf16[32,4224]{1,0:T(8,128)(2,1)S(1)}, bf16[32,4224]{1,0:T(8,128)(2,1)S(1)}, u32[]{:S(2)}, u32[]{:S(2)}) collective-permute-start(bf16[32,4224]{1,0:T(8,128)(2,1)S(1)} %get-tuple-element.36.refs_5_), channel_id=1, source_target_pairs={{0,4},{1,3},{2,6},{3,1},{4,0},{5,7},{6,2},{7,5},{8,12},{9,11},{10,... | collective-permute-start | bytes 811016 | tf_op jit(solution)/shard_map/ppermute | solution.py:320
  21.6 9.3 %collective-permute-start.10 = (bf16[2048,384]{1,0:T(8,128)(2,1)}, bf16[2048,384]{1,0:T(8,128)(2,1)}, u32[]{:S(2)}, u32[]{:S(2)}) collective-permute-start(bf16[2048,384]{1,0:T(8,128)(2,1)} %bitcast.14), channel_id=1, source_target_pairs={{0,1},{1,0},{2,3},{3,2},{4,5},{5,4},{6,7},{7,6},{8,9},{9,8},{10,11... | collective-permute-start | bytes 4718600 | tf_op jit(solution)/shard_map/ppermute | solution.py:321
  26.6 9.7 %collective-permute-start.5 = (bf16[32,4224]{1,0:T(8,128)(2,1)S(1)}, bf16[32,4224]{1,0:T(8,128)(2,1)S(1)}, u32[]{:S(2)}, u32[]{:S(2)}) collective-permute-start(bf16[32,4224]{1,0:T(8,128)(2,1)S(1)} %get-tuple-element.35.refs_1_), channel_id=1, source_target_pairs={{0,16},{2,18},{4,20},{6,22},{16,24},{18,26},{20,28},{22,30},{24,8}... | collective-permute-start | bytes 811016 | tf_op jit(solution)/shard_map/ppermute | solution.py:328
  28.5 9.4 %collective-permute-start.6 = (bf16[32,4224]{1,0:T(8,128)(2,1)S(1)}, bf16[32,4224]{1,0:T(8,128)(2,1)S(1)}, u32[]{:S(2)}, u32[]{:S(2)}) collective-permute-start(bf16[32,4224]{1,0:T(8,128)(2,1)S(1)} %get-tuple-element.35.refs_1_), channel_id=1, source_target_pairs={{0,2},{1,5},{2,0},{3,7},{4,6},{5,1},{6,4},{7,3},{8,10},{9,13},{10,... | collective-permute-start | bytes 811016 | tf_op jit(solution)/shard_map/ppermute | solution.py:319
  29.0 17.8 %collective-permute-start.16 = (bf16[32,4224]{1,0:T(8,128)(2,1)S(1)}, bf16[32,4224]{1,0:T(8,128)(2,1)S(1)}, u32[]{:S(2)}, u32[]{:S(2)}) collective-permute-start(bf16[32,4224]{1,0:T(8,128)(2,1)S(1)} %get-tuple-element.35.refs_1_), channel_id=1, source_target_pairs={{0,4},{1,3},{2,6},{3,1},{4,0},{5,7},{6,2},{7,5},{8,12},{9,11},{10,... | collective-permute-start | bytes 811016 | tf_op jit(solution)/shard_map/ppermute | solution.py:320
  31.0 9.4 %collective-permute-start.12 = (bf16[32,4224]{1,0:T(8,128)(2,1)S(1)}, bf16[32,4224]{1,0:T(8,128)(2,1)S(1)}, u32[]{:S(2)}, u32[]{:S(2)}) collective-permute-start(bf16[32,4224]{1,0:T(8,128)(2,1)S(1)} %get-tuple-element.44.refs_1_), channel_id=1, source_target_pairs={{0,4},{1,3},{2,6},{3,1},{4,0},{5,7},{6,2},{7,5},{8,12},{9,11},{10,... | collective-permute-start | bytes 811016 | tf_op jit(solution)/shard_map/ppermute | solution.py:320
  37.9 13.8 %collective-permute-start.23 = (bf16[32,4224]{1,0:T(8,128)(2,1)S(1)}, bf16[32,4224]{1,0:T(8,128)(2,1)S(1)}, u32[]{:S(2)}, u32[]{:S(2)}) collective-permute-start(bf16[32,4224]{1,0:T(8,128)(2,1)S(1)} %get-tuple-element.56.refs_1_), channel_id=1, source_target_pairs={{0,2},{1,5},{2,0},{3,7},{4,6},{5,1},{6,4},{7,3},{8,10},{9,13},{10,... | collective-permute-start | bytes 811016 | tf_op jit(solution)/shard_map/ppermute | solution.py:319
  38.3 13.4 %collective-permute-start.24 = (bf16[32,4224]{1,0:T(8,128)(2,1)S(1)}, bf16[32,4224]{1,0:T(8,128)(2,1)S(1)}, u32[]{:S(2)}, u32[]{:S(2)}) collective-permute-start(bf16[32,4224]{1,0:T(8,128)(2,1)S(1)} %get-tuple-element.56.refs_1_), channel_id=1, source_target_pairs={{0,4},{1,3},{2,6},{3,1},{4,0},{5,7},{6,2},{7,5},{8,12},{9,11},{10,... | collective-permute-start | bytes 811016 | tf_op jit(solution)/shard_map/ppermute | solution.py:320
  39.4 8.2 %collective-permute-start.17 = (bf16[32,4224]{1,0:T(8,128)(2,1)S(1)}, bf16[32,4224]{1,0:T(8,128)(2,1)S(1)}, u32[]{:S(2)}, u32[]{:S(2)}) collective-permute-start(bf16[32,4224]{1,0:T(8,128)(2,1)S(1)} %get-tuple-element.53.refs_1_), channel_id=1, source_target_pairs={{0,4},{1,3},{2,6},{3,1},{4,0},{5,7},{6,2},{7,5},{8,12},{9,11},{10,... | collective-permute-start | bytes 811016 | tf_op jit(solution)/shard_map/ppermute | solution.py:320
  40.4 12.2 %collective-permute-start.25 = (bf16[32,4224]{1,0:T(8,128)(2,1)S(1)}, bf16[32,4224]{1,0:T(8,128)(2,1)S(1)}, u32[]{:S(2)}, u32[]{:S(2)}) collective-permute-start(bf16[32,4224]{1,0:T(8,128)(2,1)S(1)} %get-tuple-element.47.refs_7_), channel_id=1, source_target_pairs={{0,8},{2,10},{4,12},{6,14},{16,0},{18,2},{20,4},{22,6},{24,16},{26... | collective-permute-start | bytes 811016 | tf_op jit(solution)/shard_map/ppermute | solution.py:328
  46.8 9.9 %collective-permute-start.13 = (bf16[64,2176]{1,0:T(8,128)(2,1)S(1)}, bf16[64,2176]{1,0:T(8,128)(2,1)S(1)}, u32[]{:S(2)}, u32[]{:S(2)}) collective-permute-start(bf16[64,2176]{1,0:T(8,128)(2,1)S(1)} %get-tuple-element.50), channel_id=1, source_target_pairs={{0,4},{1,3},{2,6},{3,1},{4,0},{5,7},{6,2},{7,5},{8,12},{9,11},{10,... | collective-permute-start | bytes 835592 | tf_op jit(solution)/shard_map/ppermute | solution.py:320
  47.7 13.9 %collective-permute-start.15 = (bf16[64,2176]{1,0:T(8,128)(2,1)S(1)}, bf16[64,2176]{1,0:T(8,128)(2,1)S(1)}, u32[]{:S(2)}, u32[]{:S(2)}) collective-permute-start(bf16[64,2176]{1,0:T(8,128)(2,1)S(1)} %get-tuple-element.51), channel_id=1, source_target_pairs={{0,4},{1,3},{2,6},{3,1},{4,0},{5,7},{6,2},{7,5},{8,12},{9,11},{10,... | collective-permute-start | bytes 835592 | tf_op jit(solution)/shard_map/ppermute | solution.py:320
  51.7 7.7 %collective-permute-start.18 = (bf16[64,2176]{1,0:T(8,128)(2,1)S(1)}, bf16[64,2176]{1,0:T(8,128)(2,1)S(1)}, u32[]{:S(2)}, u32[]{:S(2)}) collective-permute-start(bf16[64,2176]{1,0:T(8,128)(2,1)S(1)} %get-tuple-element.57), channel_id=1, source_target_pairs={{0,4},{1,3},{2,6},{3,1},{4,0},{5,7},{6,2},{7,5},{8,12},{9,11},{10,... | collective-permute-start | bytes 835592 | tf_op jit(solution)/shard_map/ppermute | solution.py:320
  55.5 10.2 %collective-permute-start.26 = (bf16[64,2176]{1,0:T(8,128)(2,1)S(1)}, bf16[64,2176]{1,0:T(8,128)(2,1)S(1)}, u32[]{:S(2)}, u32[]{:S(2)}) collective-permute-start(bf16[64,2176]{1,0:T(8,128)(2,1)S(1)} %get-tuple-element.63), channel_id=1, source_target_pairs={{0,4},{1,3},{2,6},{3,1},{4,0},{5,7},{6,2},{7,5},{8,12},{9,11},{10,... | collective-permute-start | bytes 835592 | tf_op jit(solution)/shard_map/ppermute | solution.py:320
  59.4 7.5 %collective-permute-start.21 = (bf16[32,2176]{1,0:T(8,128)(2,1)S(1)}, bf16[32,2176]{1,0:T(8,128)(2,1)S(1)}, u32[]{:S(2)}, u32[]{:S(2)}) collective-permute-start(bf16[32,2176]{1,0:T(8,128)(2,1)S(1)} %add_convert_fusion.6.refs_2_), channel_id=1, source_target_pairs={{0,2},{1,5},{2,0},{3,7},{4,6},{5,1},{6,4},{7,3},{8,10},{9,13},{10,... | collective-permute-start | bytes 417800 | tf_op jit(solution)/shard_map/ppermute | solution.py:319
  62.8 9.9 %collective-permute-start.19 = (bf16[32,2176]{1,0:T(8,128)(2,1)S(1)}, bf16[32,2176]{1,0:T(8,128)(2,1)S(1)}, u32[]{:S(2)}, u32[]{:S(2)}) collective-permute-start(bf16[32,2176]{1,0:T(8,128)(2,1)S(1)} %add_convert_fusion.5), channel_id=1, source_target_pairs={{0,8},{2,10},{4,12},{6,14},{16,0},{18,2},{20,4},{22,6},{24,16},{26... | collective-permute-start | bytes 417800 | tf_op jit(solution)/shard_map/ppermute | solution.py:328
  64.1 8.6 %collective-permute-start.20 = (bf16[32,2176]{1,0:T(8,128)(2,1)S(1)}, bf16[32,2176]{1,0:T(8,128)(2,1)S(1)}, u32[]{:S(2)}, u32[]{:S(2)}) collective-permute-start(bf16[32,2176]{1,0:T(8,128)(2,1)S(1)} %add_convert_fusion.4), channel_id=1, source_target_pairs={{0,2},{1,5},{2,0},{3,7},{4,6},{5,1},{6,4},{7,3},{8,10},{9,13},{10,... | collective-permute-start | bytes 417800 | tf_op jit(solution)/shard_map/ppermute | solution.py:319
  67.0 7.6 %collective-permute-start.22 = (bf16[32,2176]{1,0:T(8,128)(2,1)S(1)}, bf16[32,2176]{1,0:T(8,128)(2,1)S(1)}, u32[]{:S(2)}, u32[]{:S(2)}) collective-permute-start(bf16[32,2176]{1,0:T(8,128)(2,1)S(1)} %add_convert_fusion.3), channel_id=1, source_target_pairs={{0,24},{2,26},{4,28},{6,30},{16,8},{18,10},{20,12},{22,14},{24,0},... | collective-permute-start | bytes 417800 | tf_op jit(solution)/shard_map/ppermute | solution.py:328
  (11 other events, 66.9 us)

commit v6 on v5

--- a/solution.py
+++ b/solution.py
@@ -361,7 +361,7 @@
         boths.append(to_second(firsts[level]))
 
     total, results, previous = [], {}, None
-    for batch in [(1, 0)] + [(level,) for level in range(2, levels)]:
+    for batch in [(1,), (0,)] + [(level,) for level in range(2, levels)]:
         planes = [[shards[i], firsts[i], seconds[i], boths[i]] for i in batch]
         if previous is not None:
             results[previous][1], planes[0][0] = tie(results[previous][1], planes[0][0])

time: 79.3 us -> 80.3 us (1.013)
  starting transfers between devices: 34.7 us -> 37.7 us
  waiting for transfers between devices: 24.9 us -> 22.3 us
    ppermute x8, waiting for transfers between devices: 13.3 us -> 10.5 us  [dense_plan(): to_first = lambda a: lax.ppermute(a, axes, first_pairs)]
    ppermute x11, starting transfers between devices: 11.4 us -> 12.8 us  [dense_plan(): to_second = lambda a: lax.ppermute(a, axes, second_pairs)]
    ppermute x8, starting transfers between devices: 11.8 us -> 13.1 us  [dense_plan(): to_first = lambda a: lax.ppermute(a, axes, first_pairs)]
    pallas_call x3 -> x4, Pallas kernels: 10.4 us -> 11 us  [expert_call(): pl.pallas_call(functools.partial(expert_kernel, experts), in_specs=[pl.Bl...]
  transfers between devices with their start and end apart: 30 -> 30, of which waited for: 13 -> 12; matrix products, arithmetic and copies ran while one was open for 0% -> 0% of each run, Pallas kernels for 20% -> 20%
where the time goes in v6:
time: 80.3 us; the launch traced here: 80.2 us
  starting transfers between devices  37.7 us (47%)
  waiting for transfers between devices  22.3 us (28%)
  Pallas kernels  18.9 us (24%)
  between operations  0.83 us (1%)
    ppermute x8, starting transfers between devices, dense_plan(): to_first = lambda a: lax.ppermute(a, axes, first_pairs)  13.1 us
    ppermute x11, starting transfers between devices, dense_plan(): to_second = lambda a: lax.ppermute(a, axes, second_pairs)  12.8 us
    ppermute x7, starting transfers between devices, dense_plan(): lax.ppermute(a, 'expert', [(ring[i] * 4 + j, ring[(i + by) % levels] * 4...  11.6 us
    pallas_call x4, Pallas kernels, expert_call(): pl.pallas_call(functools.partial(expert_kernel, experts), in_specs=[pl.Bl...  11 us
    ppermute x8, waiting for transfers between devices, dense_plan(): to_first = lambda a: lax.ppermute(a, axes, first_pairs)  10.5 us
    ppermute x7, waiting for transfers between devices, dense_plan(): lax.ppermute(a, 'expert', [(ring[i] * 4 + j, ring[(i + by) % levels] * 4...  7.4 us
    pallas_call x1, Pallas kernels, lay_out(): pl.pallas_call(lambda a, b, c, d, e, f: layout_kernel((a, c), (b, d), e,...  4.19 us
    ppermute x11, waiting for transfers between devices, dense_plan(): to_second = lambda a: lax.ppermute(a, axes, second_pairs)  3.06 us
  transfers between devices with their start and end apart: 30, of which 12 were waited for; matrix products, arithmetic and copies ran while one was open for 0% of the time, Pallas kernels for 20%

profile of v6, /device:TPU:0, one launch (start us, length us, event | category | flops | bytes accessed | tf_op | source)
XLA Modules:
  0.0 80.2 jit_solution(8394662778625186428)
XLA Ops:
  0.6 1.9 %pack.1.refs_1_ = bf16[32,4224]{1,0:T(8,128)(2,1)} custom-call(s32[1]{0:T(128)} %bitcast.half_ref, bf16[64,2048]{1,0:T(8,128)(2,1)} %tok_ref.1, bf16[64,2048]{1,0:T(8,128)(2,1)} %cot_ref.1, s32[8,64]{1,0:T(8,128)} %bitcast.8, f32[8,64]{1,0:T(8,128)} %bitcast.16), custom_call_target="tpu_custom_call" | custom-call | tf_op jit(solution)/shard_map/pack/pallas_call | solution.py:121
  2.5 4.0 %collective-permute-start = (bf16[32,4224]{1,0:T(8,128)(2,1)}, bf16[32,4224]{1,0:T(8,128)(2,1)S(1)}, u32[]{:S(2)}, u32[]{:S(2)}) collective-permute-start(bf16[32,4224]{1,0:T(8,128)(2,1)} %pack.1.refs_1_), channel_id=1, source_target_pairs={{0,16},{2,18},{4,20},{6,22},{16,24},{18,26},{20,28},{22,30},{24,8}... | collective-permute-start | bytes 811016 | tf_op jit(solution)/shard_map/ppermute | solution.py:328
  6.6 1.5 %collective-permute-start.1 = (bf16[32,4224]{1,0:T(8,128)(2,1)}, bf16[32,4224]{1,0:T(8,128)(2,1)S(1)}, u32[]{:S(2)}, u32[]{:S(2)}) collective-permute-start(bf16[32,4224]{1,0:T(8,128)(2,1)} %pack.1.refs_1_), channel_id=1, source_target_pairs={{0,2},{1,5},{2,0},{3,7},{4,6},{5,1},{6,4},{7,3},{8,10},{9,13},{10,... | collective-permute-start | bytes 811016 | tf_op jit(solution)/shard_map/ppermute | solution.py:319
  8.0 1.5 %collective-permute-start.4 = (bf16[32,4224]{1,0:T(8,128)(2,1)}, bf16[32,4224]{1,0:T(8,128)(2,1)S(1)}, u32[]{:S(2)}, u32[]{:S(2)}) collective-permute-start(bf16[32,4224]{1,0:T(8,128)(2,1)} %pack.1.refs_1_), channel_id=1, source_target_pairs={{0,4},{1,3},{2,6},{3,1},{4,0},{5,7},{6,2},{7,5},{8,12},{9,11},{10,... | collective-permute-start | bytes 811016 | tf_op jit(solution)/shard_map/ppermute | solution.py:320
  9.6 3.0 %collective-permute-done.refs_0_ = bf16[32,4224]{1,0:T(8,128)(2,1)S(1)} collective-permute-done((bf16[32,4224]{1,0:T(8,128)(2,1)}, bf16[32,4224]{1,0:T(8,128)(2,1)S(1)}, u32[]{:S(2)}, u32[]{:S(2)}) %collective-permute-start) | collective-permute-done | bytes 270368 | tf_op jit(solution)/shard_map/ppermute | solution.py:328
  12.6 2.5 %collective-permute-done.1.refs_1_ = bf16[32,4224]{1,0:T(8,128)(2,1)S(1)} collective-permute-done((bf16[32,4224]{1,0:T(8,128)(2,1)}, bf16[32,4224]{1,0:T(8,128)(2,1)S(1)}, u32[]{:S(2)}, u32[]{:S(2)}) %collective-permute-start.1) | collective-permute-done | bytes 270368 | tf_op jit(solution)/shard_map/ppermute | solution.py:319
  15.2 1.6 %collective-permute-start.2 = (bf16[32,4224]{1,0:T(8,128)(2,1)S(1)}, bf16[32,4224]{1,0:T(8,128)(2,1)S(1)}, u32[]{:S(2)}, u32[]{:S(2)}) collective-permute-start(bf16[32,4224]{1,0:T(8,128)(2,1)S(1)} %get-tuple-element.36.refs_0_), channel_id=1, source_target_pairs={{0,16},{2,18},{4,20},{6,22},{16,24},{18,26},{20,28},{22,30},{24,8}... | collective-permute-start | bytes 811016 | tf_op jit(solution)/shard_map/ppermute | solution.py:328
  16.7 2.4 %collective-permute-start.3 = (bf16[32,4224]{1,0:T(8,128)(2,1)S(1)}, bf16[32,4224]{1,0:T(8,128)(2,1)S(1)}, u32[]{:S(2)}, u32[]{:S(2)}) collective-permute-start(bf16[32,4224]{1,0:T(8,128)(2,1)S(1)} %get-tuple-element.36.refs_0_), channel_id=1, source_target_pairs={{0,2},{1,5},{2,0},{3,7},{4,6},{5,1},{6,4},{7,3},{8,10},{9,13},{10,... | collective-permute-start | bytes 811016 | tf_op jit(solution)/shard_map/ppermute | solution.py:319
  19.1 1.5 %collective-permute-start.7 = (bf16[32,4224]{1,0:T(8,128)(2,1)S(1)}, bf16[32,4224]{1,0:T(8,128)(2,1)S(1)}, u32[]{:S(2)}, u32[]{:S(2)}) collective-permute-start(bf16[32,4224]{1,0:T(8,128)(2,1)S(1)} %get-tuple-element.36.refs_0_), channel_id=1, source_target_pairs={{0,4},{1,3},{2,6},{3,1},{4,0},{5,7},{6,2},{7,5},{8,12},{9,11},{10,... | collective-permute-start | bytes 811016 | tf_op jit(solution)/shard_map/ppermute | solution.py:320
  21.6 4.9 %collective-permute-done.3.refs_1_ = bf16[32,4224]{1,0:T(8,128)(2,1)S(1)} collective-permute-done((bf16[32,4224]{1,0:T(8,128)(2,1)S(1)}, bf16[32,4224]{1,0:T(8,128)(2,1)S(1)}, u32[]{:S(2)}, u32[]{:S(2)}) %collective-permute-start.3) | collective-permute-done | bytes 270368 | tf_op jit(solution)/shard_map/ppermute | solution.py:319
  26.9 1.6 %collective-permute-done.8.refs_1_ = bf16[32,4224]{1,0:T(8,128)(2,1)S(1)} collective-permute-done((bf16[32,4224]{1,0:T(8,128)(2,1)S(1)}, bf16[32,4224]{1,0:T(8,128)(2,1)S(1)}, u32[]{:S(2)}, u32[]{:S(2)}) %collective-permute-start.8) | collective-permute-done | bytes 270368 | tf_op jit(solution)/shard_map/ppermute | solution.py:320
  32.0 4.2 %layout.1 = (bf16[2048,1536]{1,0:T(8,128)(2,1)S(1)}, bf16[1536,2048]{1,0:T(8,128)(2,1)S(1)}) custom-call(bf16[2048,384]{1,0:T(8,128)(2,1)S(1)} %bitcast.13, bf16[2048,384]{1,0:T(8,128)(2,1)} %collective-permute-done.9.b, bf16[2048,384]{1,0:T(8,128)(2,1)S(1)} %bitcast.15, bf16[2048,384]{1,0:T(8,128)(2,1)} %collective-permute-done.10.d), custom_call_target="tpu_custom_call" | custom-call | flops 4000000000 | bytes 1 | tf_op jit(solution)/shard_map/layout/pallas_call | solution.py:207
  36.2 1.6 %collective-permute-done.6.refs_1_ = bf16[32,4224]{1,0:T(8,128)(2,1)S(1)} collective-permute-done((bf16[32,4224]{1,0:T(8,128)(2,1)S(1)}, bf16[32,4224]{1,0:T(8,128)(2,1)S(1)}, u32[]{:S(2)}, u32[]{:S(2)}) %collective-permute-start.6) | collective-permute-done | bytes 270368 | tf_op jit(solution)/shard_map/ppermute | solution.py:319
  39.4 2.7 %expert.4 = (bf16[64,2176]{1,0:T(8,128)(2,1)S(1)}, bf16[64,2176]{1,0:T(8,128)(2,1)S(1)}) custom-call(s32[1]{0:T(128)} %bitcast.1.expert_ref, bf16[2048,1536]{1,0:T(8,128)(2,1)S(1)} %get-tuple-element.43.gate_up_ref, bf16[1536,2048]{1,0:T(8,128)(2,1)S(1)} %get-tuple-element.44.gate_up_t_ref, bf16[2048,768]{1,0:T(8,128)(2,1)S(1)} %get-tuple-element.45.down_t_ref, ...), custom_call_target="tpu_custom_call" | custom-call | flops 6000000000 | bytes 1 | tf_op jit(solution)/shard_map/expert/pallas_call | solution.py:236
  42.2 1.4 %collective-permute-start.17 = (bf16[32,4224]{1,0:T(8,128)(2,1)S(1)}, bf16[32,4224]{1,0:T(8,128)(2,1)S(1)}, u32[]{:S(2)}, u32[]{:S(2)}) collective-permute-start(bf16[32,4224]{1,0:T(8,128)(2,1)S(1)} %get-tuple-element.57.refs_1_), channel_id=1, source_target_pairs={{0,4},{1,3},{2,6},{3,1},{4,0},{5,7},{6,2},{7,5},{8,12},{9,11},{10,... | collective-permute-start | bytes 811016 | tf_op jit(solution)/shard_map/ppermute | solution.py:320
  44.9 2.8 %expert.5 = (bf16[64,2176]{1,0:T(8,128)(2,1)S(1)}, bf16[64,2176]{1,0:T(8,128)(2,1)S(1)}) custom-call(s32[1]{0:T(128)} %bitcast.1.expert_ref, bf16[2048,1536]{1,0:T(8,128)(2,1)S(1)} %get-tuple-element.43.gate_up_ref, bf16[1536,2048]{1,0:T(8,128)(2,1)S(1)} %get-tuple-element.44.gate_up_t_ref, bf16[2048,768]{1,0:T(8,128)(2,1)S(1)} %get-tuple-element.45.down_t_ref, ...), custom_call_target="tpu_custom_call" | custom-call | flops 6000000000 | bytes 1 | tf_op jit(solution)/shard_map/expert/pallas_call | solution.py:236
  50.1 2.7 %expert.6 = (bf16[64,2176]{1,0:T(8,128)(2,1)S(1)}, bf16[64,2176]{1,0:T(8,128)(2,1)S(1)}) custom-call(s32[1]{0:T(128)} %bitcast.1.expert_ref, bf16[2048,1536]{1,0:T(8,128)(2,1)S(1)} %get-tuple-element.43.gate_up_ref, bf16[1536,2048]{1,0:T(8,128)(2,1)S(1)} %get-tuple-element.44.gate_up_t_ref, bf16[2048,768]{1,0:T(8,128)(2,1)S(1)} %get-tuple-element.45.down_t_ref, ...), custom_call_target="tpu_custom_call" | custom-call | flops 6000000000 | bytes 1 | tf_op jit(solution)/shard_map/expert/pallas_call | solution.py:236
  53.6 2.8 %expert.7 = (bf16[64,2176]{1,0:T(8,128)(2,1)S(1)}, bf16[64,2176]{1,0:T(8,128)(2,1)S(1)}) custom-call(s32[1]{0:T(128)} %bitcast.1.expert_ref, bf16[2048,1536]{1,0:T(8,128)(2,1)S(1)} %get-tuple-element.43.gate_up_ref, bf16[1536,2048]{1,0:T(8,128)(2,1)S(1)} %get-tuple-element.44.gate_up_t_ref, bf16[2048,768]{1,0:T(8,128)(2,1)S(1)} %get-tuple-element.45.down_t_ref, ...), custom_call_target="tpu_custom_call" | custom-call | flops 6000000000 | bytes 1 | tf_op jit(solution)/shard_map/expert/pallas_call | solution.py:236
  57.9 1.8 %collective-permute-start.14 = (bf16[32,2176]{1,0:T(8,128)(2,1)S(1)}, bf16[32,2176]{1,0:T(8,128)(2,1)S(1)}, u32[]{:S(2)}, u32[]{:S(2)}) collective-permute-start(bf16[32,2176]{1,0:T(8,128)(2,1)S(1)} %add_convert_fusion.7), channel_id=1, source_target_pairs={{0,2},{1,5},{2,0},{3,7},{4,6},{5,1},{6,4},{7,3},{8,10},{9,13},{10,... | collective-permute-start | bytes 417800 | tf_op jit(solution)/shard_map/ppermute | solution.py:319
  60.9 2.8 %collective-permute-start.21 = (bf16[32,2176]{1,0:T(8,128)(2,1)S(1)}, bf16[32,2176]{1,0:T(8,128)(2,1)S(1)}, u32[]{:S(2)}, u32[]{:S(2)}) collective-permute-start(bf16[32,2176]{1,0:T(8,128)(2,1)S(1)} %add_convert_fusion.6.refs_2_), channel_id=1, source_target_pairs={{0,2},{1,5},{2,0},{3,7},{4,6},{5,1},{6,4},{7,3},{8,10},{9,13},{10,... | collective-permute-start | bytes 417800 | tf_op jit(solution)/shard_map/ppermute | solution.py:319
  66.2 2.4 %collective-permute-start.27 = (bf16[32,2176]{1,0:T(8,128)(2,1)S(1)}, bf16[32,2176]{1,0:T(8,128)(2,1)S(1)}, u32[]{:S(2)}, u32[]{:S(2)}) collective-permute-start(bf16[32,2176]{1,0:T(8,128)(2,1)S(1)} %add_convert_fusion.2), channel_id=1, source_target_pairs={{0,2},{1,5},{2,0},{3,7},{4,6},{5,1},{6,4},{7,3},{8,10},{9,13},{10,... | collective-permute-start | bytes 417800 | tf_op jit(solution)/shard_map/ppermute | solution.py:319
  68.7 1.6 %collective-permute-start.22 = (bf16[32,2176]{1,0:T(8,128)(2,1)S(1)}, bf16[32,2176]{1,0:T(8,128)(2,1)S(1)}, u32[]{:S(2)}, u32[]{:S(2)}) collective-permute-start(bf16[32,2176]{1,0:T(8,128)(2,1)S(1)} %add_convert_fusion.3), channel_id=1, source_target_pairs={{0,24},{2,26},{4,28},{6,30},{16,8},{18,10},{20,12},{22,14},{24,0},... | collective-permute-start | bytes 417800 | tf_op jit(solution)/shard_map/ppermute | solution.py:328
  71.7 2.1 %collective-permute-start.28 = (bf16[32,2176]{1,0:T(8,128)(2,1)S(1)}, bf16[32,2176]{1,0:T(8,128)(2,1)S(1)}, u32[]{:S(2)}, u32[]{:S(2)}) collective-permute-start(bf16[32,2176]{1,0:T(8,128)(2,1)S(1)} %add_convert_fusion.1), channel_id=1, source_target_pairs={{0,16},{2,18},{4,20},{6,22},{16,24},{18,26},{20,28},{22,30},{24,8}... | collective-permute-start | bytes 417800 | tf_op jit(solution)/shard_map/ppermute | solution.py:328
  73.8 3.0 %collective-permute-done.22 = bf16[32,2176]{1,0:T(8,128)(2,1)S(1)} collective-permute-done((bf16[32,2176]{1,0:T(8,128)(2,1)S(1)}, bf16[32,2176]{1,0:T(8,128)(2,1)S(1)}, u32[]{:S(2)}, u32[]{:S(2)}) %collective-permute-start.22) | collective-permute-done | bytes 139296 | tf_op jit(solution)/shard_map/ppermute | solution.py:328
  (70 shorter events, 21.0 us)
Async XLA Ops:
  2.5 10.1 %collective-permute-start = (bf16[32,4224]{1,0:T(8,128)(2,1)}, bf16[32,4224]{1,0:T(8,128)(2,1)S(1)}, u32[]{:S(2)}, u32[]{:S(2)}) collective-permute-start(bf16[32,4224]{1,0:T(8,128)(2,1)} %pack.1.refs_1_), channel_id=1, source_target_pairs={{0,16},{2,18},{4,20},{6,22},{16,24},{18,26},{20,28},{22,30},{24,8}... | collective-permute-start | bytes 811016 | tf_op jit(solution)/shard_map/ppermute | solution.py:328
  6.6 8.6 %collective-permute-start.1 = (bf16[32,4224]{1,0:T(8,128)(2,1)}, bf16[32,4224]{1,0:T(8,128)(2,1)S(1)}, u32[]{:S(2)}, u32[]{:S(2)}) collective-permute-start(bf16[32,4224]{1,0:T(8,128)(2,1)} %pack.1.refs_1_), channel_id=1, source_target_pairs={{0,2},{1,5},{2,0},{3,7},{4,6},{5,1},{6,4},{7,3},{8,10},{9,13},{10,... | collective-permute-start | bytes 811016 | tf_op jit(solution)/shard_map/ppermute | solution.py:319
  8.0 20.9 %collective-permute-start.11 = (bf16[384,2048]{1,0:T(8,128)(2,1)}, bf16[384,2048]{1,0:T(8,128)(2,1)S(1)}, u32[]{:S(2)}, u32[]{:S(2)}) collective-permute-start(bf16[384,2048]{1,0:T(8,128)(2,1)} %bitcast.10), channel_id=1, source_target_pairs={{0,1},{1,0},{2,3},{3,2},{4,5},{5,4},{6,7},{7,6},{8,9},{9,8},{10,11... | collective-permute-start | bytes 4718600 | tf_op jit(solution)/shard_map/ppermute | solution.py:321
  8.0 12.6 %collective-permute-start.4 = (bf16[32,4224]{1,0:T(8,128)(2,1)}, bf16[32,4224]{1,0:T(8,128)(2,1)S(1)}, u32[]{:S(2)}, u32[]{:S(2)}) collective-permute-start(bf16[32,4224]{1,0:T(8,128)(2,1)} %pack.1.refs_1_), channel_id=1, source_target_pairs={{0,4},{1,3},{2,6},{3,1},{4,0},{5,7},{6,2},{7,5},{8,12},{9,11},{10,... | collective-permute-start | bytes 811016 | tf_op jit(solution)/shard_map/ppermute | solution.py:320
  16.7 9.8 %collective-permute-start.3 = (bf16[32,4224]{1,0:T(8,128)(2,1)S(1)}, bf16[32,4224]{1,0:T(8,128)(2,1)S(1)}, u32[]{:S(2)}, u32[]{:S(2)}) collective-permute-start(bf16[32,4224]{1,0:T(8,128)(2,1)S(1)} %get-tuple-element.36.refs_0_), channel_id=1, source_target_pairs={{0,2},{1,5},{2,0},{3,7},{4,6},{5,1},{6,4},{7,3},{8,10},{9,13},{10,... | collective-permute-start | bytes 811016 | tf_op jit(solution)/shard_map/ppermute | solution.py:319
  19.1 7.4 %collective-permute-start.7 = (bf16[32,4224]{1,0:T(8,128)(2,1)S(1)}, bf16[32,4224]{1,0:T(8,128)(2,1)S(1)}, u32[]{:S(2)}, u32[]{:S(2)}) collective-permute-start(bf16[32,4224]{1,0:T(8,128)(2,1)S(1)} %get-tuple-element.36.refs_0_), channel_id=1, source_target_pairs={{0,4},{1,3},{2,6},{3,1},{4,0},{5,7},{6,2},{7,5},{8,12},{9,11},{10,... | collective-permute-start | bytes 811016 | tf_op jit(solution)/shard_map/ppermute | solution.py:320
  20.6 7.8 %collective-permute-start.8 = (bf16[32,4224]{1,0:T(8,128)(2,1)S(1)}, bf16[32,4224]{1,0:T(8,128)(2,1)S(1)}, u32[]{:S(2)}, u32[]{:S(2)}) collective-permute-start(bf16[32,4224]{1,0:T(8,128)(2,1)S(1)} %get-tuple-element.38.refs_1_), channel_id=1, source_target_pairs={{0,4},{1,3},{2,6},{3,1},{4,0},{5,7},{6,2},{7,5},{8,12},{9,11},{10,... | collective-permute-start | bytes 811016 | tf_op jit(solution)/shard_map/ppermute | solution.py:320
  21.6 9.3 %collective-permute-start.10 = (bf16[2048,384]{1,0:T(8,128)(2,1)}, bf16[2048,384]{1,0:T(8,128)(2,1)}, u32[]{:S(2)}, u32[]{:S(2)}) collective-permute-start(bf16[2048,384]{1,0:T(8,128)(2,1)} %bitcast.14), channel_id=1, source_target_pairs={{0,1},{1,0},{2,3},{3,2},{4,5},{5,4},{6,7},{7,6},{8,9},{9,8},{10,11... | collective-permute-start | bytes 4718600 | tf_op jit(solution)/shard_map/ppermute | solution.py:321
  26.5 9.7 %collective-permute-start.5 = (bf16[32,4224]{1,0:T(8,128)(2,1)S(1)}, bf16[32,4224]{1,0:T(8,128)(2,1)S(1)}, u32[]{:S(2)}, u32[]{:S(2)}) collective-permute-start(bf16[32,4224]{1,0:T(8,128)(2,1)S(1)} %get-tuple-element.37.refs_1_), channel_id=1, source_target_pairs={{0,16},{2,18},{4,20},{6,22},{16,24},{18,26},{20,28},{22,30},{24,8}... | collective-permute-start | bytes 811016 | tf_op jit(solution)/shard_map/ppermute | solution.py:328
  28.5 9.4 %collective-permute-start.6 = (bf16[32,4224]{1,0:T(8,128)(2,1)S(1)}, bf16[32,4224]{1,0:T(8,128)(2,1)S(1)}, u32[]{:S(2)}, u32[]{:S(2)}) collective-permute-start(bf16[32,4224]{1,0:T(8,128)(2,1)S(1)} %get-tuple-element.37.refs_1_), channel_id=1, source_target_pairs={{0,2},{1,5},{2,0},{3,7},{4,6},{5,1},{6,4},{7,3},{8,10},{9,13},{10,... | collective-permute-start | bytes 811016 | tf_op jit(solution)/shard_map/ppermute | solution.py:319
  29.0 18.7 %collective-permute-start.16 = (bf16[32,4224]{1,0:T(8,128)(2,1)S(1)}, bf16[32,4224]{1,0:T(8,128)(2,1)S(1)}, u32[]{:S(2)}, u32[]{:S(2)}) collective-permute-start(bf16[32,4224]{1,0:T(8,128)(2,1)S(1)} %get-tuple-element.37.refs_1_), channel_id=1, source_target_pairs={{0,4},{1,3},{2,6},{3,1},{4,0},{5,7},{6,2},{7,5},{8,12},{9,11},{10,... | collective-permute-start | bytes 811016 | tf_op jit(solution)/shard_map/ppermute | solution.py:320
  31.0 8.5 %collective-permute-start.12 = (bf16[32,4224]{1,0:T(8,128)(2,1)S(1)}, bf16[32,4224]{1,0:T(8,128)(2,1)S(1)}, u32[]{:S(2)}, u32[]{:S(2)}) collective-permute-start(bf16[32,4224]{1,0:T(8,128)(2,1)S(1)} %get-tuple-element.46.refs_1_), channel_id=1, source_target_pairs={{0,4},{1,3},{2,6},{3,1},{4,0},{5,7},{6,2},{7,5},{8,12},{9,11},{10,... | collective-permute-start | bytes 811016 | tf_op jit(solution)/shard_map/ppermute | solution.py:320
  37.8 15.0 %collective-permute-start.23 = (bf16[32,4224]{1,0:T(8,128)(2,1)S(1)}, bf16[32,4224]{1,0:T(8,128)(2,1)S(1)}, u32[]{:S(2)}, u32[]{:S(2)}) collective-permute-start(bf16[32,4224]{1,0:T(8,128)(2,1)S(1)} %get-tuple-element.60.refs_1_), channel_id=1, source_target_pairs={{0,2},{1,5},{2,0},{3,7},{4,6},{5,1},{6,4},{7,3},{8,10},{9,13},{10,... | collective-permute-start | bytes 811016 | tf_op jit(solution)/shard_map/ppermute | solution.py:319
  38.3 14.5 %collective-permute-start.24 = (bf16[32,4224]{1,0:T(8,128)(2,1)S(1)}, bf16[32,4224]{1,0:T(8,128)(2,1)S(1)}, u32[]{:S(2)}, u32[]{:S(2)}) collective-permute-start(bf16[32,4224]{1,0:T(8,128)(2,1)S(1)} %get-tuple-element.60.refs_1_), channel_id=1, source_target_pairs={{0,4},{1,3},{2,6},{3,1},{4,0},{5,7},{6,2},{7,5},{8,12},{9,11},{10,... | collective-permute-start | bytes 811016 | tf_op jit(solution)/shard_map/ppermute | solution.py:320
  42.2 6.6 %collective-permute-start.17 = (bf16[32,4224]{1,0:T(8,128)(2,1)S(1)}, bf16[32,4224]{1,0:T(8,128)(2,1)S(1)}, u32[]{:S(2)}, u32[]{:S(2)}) collective-permute-start(bf16[32,4224]{1,0:T(8,128)(2,1)S(1)} %get-tuple-element.57.refs_1_), channel_id=1, source_target_pairs={{0,4},{1,3},{2,6},{3,1},{4,0},{5,7},{6,2},{7,5},{8,12},{9,11},{10,... | collective-permute-start | bytes 811016 | tf_op jit(solution)/shard_map/ppermute | solution.py:320
  43.6 10.0 %collective-permute-start.25 = (bf16[32,4224]{1,0:T(8,128)(2,1)S(1)}, bf16[32,4224]{1,0:T(8,128)(2,1)S(1)}, u32[]{:S(2)}, u32[]{:S(2)}) collective-permute-start(bf16[32,4224]{1,0:T(8,128)(2,1)S(1)} %get-tuple-element.53.refs_3_), channel_id=1, source_target_pairs={{0,8},{2,10},{4,12},{6,14},{16,0},{18,2},{20,4},{22,6},{24,16},{26... | collective-permute-start | bytes 811016 | tf_op jit(solution)/shard_map/ppermute | solution.py:328
  47.6 10.2 %collective-permute-start.13 = (bf16[64,2176]{1,0:T(8,128)(2,1)S(1)}, bf16[64,2176]{1,0:T(8,128)(2,1)S(1)}, u32[]{:S(2)}, u32[]{:S(2)}) collective-permute-start(bf16[64,2176]{1,0:T(8,128)(2,1)S(1)} %get-tuple-element.50), channel_id=1, source_target_pairs={{0,4},{1,3},{2,6},{3,1},{4,0},{5,7},{6,2},{7,5},{8,12},{9,11},{10,... | collective-permute-start | bytes 835592 | tf_op jit(solution)/shard_map/ppermute | solution.py:320
  48.8 14.9 %collective-permute-start.15 = (bf16[64,2176]{1,0:T(8,128)(2,1)S(1)}, bf16[64,2176]{1,0:T(8,128)(2,1)S(1)}, u32[]{:S(2)}, u32[]{:S(2)}) collective-permute-start(bf16[64,2176]{1,0:T(8,128)(2,1)S(1)} %get-tuple-element.55), channel_id=1, source_target_pairs={{0,4},{1,3},{2,6},{3,1},{4,0},{5,7},{6,2},{7,5},{8,12},{9,11},{10,... | collective-permute-start | bytes 835592 | tf_op jit(solution)/shard_map/ppermute | solution.py:320
  52.8 8.0 %collective-permute-start.18 = (bf16[64,2176]{1,0:T(8,128)(2,1)S(1)}, bf16[64,2176]{1,0:T(8,128)(2,1)S(1)}, u32[]{:S(2)}, u32[]{:S(2)}) collective-permute-start(bf16[64,2176]{1,0:T(8,128)(2,1)S(1)} %get-tuple-element.61), channel_id=1, source_target_pairs={{0,4},{1,3},{2,6},{3,1},{4,0},{5,7},{6,2},{7,5},{8,12},{9,11},{10,... | collective-permute-start | bytes 835592 | tf_op jit(solution)/shard_map/ppermute | solution.py:320
  56.5 9.7 %collective-permute-start.26 = (bf16[64,2176]{1,0:T(8,128)(2,1)S(1)}, bf16[64,2176]{1,0:T(8,128)(2,1)S(1)}, u32[]{:S(2)}, u32[]{:S(2)}) collective-permute-start(bf16[64,2176]{1,0:T(8,128)(2,1)S(1)} %get-tuple-element.67), channel_id=1, source_target_pairs={{0,4},{1,3},{2,6},{3,1},{4,0},{5,7},{6,2},{7,5},{8,12},{9,11},{10,... | collective-permute-start | bytes 835592 | tf_op jit(solution)/shard_map/ppermute | solution.py:320
  60.9 7.7 %collective-permute-start.21 = (bf16[32,2176]{1,0:T(8,128)(2,1)S(1)}, bf16[32,2176]{1,0:T(8,128)(2,1)S(1)}, u32[]{:S(2)}, u32[]{:S(2)}) collective-permute-start(bf16[32,2176]{1,0:T(8,128)(2,1)S(1)} %add_convert_fusion.6.refs_2_), channel_id=1, source_target_pairs={{0,2},{1,5},{2,0},{3,7},{4,6},{5,1},{6,4},{7,3},{8,10},{9,13},{10,... | collective-permute-start | bytes 417800 | tf_op jit(solution)/shard_map/ppermute | solution.py:319
  63.8 10.1 %collective-permute-start.19 = (bf16[32,2176]{1,0:T(8,128)(2,1)S(1)}, bf16[32,2176]{1,0:T(8,128)(2,1)S(1)}, u32[]{:S(2)}, u32[]{:S(2)}) collective-permute-start(bf16[32,2176]{1,0:T(8,128)(2,1)S(1)} %add_convert_fusion.5), channel_id=1, source_target_pairs={{0,8},{2,10},{4,12},{6,14},{16,0},{18,2},{20,4},{22,6},{24,16},{26... | collective-permute-start | bytes 417800 | tf_op jit(solution)/shard_map/ppermute | solution.py:328
  64.5 9.3 %collective-permute-start.20 = (bf16[32,2176]{1,0:T(8,128)(2,1)S(1)}, bf16[32,2176]{1,0:T(8,128)(2,1)S(1)}, u32[]{:S(2)}, u32[]{:S(2)}) collective-permute-start(bf16[32,2176]{1,0:T(8,128)(2,1)S(1)} %add_convert_fusion.4), channel_id=1, source_target_pairs={{0,2},{1,5},{2,0},{3,7},{4,6},{5,1},{6,4},{7,3},{8,10},{9,13},{10,... | collective-permute-start | bytes 417800 | tf_op jit(solution)/shard_map/ppermute | solution.py:319
  68.7 8.1 %collective-permute-start.22 = (bf16[32,2176]{1,0:T(8,128)(2,1)S(1)}, bf16[32,2176]{1,0:T(8,128)(2,1)S(1)}, u32[]{:S(2)}, u32[]{:S(2)}) collective-permute-start(bf16[32,2176]{1,0:T(8,128)(2,1)S(1)} %add_convert_fusion.3), channel_id=1, source_target_pairs={{0,24},{2,26},{4,28},{6,30},{16,8},{18,10},{20,12},{22,14},{24,0},... | collective-permute-start | bytes 417800 | tf_op jit(solution)/shard_map/ppermute | solution.py:328
  (11 other events, 65.9 us)
